TPU v7x, 32 devices: a whole 2x2x4 slice. The times are simulated.
32 devices in a mesh: dp: 2 (over x), row: 4 (over z), col: 4 (over y, core).
Axes of the slice: x: 2, y: 2, z: 4, core: 2. Of those that a mesh axis runs over, the one named last changes fastest.
Arguments:
- activations: bfloat16 [8192, 1536], P(('dp', 'row'), 'col'), may hold values from -6 to 6
- cotangent: bfloat16 [8192, 1536], P(('dp', 'row'), 'col'), may hold values from -6 to 6
- gain_one: bfloat16 [1536], P('col'), may hold values from 0.5 to 1.5
- gain_two: bfloat16 [1536], P('col'), may hold values from 0.5 to 1.5
- w_query: bfloat16 [1536, 1536], P('col', 'row'), may hold values from -0.15625 to 0.15625
- key_projection_weight: bfloat16 [1536, 512], P('col', 'row'), may hold values from -0.15625 to 0.15625
- value_projection_weight: bfloat16 [1536, 512], P('col', 'row'), may hold values from -0.15625 to 0.15625
- w_out: bfloat16 [1536, 1536], P('row', 'col'), may hold values from -0.625 to 0.625
- w_router: bfloat16 [1536, 40], P('col'), may hold values from -0.078125 to 0.078125
- w_gate: bfloat16 [40, 1536, 512], P(None, 'col', 'row'), may hold values from -0.15625 to 0.15625
- w_up: bfloat16 [40, 1536, 512], P(None, 'col', 'row'), may hold values from -0.15625 to 0.15625
- w_down: bfloat16 [40, 512, 1536], P(None, 'row', 'col'), may hold values from -1 to 1
- routes: int32 [8192, 8], P('dp'), may hold values from 0 to 39, all different within a row; in each aligned block of 4096 rows (0 to 4095, 4096 to 8191, ...) at most 1024 rows name the same one
- doc_lengths: int32 [8, 4], P('dp'), may hold values from 1 to 512, 1024 in all within a row
Outputs:
- block_out: bfloat16 [8192, 1536], P(('dp', 'row'), 'col')
- input_grad: bfloat16 [8192, 1536], P(('dp', 'row'), 'col')
- gain_one_grad: float32 [1536], P('col')
- gain_two_grad: float32 [1536], P('col')
- w_query_grad: float32 [1536, 1536], P(('col', 'dp'), 'row')
- w_key_grad: float32 [1536, 512], P(('col', 'dp'), 'row')
- w_value_grad: float32 [1536, 512], P(('col', 'dp'), 'row')
- w_out_grad: float32 [1536, 1536], P(('row', 'dp'), 'col')
- w_router_grad: float32 [1536, 40], P(('col', 'dp'))
- w_gate_grad: float32 [40, 1536, 512], P(None, ('col', 'dp'), 'row')
- w_up_grad: float32 [40, 1536, 512], P(None, ('col', 'dp'), 'row')
- w_down_grad: float32 [40, 512, 1536], P(None, 'row', ('col', 'dp'))
Inputs may be any that keep to these rules, and one draw needn't show every extreme that they name: `routes`: each row names 8 different experts; within each aligned block of 4096 rows no expert is named by more than 1024 rows, a bound that some block reaches. `doc_lengths`: each row sums to 1024.
All inputs are finite; a program needn't handle non-finite values.
Results may differ from a plain program's by a relative error of at most 0.025.
Values may be sent and summed in bfloat16 or wider, within the bound.
No kernel may reach another device: no remote copies, remote signals or barrier semaphores. Data moves between devices by JAX's collectives and lax.ppermute only.
A program may use at most 512 MiB of HBM per device.

v0:
```python
import math

import jax
import jax.numpy as jnp
from jax import lax
from jax.sharding import PartitionSpec as P

MODEL_WIDTH = 1536
HEAD_SIZE = 64
SEQUENCE_LENGTH = 1024
CAP = 1024


epsilon = 1e-06


def row_totals(per_row):
    return lax.psum(per_row, "col")


def gather_rows(block):
    return lax.all_gather(block, "row", axis=0, tiled=True)


def gather_columns(block):
    return lax.all_gather(block, "col", axis=0, tiled=True)


def column_sums(term_fn, keep_rows):
    return lax.psum_scatter(
        term_fn(jnp.int32(0), keep_rows * lax.axis_size("col")),
        "col",
        scatter_dimension=0,
        tiled=True,
    )


def token_sums(partial_rows):
    return lax.psum_scatter(partial_rows, "row", scatter_dimension=0, tiled=True)


def rotation_tables(positions):
    half_width = HEAD_SIZE // 2
    frequency = 10000.0 ** (-jnp.arange(half_width).astype(jnp.float32) / half_width)
    angles = positions.astype(jnp.float32)[:, None] * frequency[None, :]
    return (jnp.cos(angles)[:, None, :], jnp.sin(angles)[:, None, :])


def rotate(values_in, cosine, sine_part, direction):
    half_width = HEAD_SIZE // 2
    first_half = values_in[..., :half_width]
    second = values_in[..., half_width:]
    return jnp.concatenate(
        [
            first_half * cosine - direction * second * sine_part,
            second * cosine + direction * first_half * sine_part,
        ],
        axis=-1,
    )


def doc_mask(sequence_lengths):
    positions = jnp.arange(SEQUENCE_LENGTH)
    doc_ends = jnp.cumsum(sequence_lengths)
    doc_ids = jnp.sum((positions[:, None] >= doc_ends[None, :]).astype(jnp.int32), axis=1)
    return (doc_ids[:, None] == doc_ids[None, :]) & (positions[:, None] >= positions[None, :])


def slot_numbers(flat_match):
    pair_count, expert_count = flat_match.shape
    block_size = math.gcd(pair_count, 512)
    blocks = flat_match.astype(jnp.float32).reshape(
        pair_count // block_size, block_size, expert_count
    )
    lower = (jnp.arange(block_size)[:, None] >= jnp.arange(block_size)[None, :]).astype(jnp.float32)
    within = jnp.einsum("ij,bje->bie", lower, blocks, precision=lax.Precision.HIGHEST)
    block_totals = within[:, -1, :]
    offsets = jnp.cumsum(block_totals, axis=0) - block_totals
    counts = (within + offsets[:, None, :]).reshape(pair_count, expert_count)
    return jnp.sum((counts - 1.0) * flat_match.astype(jnp.float32), axis=1).astype(jnp.int32)


def score_block(query_matrix, projected_keys, sequence_lengths):
    local_kv = projected_keys.shape[1] // HEAD_SIZE
    grouped_queries = query_matrix.reshape(SEQUENCE_LENGTH, local_kv, -1, HEAD_SIZE)
    key_heads = projected_keys.reshape(SEQUENCE_LENGTH, local_kv, HEAD_SIZE)
    scores = jnp.einsum(
        "qkgd,skd->kgqs", grouped_queries, key_heads, preferred_element_type=jnp.float32
    ) * HEAD_SIZE ** (-0.5)
    return (
        jnp.where(doc_mask(sequence_lengths)[None, None], scores, -1e30),
        grouped_queries,
        key_heads,
    )


def attend_forward(seq_items):
    query_matrix, projected_keys, projected_values, sequence_lengths = seq_items
    scores, grouped_queries, key_heads = score_block(query_matrix, projected_keys, sequence_lengths)
    top_score = jnp.max(scores, axis=-1, keepdims=True)
    expo_scores = jnp.exp(scores - top_score)
    totals = jnp.sum(expo_scores, axis=-1, keepdims=True)
    softmax_probs = (expo_scores / totals).astype(jnp.bfloat16)
    value_heads = projected_values.reshape(SEQUENCE_LENGTH, key_heads.shape[1], HEAD_SIZE)
    attention_output = jnp.einsum(
        "kgqs,skd->qkgd", softmax_probs, value_heads, preferred_element_type=jnp.float32
    )
    return (attention_output.reshape(SEQUENCE_LENGTH, -1), (top_score + jnp.log(totals))[..., 0])


def attend_backward(seq_items):
    query_matrix, projected_keys, projected_values, sequence_lengths, log_totals, out_grad = (
        seq_items
    )
    scores, grouped_queries, key_heads = score_block(query_matrix, projected_keys, sequence_lengths)
    softmax_probs = jnp.exp(scores - log_totals[..., None])
    local_kv = key_heads.shape[1]
    grad_grouped = out_grad.reshape(SEQUENCE_LENGTH, local_kv, -1, HEAD_SIZE)
    value_heads = projected_values.reshape(SEQUENCE_LENGTH, local_kv, HEAD_SIZE)
    prob_grads = jnp.einsum(
        "qkgd,skd->kgqs", grad_grouped, value_heads, preferred_element_type=jnp.float32
    )
    score_grads = (
        softmax_probs * (prob_grads - jnp.sum(softmax_probs * prob_grads, axis=-1, keepdims=True))
    ).astype(jnp.bfloat16)
    query_grads = jnp.einsum(
        "kgqs,skd->qkgd", score_grads, key_heads, preferred_element_type=jnp.float32
    ) * HEAD_SIZE ** (-0.5)
    key_grads = jnp.einsum(
        "kgqs,qkgd->skd", score_grads, grouped_queries, preferred_element_type=jnp.float32
    ) * HEAD_SIZE ** (-0.5)
    value_grads = jnp.einsum(
        "kgqs,qkgd->skd",
        softmax_probs.astype(jnp.bfloat16),
        grad_grouped,
        preferred_element_type=jnp.float32,
    )
    return (
        query_grads.reshape(SEQUENCE_LENGTH, -1),
        key_grads.reshape(SEQUENCE_LENGTH, -1),
        value_grads.reshape(SEQUENCE_LENGTH, -1),
    )


def on_device(
    activations,
    cotangent,
    gain_one,
    gain_two,
    w_query,
    key_projection_weight,
    value_projection_weight,
    w_out,
    w_router,
    w_gate,
    w_up,
    w_down,
    routes,
    doc_lengths,
):
    local_rows = activations.shape[0]
    group_rows = routes.shape[0]
    top_count = routes.shape[1]
    band_rows = group_rows // lax.axis_size("col")
    slot_keep = CAP // lax.axis_size("col")
    col_index = lax.axis_index("col")
    row_index = lax.axis_index("row")
    query_width = w_query.shape[1]
    kv_width = key_projection_weight.shape[1]
    local_q = query_width // HEAD_SIZE
    local_kv = kv_width // HEAD_SIZE
    sequence_count = band_rows // SEQUENCE_LENGTH
    expert_count = w_router.shape[1]
    hidden_width = w_gate.shape[2]
    gain_one_f = gain_one.astype(jnp.float32)
    gain_two_f = gain_two.astype(jnp.float32)
    inputs_f = activations.astype(jnp.float32)
    inverse_one = lax.rsqrt(
        row_totals(jnp.sum(inputs_f * inputs_f, axis=1)) / MODEL_WIDTH + epsilon
    )
    scaled_one = inputs_f * inverse_one[:, None]
    first_normed_input = gather_rows((scaled_one * gain_one_f).astype(jnp.bfloat16))
    qkv_weight = jnp.concatenate([w_query, key_projection_weight, value_projection_weight], axis=1)
    both_weights = jnp.concatenate([w_gate, w_up], axis=2)

    def qkv_term(start, count):
        return jnp.dot(first_normed_input, qkv_weight, preferred_element_type=jnp.float32)

    qkv_totals = column_sums(qkv_term, band_rows)
    positions = jnp.arange(band_rows) % SEQUENCE_LENGTH
    cosine, sine_part = rotation_tables(positions)
    query_matrix = (
        rotate(qkv_totals[:, :query_width].reshape(-1, local_q, HEAD_SIZE), cosine, sine_part, 1.0)
        .astype(jnp.bfloat16)
        .reshape(-1, query_width)
    )
    projected_keys = (
        rotate(
            qkv_totals[:, query_width : query_width + kv_width].reshape(-1, local_kv, HEAD_SIZE),
            cosine,
            sine_part,
            1.0,
        )
        .astype(jnp.bfloat16)
        .reshape(-1, kv_width)
    )
    projected_values = qkv_totals[:, query_width + kv_width :].astype(jnp.bfloat16)
    own_lengths = lax.dynamic_slice_in_dim(
        doc_lengths, col_index * sequence_count, sequence_count, 0
    )
    seq_queries = query_matrix.reshape(sequence_count, SEQUENCE_LENGTH, query_width)
    seq_keys = projected_keys.reshape(sequence_count, SEQUENCE_LENGTH, kv_width)
    seq_values = projected_values.reshape(sequence_count, SEQUENCE_LENGTH, kv_width)
    attention_output, log_totals = lax.map(
        attend_forward, (seq_queries, seq_keys, seq_values, own_lengths)
    )
    attn_rows = gather_columns(attention_output.reshape(-1, query_width).astype(jnp.bfloat16))
    hidden = inputs_f + token_sums(jnp.dot(attn_rows, w_out, preferred_element_type=jnp.float32))
    inverse_two = lax.rsqrt(row_totals(jnp.sum(hidden * hidden, axis=1)) / MODEL_WIDTH + epsilon)
    scaled_two = hidden * inverse_two[:, None]
    normed_two = gather_rows((scaled_two * gain_two_f).astype(jnp.bfloat16))
    cot_rows = gather_rows(cotangent)
    feature_width = normed_two.shape[1]
    logits = lax.psum(
        jnp.dot(normed_two, w_router, preferred_element_type=jnp.float32).astype(jnp.bfloat16),
        "col",
    ).astype(jnp.float32)
    expert_ids = jnp.arange(expert_count)
    route_match = routes[:, :, None] == expert_ids[None, None, :]
    chosen = jnp.sum(jnp.where(route_match, logits[:, None, :], 0.0), axis=-1)
    gate_weights = jax.nn.softmax(chosen, axis=-1)
    flat_routes = routes.reshape(-1)
    slot_index = slot_numbers(route_match.reshape(-1, expert_count))
    slot_flat = slot_index * expert_count + flat_routes
    token_ids = jnp.arange(flat_routes.shape[0]) // top_count
    slot_owner = jnp.full((CAP * expert_count,), group_rows, jnp.int32).at[slot_flat].set(token_ids)
    slot_gate = (
        jnp.zeros((CAP * expert_count,), jnp.float32)
        .at[slot_flat]
        .set(gate_weights.reshape(-1))
        .reshape(CAP, expert_count)
    )
    paired_rows = jnp.concatenate(
        [
            jnp.concatenate([normed_two, cot_rows], axis=1),
            jnp.zeros((1, 2 * feature_width), jnp.bfloat16),
        ],
        axis=0,
    )
    slot_rows = paired_rows[slot_owner].reshape(CAP, expert_count, 2 * feature_width)
    expert_inputs = slot_rows[..., :feature_width]
    slot_cot = slot_rows[..., feature_width:]
    gate_up = lax.psum_scatter(
        jnp.einsum(
            "ced,edh->ceh", expert_inputs, both_weights, preferred_element_type=jnp.float32
        ).astype(jnp.bfloat16),
        "col",
        scatter_dimension=0,
        tiled=True,
    ).astype(jnp.float32)
    gate_act = gate_up[..., :hidden_width]
    up_act = gate_up[..., hidden_width:]
    sigmoid_gate = jax.nn.sigmoid(gate_act)
    silu_gate = gate_act * sigmoid_gate
    inner_rows = gather_columns((silu_gate * up_act).astype(jnp.bfloat16))
    expert_out = jnp.einsum("ceh,ehd->ced", inner_rows, w_down, preferred_element_type=jnp.float32)
    slot_gate_grads = lax.psum(
        jnp.sum(expert_out * slot_cot, axis=2).astype(jnp.bfloat16), ("row", "col")
    ).astype(jnp.float32)
    weighted = (expert_out * slot_gate[..., None]).reshape(-1, expert_out.shape[2])
    mixture_part = jnp.sum(weighted[slot_flat].reshape(group_rows, top_count, -1), axis=1)
    block_out = (hidden + token_sums(mixture_part)).astype(jnp.bfloat16)
    gate_grads = slot_gate_grads.reshape(-1)[slot_flat].reshape(group_rows, -1)
    chosen_grads = gate_weights * (
        gate_grads - jnp.sum(gate_weights * gate_grads, axis=1, keepdims=True)
    )
    logit_grads = jnp.sum(jnp.where(route_match, chosen_grads[:, :, None], 0.0), axis=1).astype(
        jnp.bfloat16
    )
    router_grad = jnp.einsum(
        "gd,ge->de", normed_two, logit_grads, preferred_element_type=jnp.float32
    )
    own_logit_grads = lax.dynamic_slice_in_dim(logit_grads, row_index * local_rows, local_rows, 0)
    router_input_grads = jnp.einsum(
        "ge,de->gd", own_logit_grads, w_router, preferred_element_type=jnp.float32
    )
    out_grads = (slot_gate[..., None] * slot_cot).astype(jnp.bfloat16)
    down_grad = jnp.einsum(
        "ceh,ced->ehd", inner_rows, out_grads, preferred_element_type=jnp.float32
    )

    def inner_term(start, count):
        return jnp.einsum("ced,ehd->ceh", out_grads, w_down, preferred_element_type=jnp.float32)

    inner_grads = column_sums(inner_term, slot_keep)
    gate_grad_act = inner_grads * up_act * sigmoid_gate * (1.0 + gate_act * (1.0 - sigmoid_gate))
    up_grad_act = inner_grads * silu_gate
    gate_up_grads = gather_columns(
        jnp.concatenate([gate_grad_act, up_grad_act], axis=2).astype(jnp.bfloat16)
    )
    both_grad = jnp.einsum(
        "ced,ceh->edh", expert_inputs, gate_up_grads, preferred_element_type=jnp.float32
    )
    input_part = jnp.einsum(
        "ceh,edh->ced", gate_up_grads, both_weights, preferred_element_type=jnp.float32
    )
    token_part = jnp.sum(
        input_part.reshape(-1, input_part.shape[2])[slot_flat].reshape(group_rows, top_count, -1),
        axis=1,
    )
    normed_two_grads = token_sums(token_part) + router_input_grads
    grad_scaled_two = normed_two_grads * gain_two_f
    stat_two = row_totals(jnp.sum(grad_scaled_two * scaled_two, axis=1)) / MODEL_WIDTH
    hidden_grads = cotangent.astype(jnp.float32) + inverse_two[:, None] * (
        grad_scaled_two - scaled_two * stat_two[:, None]
    )
    gain_two_part = jnp.sum(normed_two_grads * scaled_two, axis=0)
    branch_rows = gather_rows(hidden_grads.astype(jnp.bfloat16))
    out_weight_grad = jnp.einsum(
        "gq,gd->qd", attn_rows, branch_rows, preferred_element_type=jnp.float32
    )

    def attended_term(start, count):
        return jnp.einsum("gd,qd->gq", branch_rows, w_out, preferred_element_type=jnp.float32)

    attended_grads = column_sums(attended_term, band_rows).astype(jnp.bfloat16)
    query_grads, key_grads, value_grads = lax.map(
        attend_backward,
        (
            seq_queries,
            seq_keys,
            seq_values,
            own_lengths,
            log_totals,
            attended_grads.reshape(sequence_count, SEQUENCE_LENGTH, query_width),
        ),
    )
    query_grads = rotate(
        query_grads.reshape(-1, local_q, HEAD_SIZE), cosine, sine_part, -1.0
    ).reshape(-1, query_width)
    key_grads = rotate(key_grads.reshape(-1, local_kv, HEAD_SIZE), cosine, sine_part, -1.0).reshape(
        -1, kv_width
    )
    qkv_grads = jnp.concatenate(
        [query_grads, key_grads, value_grads.reshape(-1, kv_width)], axis=1
    ).astype(jnp.bfloat16)
    qkv_rows = gather_columns(qkv_grads)
    qkv_weight_grad = jnp.einsum(
        "gd,gq->dq", first_normed_input, qkv_rows, preferred_element_type=jnp.float32
    )
    normed_one_grads = token_sums(
        jnp.einsum("gq,dq->gd", qkv_rows, qkv_weight, preferred_element_type=jnp.float32)
    )
    grad_scaled_one = normed_one_grads * gain_one_f
    stat_one = row_totals(jnp.sum(grad_scaled_one * scaled_one, axis=1)) / MODEL_WIDTH
    input_grad = (
        hidden_grads + inverse_one[:, None] * (grad_scaled_one - scaled_one * stat_one[:, None])
    ).astype(jnp.bfloat16)
    gain_one_part = jnp.sum(normed_one_grads * scaled_one, axis=0)
    gain_one_grad, gain_two_grad = lax.psum((gain_one_part, gain_two_part), ("dp", "row"))
    summed = (
        lax.psum_scatter(
            qkv_weight_grad[:, :query_width].astype(jnp.bfloat16),
            "dp",
            scatter_dimension=0,
            tiled=True,
        ).astype(jnp.float32),
        lax.psum_scatter(
            qkv_weight_grad[:, query_width : query_width + kv_width].astype(jnp.bfloat16),
            "dp",
            scatter_dimension=0,
            tiled=True,
        ).astype(jnp.float32),
        lax.psum_scatter(
            qkv_weight_grad[:, query_width + kv_width :].astype(jnp.bfloat16),
            "dp",
            scatter_dimension=0,
            tiled=True,
        ).astype(jnp.float32),
        lax.psum_scatter(
            out_weight_grad.astype(jnp.bfloat16), "dp", scatter_dimension=0, tiled=True
        ).astype(jnp.float32),
        lax.psum_scatter(
            router_grad.astype(jnp.bfloat16), "dp", scatter_dimension=0, tiled=True
        ).astype(jnp.float32),
        lax.psum_scatter(
            both_grad[..., :hidden_width].astype(jnp.bfloat16),
            "dp",
            scatter_dimension=1,
            tiled=True,
        ).astype(jnp.float32),
        lax.psum_scatter(
            both_grad[..., hidden_width:].astype(jnp.bfloat16),
            "dp",
            scatter_dimension=1,
            tiled=True,
        ).astype(jnp.float32),
        lax.psum_scatter(
            down_grad.astype(jnp.bfloat16), "dp", scatter_dimension=2, tiled=True
        ).astype(jnp.float32),
    )
    return (
        block_out,
        input_grad,
        gain_one_grad,
        gain_two_grad,
        summed[0],
        summed[1],
        summed[2],
        summed[3],
        summed[4],
        summed[5],
        summed[6],
        summed[7],
    )


def solution(mesh):
    placed = (
        P(("dp", "row"), "col"),
        P(("dp", "row"), "col"),
        P("col"),
        P("col"),
        P("col", "row"),
        P("col", "row"),
        P("col", "row"),
        P("row", "col"),
        P("col", None),
        P(None, "col", "row"),
        P(None, "col", "row"),
        P(None, "row", "col"),
        P("dp", None),
        P("dp", None),
    )
    return jax.shard_map(
        on_device,
        mesh=mesh,
        in_specs=placed,
        out_specs=(
            P(("dp", "row"), "col"),
            P(("dp", "row"), "col"),
            P("col"),
            P("col"),
            P(("col", "dp"), "row"),
            P(("col", "dp"), "row"),
            P(("col", "dp"), "row"),
            P(("row", "dp"), "col"),
            P(("col", "dp"), None),
            P(None, ("col", "dp"), "row"),
            P(None, ("col", "dp"), "row"),
            P(None, "row", ("col", "dp")),
        ),
        check_vma=False,
    )
```

profile of v0, /device:TPU:0, one launch (start us, length us, event | category | flops | bytes accessed | tf_op | source)
XLA Modules:
  0.0 2916.5 jit_solution(7728258502522629305)
XLA Ops:
  23.5 61.0 %all-gather.9.cloned.1.call-done = bf16[4096,384]{1,0:T(8,128)(2,1)} async-done(((bf16[1024,384]{1,0:T(8,128)(2,1)}), bf16[4096,384]{1,0:T(8,128)(2,1)}) %all-gather.9.cloned.1.call-update) | async-done | bytes 3145744 | tf_op jit(solution)/shard_map/all_gather | solution.py:22
  97.7 80.1 %reduce-scatter.19.cloned.1.call-done = f32[1024,640]{1,0:T(8,128)} async-done(((f32[4096,640]{1,0:T(8,128)}), f32[1024,640]{1,0:T(8,128)}) %reduce-scatter.19.cloned.1.call-update) | async-done | bytes 2621456 | tf_op jit(solution)/shard_map/reduce_scatter | solution.py:30
  210.9 28.6 all-gather.11.cloned.1.call-done
  283.0 74.1 %reduce-scatter.21.cloned.1.call-done = f32[1024,384]{1,0:T(8,128)} async-done(((f32[4096,384]{1,0:T(8,128)}), f32[1024,384]{1,0:T(8,128)}) %reduce-scatter.21.cloned.1.call-update) | async-done | bytes 1572880 | tf_op jit(solution)/shard_map/reduce_scatter | solution.py:39
  379.7 120.2 %scatter_custom_fusion = s32[40960]{0:T(1024)S(1)} fusion(s32[32768]{0:T(1024)S(1)} %bitcast.139, s32[32768]{0:T(1024)S(1)} %add_select_fusion, s32[]{:T(128)} %constant.132.clone.1), kind=kCustom, calls=%fused_computation.127 | custom fusion | bytes 163844 | tf_op jit(solution)/shard_map/scatter | solution.py:236
  508.4 185.4 %gather_fusion = bf16[40960,768]{1,0:T(8,128)(2,1)} fusion(bf16[4097,768]{1,0:T(8,128)(2,1)} %fusion.29, s32[40960]{0:T(1024)S(1)} %fusion.59), kind=kCustom, calls=%fused_computation | custom fusion | bytes 125992960 | tf_op jit(solution)/shard_map/gather | solution.py:250
  693.8 42.2 %fusion.82 = (bf16[1024,40,384]{2,1,0:T(8,128)(2,1)}, bf16[1024,40,384]{2,1,0:T(8,128)(2,1)}) fusion(bf16[1024,40,768]{2,1,0:T(8,128)(2,1)} %bitcast.121), kind=kLoop, calls=%fused_computation.157 | loop fusion | bytes 125829120 | tf_op jit(solution)/shard_map/slice | solution.py:252
  735.9 26.5 convert_bitcast_fusion
  766.4 149.0 %reduce-scatter.23.cloned.1.call-done = bf16[256,40,256]{0,2,1:T(8,128)(2,1)} async-done(((bf16[1024,40,256]{0,2,1:T(8,128)(2,1)}), bf16[256,40,256]{0,2,1:T(8,128)(2,1)}) %reduce-scatter.23.cloned.1.call-update) | async-done | bytes 5242896 | tf_op jit(solution)/shard_map/reduce_scatter | solution.py:253
  926.0 24.8 all-reduce.5.cloned.1.call-done
  952.8 71.8 %all-gather.17.cloned.1.call-done = bf16[1024,40,128]{0,2,1:T(8,128)(2,1)} async-done(((bf16[256,40,128]{0,2,1:T(8,128)(2,1)}), bf16[1024,40,128]{0,2,1:T(8,128)(2,1)}) %all-gather.17.cloned.1.call-update) | async-done | bytes 10485776 | tf_op jit(solution)/shard_map/all_gather | solution.py:26
  1024.6 40.3 %fusion.1 = (bf16[1024,40]{0,1:T(8,128)(2,1)S(1)}, f32[40,1024,384]{2,1,0:T(8,128)}) fusion(bf16[1024,40,384]{2,1,0:T(8,128)(2,1)} %get-tuple-element.73, bf16[1024,40,128]{0,2,1:T(8,128)(2,1)} %all-gather.17.cloned.1.call-done, bf16[40,128,384]{2,1,0:T(8,128)(2,1)} %param.25), kind=kOutput, calls=%fused_computation.9 | convolution fusion | flops 4073676800 | bytes 108871680 | tf_op jit(solution)/shard_map/ceh,ehd->ced/dot_general | solution.py:266
  1066.3 85.3 %all-reduce.7.cloned.1.call-done = bf16[40960]{0:T(1024)(128)(2,1)} async-done(((bf16[40960]{0:T(1024)(128)(2,1)}), bf16[40960]{0:T(1024)(128)(2,1)}) %all-reduce.7.cloned.1.call-update) | async-done | bytes 81936 | tf_op jit(solution)/shard_map/psum | solution.py:267
  1152.5 180.5 %gather_fusion.3 = f32[32768]{0:T(1024)S(1)} fusion(f32[40960]{0:T(1024)S(1)} %reshape.406, s32[32768]{0:T(1024)S(1)} %broadcast_clamp_fusion), kind=kCustom, calls=%fused_computation.3 | custom fusion | bytes 393216 | tf_op jit(solution)/shard_map/gather | solution.py:273
  1337.1 120.2 %scatter_custom_fusion.1 = f32[40960]{0:T(1024)S(1)} fusion(s32[32768]{0:T(1024)S(1)} %bitcast.141, f32[32768]{0:T(1024)S(1)} %reshape.457, f32[]{:T(128)} %constant.118.clone.1), kind=kCustom, calls=%fused_computation.125 | custom fusion | bytes 163844 | tf_op jit(solution)/shard_map/scatter | solution.py:240
  1457.8 24.6 fusion.23
  1482.5 154.1 %reduce-scatter.27.cloned.1.call-done = f32[256,40,128]{0,2,1:T(8,128)} async-done(((f32[1024,40,128]{0,2,1:T(8,128)}), f32[256,40,128]{0,2,1:T(8,128)}) %reduce-scatter.27.cloned.1.call-update) | async-done | bytes 5242896 | tf_op jit(solution)/shard_map/reduce_scatter | solution.py:30
  1646.7 134.5 %all-gather.19.cloned.1.call-done = bf16[1024,40,256]{0,2,1:T(8,128)(2,1)} async-done(((bf16[256,40,256]{0,2,1:T(8,128)(2,1)}), bf16[1024,40,256]{0,2,1:T(8,128)(2,1)}) %all-gather.19.cloned.1.call-update) | async-done | bytes 20971536 | tf_op jit(solution)/shard_map/all_gather | solution.py:26
  1781.2 30.9 %convolution_bitcast_fusion = f32[1024,40,384]{0,2,1:T(8,128)} fusion(bf16[1024,40,256]{0,2,1:T(8,128)(2,1)} %all-gather.19.cloned.1.call-done, bf16[40,384,128]{1,2,0:T(8,128)(2,1)} %copy.228, bf16[40,384,128]{1,2,0:T(8,128)(2,1)} %copy.227), kind=kOutput, calls=%fused_computation.29 | convolution fusion | flops 8068792320 | bytes 91750400 | tf_op jit(solution)/shard_map/ceh,edh->ced/dot_general | solution.py:304
  1812.1 61.7 %copy.246 = f32[1024,40,384]{2,1,0:T(8,128)} copy(f32[1024,40,384]{0,2,1:T(8,128)} %convolution_bitcast_fusion) | data formatting | bytes 125829120 | tf_op jit(solution)/shard_map/ceh,edh->ced/transpose | solution.py:304
  1873.8 149.6 %gather_fusion.2 = f32[32768,384]{1,0:T(8,128)} fusion(f32[40960,384]{1,0:T(8,128)} %bitcast.120, s32[32768]{0:T(1024)S(1)} %broadcast_clamp_fusion), kind=kCustom, calls=%fused_computation.2 | custom fusion | bytes 100794368 | tf_op jit(solution)/shard_map/gather | solution.py:308
  2023.4 69.8 %bitcast_reduce_fusion = f32[4096,384]{1,0:T(8,128)} fusion(f32[32768,384]{1,0:T(8,128)} %gather_fusion.2), kind=kLoop, calls=%fused_computation.11 | loop fusion | flops 11010048 | bytes 56623104 | tf_op jit(solution)/shard_map/reduce_sum | solution.py:307
  2095.6 108.6 %reduce-scatter.29.cloned.1.call-done = f32[1024,384]{1,0:T(8,128)} async-done(((f32[4096,384]{1,0:T(8,128)}), f32[1024,384]{1,0:T(8,128)}) %reduce-scatter.29.cloned.1.call-update) | async-done | bytes 1572880 | tf_op jit(solution)/shard_map/reduce_scatter | solution.py:39
  2216.6 63.2 %all-gather.21.cloned.1.call-done = bf16[4096,384]{1,0:T(8,128)(2,1)} async-done(((bf16[1024,384]{1,0:T(8,128)(2,1)}), bf16[4096,384]{1,0:T(8,128)(2,1)}) %all-gather.21.cloned.1.call-update) | async-done | bytes 3145744 | tf_op jit(solution)/shard_map/all_gather | solution.py:22
  2287.1 56.4 %reduce-scatter.31.cloned.1.call-done = f32[1024,384]{1,0:T(8,128)} async-done(((f32[4096,384]{1,0:T(8,128)}), f32[1024,384]{1,0:T(8,128)}) %reduce-scatter.31.cloned.1.call-update) | async-done | bytes 1572880 | tf_op jit(solution)/shard_map/reduce_scatter | solution.py:30
  2401.1 25.9 fusion.32
  2478.5 42.5 %bitcast_multiply_fusion = f32[1024,40,384]{2,0,1:T(8,128)} fusion(f32[40,1024,384]{2,1,0:T(8,128)} %get-tuple-element.97, f32[1024,40]{0,1:T(8,128)S(1)} %copy-done.33), kind=kLoop, calls=%fused_computation.10 | loop fusion | flops 15728640 | bytes 125992960 | tf_op jit(solution)/shard_map/mul | solution.py:270
  2521.0 53.5 %copy.241 = f32[1024,40,384]{2,1,0:T(8,128)} copy(f32[1024,40,384]{2,0,1:T(8,128)} %bitcast_multiply_fusion) | data formatting | bytes 125829120 | tf_op jit(solution)/shard_map/mul | solution.py:270
  2574.5 149.6 %gather_fusion.1 = f32[32768,384]{1,0:T(8,128)} fusion(f32[40960,384]{1,0:T(8,128)} %bitcast.119, s32[32768]{0:T(1024)S(1)} %copy-done.18), kind=kCustom, calls=%fused_computation.1 | custom fusion | bytes 100794368 | tf_op jit(solution)/shard_map/gather | solution.py:271
  2724.1 69.7 %bitcast_reduce_fusion.1 = f32[4096,384]{1,0:T(8,128)} fusion(f32[32768,384]{1,0:T(8,128)} %gather_fusion.1), kind=kLoop, calls=%fused_computation.12 | loop fusion | flops 11010048 | bytes 56623104 | tf_op jit(solution)/shard_map/reduce_sum | solution.py:271
  2816.2 23.4 all-reduce.1
  2845.6 60.4 %reduce-scatter.25.cloned.1.call-done = f32[1024,384]{1,0:T(8,128)} async-done(((f32[4096,384]{1,0:T(8,128)}), f32[1024,384]{1,0:T(8,128)}) %reduce-scatter.25.cloned.1.call-update) | async-done | bytes 1572880 | tf_op jit(solution)/shard_map/reduce_scatter | solution.py:39
  (303 shorter events, 333.0 us)
Async XLA Ops:
  7.2 232.3 %copy-start = (bf16[384,384]{1,0:T(8,128)(2,1)S(1)}, bf16[384,384]{1,0:T(8,128)(2,1)}, u32[]{:S(2)}) copy-start(bf16[384,384]{1,0:T(8,128)(2,1)} %param.21) | copy-start | bytes 884740
  7.2 77.4 %all-gather.9.cloned.1.call-start = ((), (), s32[]{:S(2)}) async-start(), calls=%async_computation.16 | async-start | bytes 3932160 | tf_op jit(solution)/shard_map/all_gather | solution.py:22
  20.6 157.1 %reduce-scatter.19.cloned.1.call-start = ((), (), s32[]{:S(2)}) async-start(), calls=%async_computation.17 | async-start | bytes 13107200 | tf_op jit(solution)/shard_map/reduce_scatter | solution.py:30
  93.6 145.9 %all-gather.11.cloned.1.call-start = ((), (), s32[]{:S(2)}) async-start(), calls=%async_computation.18 | async-start | bytes 3932160 | tf_op jit(solution)/shard_map/all_gather | solution.py:26
  210.8 146.2 %reduce-scatter.21.cloned.1.call-start = ((), (), s32[]{:S(2)}) async-start(), calls=%async_computation.19 | async-start | bytes 7864320 | tf_op jit(solution)/shard_map/reduce_scatter | solution.py:39
  246.1 253.7 %all-gather.15.cloned.1.call-start = ((), (), s32[]{:S(2)}) async-start(), calls=%async_computation.21 | async-start | bytes 3932160 | tf_op jit(solution)/shard_map/all_gather | solution.py:22
  246.7 253.2 %all-gather.13.cloned.1.call-start = ((), (), s32[]{:S(2)}) async-start(), calls=%async_computation.20 | async-start | bytes 3932160 | tf_op jit(solution)/shard_map/all_gather | solution.py:22
  249.9 115.7 %copy-start.51 = (f32[384]{0:T(512)}, f32[384]{0:T(512)S(1)}, u32[]{:S(2)}) copy-start(f32[384]{0:T(512)S(1)} %convert_element_type.231) | copy-start | bytes 4612
  366.8 548.6 %reduce-scatter.23.cloned.1.call-start = ((), (), s32[]{:S(2)}) async-start(), calls=%async_computation.22 | async-start | bytes 26214400 | tf_op jit(solution)/shard_map/reduce_scatter | solution.py:253
  762.4 188.3 %all-reduce.5.cloned.1.call-start = ((), (), s32[]{:S(2)}) async-start(), calls=%async_computation.24 | async-start | bytes 655360 | tf_op jit(solution)/shard_map/psum | solution.py:224
  766.4 258.2 %all-gather.17.cloned.1.call-start = ((), (), s32[]{:S(2)}) async-start(), calls=%async_computation.23 | async-start | bytes 13107200 | tf_op jit(solution)/shard_map/all_gather | solution.py:26
  925.9 225.7 %all-reduce.7.cloned.1.call-start = ((), (), s32[]{:S(2)}) async-start(), calls=%async_computation.29 | async-start | bytes 163840 | tf_op jit(solution)/shard_map/psum | solution.py:267
  926.0 947.9 %copy-start.17 = (s32[32768]{0:T(1024)}, s32[32768]{0:T(1024)S(1)}, u32[]{:S(2)}) copy-start(s32[32768]{0:T(1024)S(1)} %broadcast_clamp_fusion) | copy-start | bytes 393220
  1066.2 570.5 %reduce-scatter.27.cloned.1.call-start = ((), (), s32[]{:S(2)}) async-start(), calls=%async_computation.26 | async-start | bytes 26214400 | tf_op jit(solution)/shard_map/reduce_scatter | solution.py:30
  1334.7 147.7 %copy-start.21 = (f32[4096,8]{0,1:T(8,128)}, f32[4096,8]{0,1:T(8,128)S(1)}, u32[]{:S(2)}) copy-start(f32[4096,8]{0,1:T(8,128)S(1)} %copy.249) | copy-start | bytes 393220
  1335.4 147.0 %copy-start.23 = (f32[4096,8]{0,1:T(8,128)}, f32[4096,8]{0,1:T(8,128)S(1)}, u32[]{:S(2)}) copy-start(f32[4096,8]{0,1:T(8,128)S(1)} %get-tuple-element.70) | copy-start | bytes 393220
  1482.5 298.8 %all-gather.19.cloned.1.call-start = ((), (), s32[]{:S(2)}) async-start(), calls=%async_computation.27 | async-start | bytes 26214400 | tf_op jit(solution)/shard_map/all_gather | solution.py:26
  1646.7 557.5 %reduce-scatter.29.cloned.1.call-start = ((), (), s32[]{:S(2)}) async-start(), calls=%async_computation.28 | async-start | bytes 7864320 | tf_op jit(solution)/shard_map/reduce_scatter | solution.py:39
  2093.2 111.0 %copy-start.6 = (f32[1024,384]{1,0:T(8,128)S(1)}, f32[1024,384]{1,0:T(8,128)}, u32[]{:S(2)}) copy-start(f32[1024,384]{1,0:T(8,128)} %copy-done.5) | copy-start | bytes 4718596
  2093.3 186.5 %all-gather.21.cloned.1.call-start = ((), (), s32[]{:S(2)}) async-start(), calls=%async_computation.30 | async-start | bytes 3932160 | tf_op jit(solution)/shard_map/all_gather | solution.py:22
  2216.5 127.0 %reduce-scatter.31.cloned.1.call-start = ((), (), s32[]{:S(2)}) async-start(), calls=%async_computation.31 | async-start | bytes 7864320 | tf_op jit(solution)/shard_map/reduce_scatter | solution.py:30
  2286.4 173.1 %all-gather.23.cloned.1.call-start = ((), (), s32[]{:S(2)}) async-start(), calls=%async_computation.32 | async-start | bytes 6553600 | tf_op jit(solution)/shard_map/all_gather | solution.py:26
  2398.3 395.6 %reduce-scatter.49.cloned.1.call-start = ((), (), s32[]{:S(2)}) async-start(), calls=%async_computation.41 | async-start | bytes 147456
  2400.7 394.7 %reduce-scatter.47.cloned.1.call-start = ((), (), s32[]{:S(2)}) async-start(), calls=%async_computation.40 | async-start | bytes 5898240 | tf_op jit(solution)/shard_map/reduce_scatter | solution.py:398
  2427.0 372.3 %reduce-scatter.43.cloned.1.call-start = ((), (), s32[]{:S(2)}) async-start(), calls=%async_computation.38 | async-start | bytes 5898240 | tf_op jit(solution)/shard_map/reduce_scatter | solution.py:386
  2453.1 350.8 %reduce-scatter.45.cloned.1.call-start = ((), (), s32[]{:S(2)}) async-start(), calls=%async_computation.39 | async-start | bytes 5898240 | tf_op jit(solution)/shard_map/reduce_scatter | solution.py:392
  2453.7 354.3 %reduce-scatter.41.cloned.1.call-start = ((), (), s32[]{:S(2)}) async-start(), calls=%async_computation.37 | async-start | bytes 442368 | tf_op jit(solution)/shard_map/reduce_scatter | solution.py:380
  2459.4 350.2 %reduce-scatter.37.cloned.1.call-start = ((), (), s32[]{:S(2)}) async-start(), calls=%async_computation.35 | async-start | bytes 147456 | tf_op jit(solution)/shard_map/reduce_scatter | solution.py:368
  2467.5 343.6 %reduce-scatter.39.cloned.1.call-start = ((), (), s32[]{:S(2)}) async-start(), calls=%async_computation.36 | async-start | bytes 147456 | tf_op jit(solution)/shard_map/reduce_scatter | solution.py:374
  2468.3 344.3 %reduce-scatter.35.cloned.1.call-start = ((), (), s32[]{:S(2)}) async-start(), calls=%async_computation.34 | async-start | bytes 442368 | tf_op jit(solution)/shard_map/reduce_scatter | solution.py:362
  2469.1 345.1 %reduce-scatter.33.cloned.1.call-start = ((), (), s32[]{:S(2)}) async-start(), calls=%async_computation.33 | async-start | bytes 7864320 | tf_op jit(solution)/shard_map/reduce_scatter | solution.py:39
  2477.6 428.4 %reduce-scatter.25.cloned.1.call-start = ((), (), s32[]{:S(2)}) async-start(), calls=%async_computation.25 | async-start | bytes 7864320 | tf_op jit(solution)/shard_map/reduce_scatter | solution.py:39
  (55 other events, 1496.9 us)
Sparse Core Ops, SparseCore 0:
  20.7 63.7 all-gather.8
  93.7 83.9 reduce-scatter.18
  210.9 28.5 all-gather.10
  246.3 110.7 reduce-scatter.20
  358.5 64.0 all-gather.14
  424.5 62.1 all-gather.12
  762.5 152.7 reduce-scatter.22
  918.4 32.3 all-reduce.4
  953.0 71.5 all-gather.16
  1066.3 85.2 all-reduce.6
  1482.6 154.0 reduce-scatter.26
  1646.8 134.3 all-gather.18
  2093.4 110.7 reduce-scatter.28
  2216.6 63.0 all-gather.20
  2286.5 56.9 reduce-scatter.30
  2398.4 40.5 all-gather.22
  2441.6 9.9 reduce-scatter.48
  2454.3 51.9 reduce-scatter.46
  2509.2 51.9 reduce-scatter.42
  2563.9 51.9 reduce-scatter.44
  2618.8 12.0 reduce-scatter.40
  2633.8 9.9 reduce-scatter.36
  2646.6 9.9 reduce-scatter.38
  2659.4 12.0 reduce-scatter.34
  2673.9 110.7 reduce-scatter.32
  2794.0 111.9 reduce-scatter.24
where the time goes:
time: 2920 us
  waiting for transfers between devices  1150 us (39%)
  local copies, waits for them, and re-layouts  1130 us (39%)
  other arithmetic  288 us (10%)
  matrix products  275 us (9%)
  blocking collectives  51.6 us (2%)
    reduce_scatter x3, waiting for transfers between devices, column_sums(): lax.psum_scatter(term_fn(jnp.int32(0), keep_rows * lax.axis_size('col')),...  291 us
    reduce_scatter x4, waiting for transfers between devices, token_sums(): lax.psum_scatter(partial_rows, 'row', scatter_dimension=0, tiled=True)  243 us
    all_gather x4, waiting for transfers between devices, gather_columns(): return lax.all_gather(block, 'col', axis=0, tiled=True)  235 us
    gather x1, local copies, waits for them, and re-layouts, on_device(): paired_rows[slot_owner].reshape(CAP, expert_count, 2 * feature_width)  185 us
    gather x1, local copies, waits for them, and re-layouts, on_device(): gate_grads = slot_gate_grads.reshape(-1)[slot_flat].reshape(group_rows, -1)  181 us
    gather x1, local copies, waits for them, and re-layouts, on_device(): weighted[slot_flat].reshape(group_rows, top_count, -1)  150 us
    gather x1, local copies, waits for them, and re-layouts, on_device(): input_part.reshape(-1, input_part.shape[2])[slot_flat]  150 us
    reduce_scatter x1, waiting for transfers between devices, on_device(): lax.psum_scatter(jnp.einsum('ced,edh->ceh', expert_inputs, both_weights,...  149 us
  transfers between devices with their start and end apart: 26, of which 14 were waited for; matrix products, arithmetic and copies ran while one was open for 21% of the time, Pallas kernels for 0%

commit v1 on v0

v1 whole, which is shorter than its diff:
```python
import jax
import jax.numpy as jnp
from jax import lax
from jax.sharding import PartitionSpec as P

MODEL_WIDTH = 1536
HEAD_SIZE = 64
SEQUENCE_LENGTH = 1024
epsilon = 1e-06
f32 = jnp.float32
bf16 = jnp.bfloat16


def swap(block, axis, bit):
    size = lax.axis_size(axis)
    return lax.ppermute(block, axis, [(i, i ^ bit) for i in range(size)])


def bits_down(size):
    return [1 << i for i in reversed(range((size - 1).bit_length()))]


def gather_col(block):
    size = lax.axis_size("col")
    blocks = {0: block}
    for bit in bits_down(size):
        for k in sorted(blocks):
            blocks[k | bit] = swap(blocks[k], "col", bit)
    return [blocks[k] for k in range(size)]


def sum_col(parts, send_dtype=bf16):
    size = lax.axis_size("col")
    parts = dict(enumerate(parts))
    for bit in reversed(bits_down(size)):
        for k in sorted(parts):
            if k & bit:
                arrived = swap(parts.pop(k).astype(send_dtype), "col", bit)
                parts[k ^ bit] = parts[k ^ bit] + arrived.astype(f32)
    return parts[0]


def shift_row(block, step):
    size = lax.axis_size("row")
    return lax.ppermute(block, "row", [(i, (i + step) % size) for i in range(size)])


def gather_row_line(block):
    size = lax.axis_size("row")
    row = lax.axis_index("row")
    from_left, from_right = [block], [block]
    for k in range(1, size):
        from_left.append(
            lax.ppermute(from_left[-1], "row", [(i, i + 1) for i in range(k - 1, size - 1)])
        )
        from_right.append(
            lax.ppermute(from_right[-1], "row", [(i + 1, i) for i in range(0, size - k)])
        )
    return [block] + [
        jnp.where(row >= k, from_left[k], from_right[size - k]) for k in range(1, size)
    ]


def sum_dp(block, dimension):
    size = lax.axis_size("dp")
    index = lax.axis_index("dp")
    part = block.shape[dimension] // size

    def piece(owner):
        return lax.dynamic_slice_in_dim(block, owner * part, part, dimension)

    total = piece(index).astype(f32)
    for step in range(1, size):
        arrived = lax.ppermute(
            piece(lax.rem(index + step, size)),
            "dp",
            [(i, (i + step) % size) for i in range(size)],
        )
        total = total + arrived.astype(f32)
    return total.astype(bf16)


def rotation_tables(positions):
    half_width = HEAD_SIZE // 2
    frequency = 10000.0 ** (-jnp.arange(half_width).astype(f32) / half_width)
    angles = positions.astype(f32)[:, None] * frequency[None, :]
    return (jnp.cos(angles)[:, None, :], jnp.sin(angles)[:, None, :])


def rotate(values_in, cosine, sine_part, direction):
    half_width = HEAD_SIZE // 2
    first_half = values_in[..., :half_width]
    second = values_in[..., half_width:]
    return jnp.concatenate(
        [
            first_half * cosine - direction * second * sine_part,
            second * cosine + direction * first_half * sine_part,
        ],
        axis=-1,
    )


def doc_mask(sequence_lengths):
    positions = jnp.arange(SEQUENCE_LENGTH)
    doc_ends = jnp.cumsum(sequence_lengths)
    doc_ids = jnp.sum((positions[:, None] >= doc_ends[None, :]).astype(jnp.int32), axis=1)
    return (doc_ids[:, None] == doc_ids[None, :]) & (positions[:, None] >= positions[None, :])


def score_block(query_matrix, projected_keys, sequence_lengths):
    local_kv = projected_keys.shape[1] // HEAD_SIZE
    grouped_queries = query_matrix.reshape(SEQUENCE_LENGTH, local_kv, -1, HEAD_SIZE)
    key_heads = projected_keys.reshape(SEQUENCE_LENGTH, local_kv, HEAD_SIZE)
    scores = jnp.einsum(
        "qkgd,skd->kgqs", grouped_queries, key_heads, preferred_element_type=f32
    ) * HEAD_SIZE ** (-0.5)
    return (
        jnp.where(doc_mask(sequence_lengths)[None, None], scores, -1e30),
        grouped_queries,
        key_heads,
    )


def attend_forward(query_matrix, projected_keys, projected_values, sequence_lengths):
    scores, grouped_queries, key_heads = score_block(query_matrix, projected_keys, sequence_lengths)
    top_score = jnp.max(scores, axis=-1, keepdims=True)
    expo_scores = jnp.exp(scores - top_score)
    totals = jnp.sum(expo_scores, axis=-1, keepdims=True)
    softmax_probs = (expo_scores / totals).astype(bf16)
    value_heads = projected_values.reshape(SEQUENCE_LENGTH, key_heads.shape[1], HEAD_SIZE)
    attention_output = jnp.einsum(
        "kgqs,skd->qkgd", softmax_probs, value_heads, preferred_element_type=f32
    )
    return (attention_output.reshape(SEQUENCE_LENGTH, -1), (top_score + jnp.log(totals))[..., 0])


def attend_backward(
    query_matrix, projected_keys, projected_values, sequence_lengths, log_totals, out_grad
):
    scores, grouped_queries, key_heads = score_block(query_matrix, projected_keys, sequence_lengths)
    softmax_probs = jnp.exp(scores - log_totals[..., None])
    local_kv = key_heads.shape[1]
    grad_grouped = out_grad.reshape(SEQUENCE_LENGTH, local_kv, -1, HEAD_SIZE)
    value_heads = projected_values.reshape(SEQUENCE_LENGTH, local_kv, HEAD_SIZE)
    prob_grads = jnp.einsum("qkgd,skd->kgqs", grad_grouped, value_heads, preferred_element_type=f32)
    score_grads = (
        softmax_probs * (prob_grads - jnp.sum(softmax_probs * prob_grads, axis=-1, keepdims=True))
    ).astype(bf16)
    query_grads = jnp.einsum(
        "kgqs,skd->qkgd", score_grads, key_heads, preferred_element_type=f32
    ) * HEAD_SIZE ** (-0.5)
    key_grads = jnp.einsum(
        "kgqs,qkgd->skd", score_grads, grouped_queries, preferred_element_type=f32
    ) * HEAD_SIZE ** (-0.5)
    value_grads = jnp.einsum(
        "kgqs,qkgd->skd", softmax_probs.astype(bf16), grad_grouped, preferred_element_type=f32
    )
    return (
        query_grads.reshape(SEQUENCE_LENGTH, -1),
        key_grads.reshape(SEQUENCE_LENGTH, -1),
        value_grads.reshape(SEQUENCE_LENGTH, -1),
    )


def row_totals(per_row):
    return lax.psum(per_row, "col")


def two_parts(values):
    high = values.astype(bf16)
    return jnp.concatenate([high, (values - high.astype(f32)).astype(bf16)], axis=1)


def on_device(
    activations,
    cotangent,
    gain_one,
    gain_two,
    w_query,
    key_projection_weight,
    value_projection_weight,
    w_out,
    w_router,
    w_gate,
    w_up,
    w_down,
    routes,
    doc_lengths,
):
    n_col = lax.axis_size("col")
    n_row = lax.axis_size("row")
    col = lax.axis_index("col")
    row = lax.axis_index("row")
    local_rows, width = activations.shape
    sequences = local_rows // SEQUENCE_LENGTH
    query_width = w_query.shape[1]
    kv_width = key_projection_weight.shape[1]
    qkv_width = query_width + 2 * kv_width
    local_q = query_width // HEAD_SIZE
    local_kv = kv_width // HEAD_SIZE
    expert_count = w_router.shape[1]
    own_experts = expert_count // n_col
    hidden_width = w_gate.shape[2]
    own_width = own_experts * hidden_width
    relative = [jnp.bitwise_xor(col, k) for k in range(n_col)]

    attn_weight = jnp.concatenate(
        [w_query, key_projection_weight, value_projection_weight, w_out.T], axis=1
    )
    swapped = lax.ppermute(
        attn_weight,
        ("row", "col"),
        [(r * n_col + c, c * n_col + r) for r in range(n_row) for c in range(n_col)],
    )
    attn_blocks = lax.all_gather(swapped, "row", axis=0)
    attn_rel = jnp.concatenate(
        [lax.dynamic_index_in_dim(attn_blocks, relative[k], 0, False) for k in range(n_col)], axis=0
    )
    qkv_weight = attn_rel[:, :qkv_width]
    out_weight = attn_rel[:, qkv_width:]

    gain_one_f = gain_one.astype(f32)
    gain_two_f = gain_two.astype(f32)
    inputs_f = activations.astype(f32)
    inverse_one = lax.rsqrt(
        row_totals(jnp.sum(inputs_f * inputs_f, axis=1)) / MODEL_WIDTH + epsilon
    )
    scaled_one = inputs_f * inverse_one[:, None]
    normed_one = jnp.concatenate(
        gather_col((scaled_one * gain_one_f).astype(bf16)), axis=1
    )

    w_gate, w_up, w_down, cot_held, router_held, _ = lax.optimization_barrier(
        (w_gate, w_up, w_down, cotangent, w_router, normed_one)
    )

    def expert_block(k):
        start = relative[k] * own_experts
        gate = lax.dynamic_slice_in_dim(w_gate, start, own_experts, 0)
        up = lax.dynamic_slice_in_dim(w_up, start, own_experts, 0)
        down = lax.dynamic_slice_in_dim(w_down, start, own_experts, 0)
        return (
            jnp.concatenate(
                [
                    jnp.transpose(gate, (1, 0, 2)).reshape(width, own_width),
                    jnp.transpose(up, (1, 0, 2)).reshape(width, own_width),
                ],
                axis=1,
            ),
            down.reshape(own_width, width),
        )

    held = []
    for k in range(n_col):
        block = expert_block(k)
        if k:
            block = tuple(swap(part, "col", k) for part in block)
        held.append(block)
    gate_up_weight = jnp.concatenate([part[0] for part in held], axis=0)
    down_weight = jnp.concatenate([part[1] for part in held], axis=1)
    router_weight = jnp.concatenate(gather_col(router_held), axis=0)

    def gather_tokens(block):
        return [jnp.concatenate(gather_col(part), axis=1) for part in gather_row_line(block)]

    cot_blocks = gather_tokens(cot_held)

    qkv = jnp.dot(normed_one, qkv_weight, preferred_element_type=f32)
    positions = jnp.arange(local_rows) % SEQUENCE_LENGTH
    cosine, sine_part = rotation_tables(positions)
    query_matrix = (
        rotate(qkv[:, :query_width].reshape(-1, local_q, HEAD_SIZE), cosine, sine_part, 1.0)
        .astype(bf16)
        .reshape(-1, query_width)
    )
    projected_keys = (
        rotate(
            qkv[:, query_width : query_width + kv_width].reshape(-1, local_kv, HEAD_SIZE),
            cosine,
            sine_part,
            1.0,
        )
        .astype(bf16)
        .reshape(-1, kv_width)
    )
    projected_values = qkv[:, query_width + kv_width :].astype(bf16)
    own_lengths = lax.dynamic_slice_in_dim(doc_lengths, row * sequences, sequences, 0)

    def sequence(array, s):
        return array[s * SEQUENCE_LENGTH : (s + 1) * SEQUENCE_LENGTH]

    attended, log_totals = zip(
        *[
            attend_forward(
                sequence(query_matrix, s),
                sequence(projected_keys, s),
                sequence(projected_values, s),
                own_lengths[s],
            )
            for s in range(sequences)
        ]
    )
    attended = jnp.concatenate(attended, axis=0).astype(bf16)

    def feature_parts(left, weight):
        return [
            jnp.einsum(
                "tj,dj->td", left, weight[k * width : (k + 1) * width], preferred_element_type=f32
            )
            for k in range(n_col)
        ]

    hidden = inputs_f + sum_col(feature_parts(attended, out_weight))
    inverse_two = lax.rsqrt(row_totals(jnp.sum(hidden * hidden, axis=1)) / MODEL_WIDTH + epsilon)
    scaled_two = hidden * inverse_two[:, None]
    normed_two = (scaled_two * gain_two_f).astype(bf16)
    normed_blocks = gather_tokens(normed_two)

    expert_ids = jnp.arange(expert_count)
    spread = (
        jnp.arange(own_experts)[:, None] == (jnp.arange(own_width) // hidden_width)[None, :]
    ).astype(bf16)
    spread_twice = jnp.concatenate([spread, spread], axis=0)

    mixed, token_terms, gate_terms = [], [], []
    weighted_all, grads_all = [], []
    own_gates = own_routed = None
    for k in range(n_row):
        source = lax.rem(row - k + n_row, n_row)
        block = normed_blocks[k]
        block_routes = lax.dynamic_slice_in_dim(routes, source * local_rows, local_rows, 0)
        routed = jnp.any(block_routes[:, :, None] == expert_ids[None, None, :], axis=1)
        logits = jnp.dot(block, router_weight, preferred_element_type=f32)
        logits = jnp.where(routed, logits, -1e30)
        raised = jnp.where(routed, jnp.exp(logits - jnp.max(logits, axis=1, keepdims=True)), 0.0)
        gates = raised / jnp.sum(raised, axis=1, keepdims=True)
        if k == 0:
            own_gates, own_routed = gates, routed
        gates_here = lax.dynamic_slice_in_dim(gates, col * own_experts, own_experts, 1)
        gate_wide = jnp.dot(two_parts(gates_here), spread_twice, preferred_element_type=f32)
        inner_raw = jnp.einsum("td,jd->tj", cot_blocks[k], down_weight, preferred_element_type=f32)
        gate_act = jnp.dot(block, gate_up_weight[:, :own_width], preferred_element_type=f32)
        up_act = jnp.dot(block, gate_up_weight[:, own_width:], preferred_element_type=f32)
        sigmoid_gate = jax.nn.sigmoid(gate_act)
        silu_gate = gate_act * sigmoid_gate
        inner = silu_gate * up_act
        inner_grads = gate_wide * inner_raw
        gate_terms.append(
            jnp.dot((inner * inner_raw).astype(bf16), spread.T, preferred_element_type=f32)
        )
        weighted = (gate_wide * inner).astype(bf16)
        gate_grad_act = (
            inner_grads * up_act * sigmoid_gate * (1.0 + gate_act * (1.0 - sigmoid_gate))
        ).astype(bf16)
        up_grad_act = (inner_grads * silu_gate).astype(bf16)
        both = jnp.concatenate([gate_grad_act, up_grad_act], axis=1)
        token_terms.append(sum_col(feature_parts(both, gate_up_weight)))
        weighted_all.append(weighted)
        grads_all.append(both)

    def sum_row(terms, send_dtype=bf16):
        total = terms[0]
        for k in range(1, n_row):
            total = total + shift_row(terms[k].astype(send_dtype), -k).astype(f32)
        return total

    gate_grads_here = sum_row(gate_terms, f32)
    gate_grads = lax.all_gather(gate_grads_here.T, "col", axis=0, tiled=True).T
    chosen_grads = own_gates * (
        gate_grads - jnp.sum(own_gates * gate_grads, axis=1, keepdims=True)
    )
    logit_grads = jnp.where(own_routed, chosen_grads, 0.0).astype(bf16)
    router_grad = jnp.einsum("gd,ge->ed", normed_two, logit_grads, preferred_element_type=f32)
    router_input_grads = jnp.einsum("ge,de->gd", logit_grads, w_router, preferred_element_type=f32)

    normed_two_grads = sum_row(token_terms) + router_input_grads
    grad_scaled_two = normed_two_grads * gain_two_f
    stat_two = row_totals(jnp.sum(grad_scaled_two * scaled_two, axis=1)) / MODEL_WIDTH
    hidden_grads = cotangent.astype(f32) + inverse_two[:, None] * (
        grad_scaled_two - scaled_two * stat_two[:, None]
    )
    gain_two_part = jnp.sum(normed_two_grads * scaled_two, axis=0)
    branch_grads = jnp.concatenate(gather_col(hidden_grads.astype(bf16)), axis=1)

    weighted_rows = jnp.concatenate(weighted_all, axis=0)
    down_grad = jnp.einsum(
        "tj,td->jd", weighted_rows, jnp.concatenate(cot_blocks, axis=0), preferred_element_type=f32
    ).astype(bf16)
    gate_up_grad = jnp.einsum(
        "td,tj->dj",
        jnp.concatenate(normed_blocks, axis=0),
        jnp.concatenate(grads_all, axis=0),
        preferred_element_type=f32,
    ).astype(bf16)
    mixed = [
        sum_col(
            [
                jnp.dot(
                    part, down_weight[:, k * width : (k + 1) * width], preferred_element_type=f32
                )
                for k in range(n_col)
            ]
        )
        for part in weighted_all
    ]
    block_out = (hidden + sum_row(mixed)).astype(bf16)

    gate_up_half = sum_dp(gate_up_grad.reshape(n_col, width, 2 * own_width), 1)
    half = gate_up_half.shape[1]
    down_half = jnp.transpose(
        sum_dp(down_grad.reshape(own_width, n_col, width), 2), (1, 0, 2)
    )
    gate_grad = jnp.zeros((expert_count, half, hidden_width), f32)
    up_grad = jnp.zeros((expert_count, half, hidden_width), f32)
    down_out = jnp.zeros((expert_count, hidden_width, half), f32)
    for k in range(n_col):
        both, down = gate_up_half[k], down_half[k]
        if k:
            both, down = swap(both, "col", k), swap(down, "col", k)
        start = relative[k] * own_experts
        gate_part = jnp.transpose(
            both[:, :own_width].reshape(half, own_experts, hidden_width), (1, 0, 2)
        ).astype(f32)
        up_part = jnp.transpose(
            both[:, own_width:].reshape(half, own_experts, hidden_width), (1, 0, 2)
        ).astype(f32)
        down_part = down.reshape(own_experts, hidden_width, half).astype(f32)
        gate_grad = lax.dynamic_update_slice_in_dim(gate_grad, gate_part, start, 0)
        up_grad = lax.dynamic_update_slice_in_dim(up_grad, up_part, start, 0)
        down_out = lax.dynamic_update_slice_in_dim(down_out, down_part, start, 0)

    attended_grads = jnp.dot(branch_grads, out_weight, preferred_element_type=f32).astype(bf16)
    query_grads, key_grads, value_grads = (
        jnp.concatenate(parts, axis=0)
        for parts in zip(
            *[
                attend_backward(
                    sequence(query_matrix, s),
                    sequence(projected_keys, s),
                    sequence(projected_values, s),
                    own_lengths[s],
                    log_totals[s],
                    sequence(attended_grads, s),
                )
                for s in range(sequences)
            ]
        )
    )
    query_grads = rotate(
        query_grads.reshape(-1, local_q, HEAD_SIZE), cosine, sine_part, -1.0
    ).reshape(-1, query_width)
    key_grads = rotate(key_grads.reshape(-1, local_kv, HEAD_SIZE), cosine, sine_part, -1.0).reshape(
        -1, kv_width
    )
    qkv_grads = jnp.concatenate([query_grads, key_grads, value_grads], axis=1).astype(bf16)
    normed_one_grads = sum_col(feature_parts(qkv_grads, qkv_weight))

    attn_grad = jnp.concatenate(
        [
            jnp.einsum("td,tj->dj", normed_one, qkv_grads, preferred_element_type=f32),
            jnp.einsum("td,tj->dj", branch_grads, attended, preferred_element_type=f32),
        ],
        axis=1,
    ).astype(bf16)
    attn_grad = attn_grad.reshape(n_col, width, -1)
    attn_grad = jnp.concatenate(
        [
            lax.dynamic_index_in_dim(attn_grad, jnp.bitwise_xor(col, j), 0, False)
            for j in range(n_col)
        ],
        axis=0,
    )
    attn_grad = lax.psum_scatter(attn_grad, "row", scatter_dimension=0, tiled=True)
    attn_grad = lax.ppermute(
        attn_grad,
        ("row", "col"),
        [(r * n_col + c, c * n_col + r) for r in range(n_row) for c in range(n_col)],
    )
    attn_grad = lax.psum_scatter(
        jnp.concatenate([attn_grad[:, :qkv_width], attn_grad[:, qkv_width:].T], axis=1),
        "dp",
        scatter_dimension=0,
        tiled=True,
    ).astype(f32)

    grad_scaled_one = normed_one_grads * gain_one_f
    stat_one = row_totals(jnp.sum(grad_scaled_one * scaled_one, axis=1)) / MODEL_WIDTH
    input_grad = (
        hidden_grads + inverse_one[:, None] * (grad_scaled_one - scaled_one * stat_one[:, None])
    ).astype(bf16)
    gain_one_part = jnp.sum(normed_one_grads * scaled_one, axis=0)
    sums = lax.psum(
        jnp.concatenate([gain_one_part[None], gain_two_part[None], router_grad], axis=0),
        ("dp", "row"),
    )
    router_out = lax.dynamic_slice_in_dim(sums[2:], lax.axis_index("dp") * half, half, 1).T
    return (
        block_out,
        input_grad,
        sums[0],
        sums[1],
        attn_grad[:, :query_width],
        attn_grad[:, query_width : query_width + kv_width],
        attn_grad[:, query_width + kv_width : qkv_width],
        attn_grad[:, qkv_width:],
        router_out,
        gate_grad,
        up_grad,
        down_out,
    )


def solution(mesh):
    placed = (
        P(("dp", "row"), "col"),
        P(("dp", "row"), "col"),
        P("col"),
        P("col"),
        P("col", "row"),
        P("col", "row"),
        P("col", "row"),
        P("row", "col"),
        P("col", None),
        P(None, "col", "row"),
        P(None, "col", "row"),
        P(None, "row", "col"),
        P("dp", None),
        P("dp", None),
    )
    return jax.shard_map(
        on_device,
        mesh=mesh,
        in_specs=placed,
        out_specs=(
            P(("dp", "row"), "col"),
            P(("dp", "row"), "col"),
            P("col"),
            P("col"),
            P(("col", "dp"), "row"),
            P(("col", "dp"), "row"),
            P(("col", "dp"), "row"),
            P(("row", "dp"), "col"),
            P(("col", "dp"), None),
            P(None, ("col", "dp"), "row"),
            P(None, ("col", "dp"), "row"),
            P(None, "row", ("col", "dp")),
        ),
        check_vma=False,
    )
```

time: 2920 us -> 1300 us (0.45)
  local copies, waits for them, and re-layouts: 1130 us -> 154 us
  waiting for transfers between devices: 1150 us -> 255 us
  matrix products: 275 us -> 531 us
  other arithmetic: 288 us -> 110 us
  starting transfers between devices: 2.03 us -> 111 us
  blocking collectives: 51.6 us -> 114 us
    reduce_scatter x15 -> x0, waiting for transfers between devices: 683 us -> none  [the longest x3 291 us: column_sums(): lax.psum_scatter(term_fn(jnp.int32(0), keep_rows * lax.axis_size('col')),...]
    gather x4 -> x0, local copies, waits for them, and re-layouts: 665 us -> none  [the longest x1 185 us: on_device(): paired_rows[slot_owner].reshape(CAP, expert_count, 2 * feature_width)]
    all_gather x8 -> x1, waiting for transfers between devices: 359 us -> 0.01 us  [on_device(): attn_blocks = lax.all_gather(swapped, 'row', axis=0)]
    ppermute x0 -> x100, waiting for transfers between devices: none -> 255 us  [the longest x75 189 us: swap(): return lax.ppermute(block, axis, [(i, i ^ bit) for i in range(size)])]
    dot_general x17 -> x73, matrix products: 235 us -> 489 us  [the longest x1 109 us: on_device(): jnp.einsum('td,tj->dj', jnp.concatenate(normed_blocks, axis=0), jnp.conca...]
    scatter x2 -> x0, local copies, waits for them, and re-layouts: 240 us -> none  [the longest x1 120 us: on_device(): slot_gate = jnp.zeros((CAP * expert_count,), jnp.float32).at[slot_flat].s...]
    reduce_sum x8 -> x6, other arithmetic: 152 us -> 5.71 us  [the longest x1 4.23 us: on_device(): gain_two_part = jnp.sum(normed_two_grads * scaled_two, axis=0)]
    ppermute x0 -> x100, starting transfers between devices: none -> 111 us  [the longest x75 42.9 us: swap(): return lax.ppermute(block, axis, [(i, i ^ bit) for i in range(size)])]
  transfers between devices with their start and end apart: 26 -> 103, of which waited for: 14 -> 21; matrix products, arithmetic and copies ran while one was open for 21% -> 60% of each run, Pallas kernels for 0% -> 0%
where the time goes in v1:
time: 1300 us; the launch traced here: 1290 us
  matrix products  531 us (41%)
  waiting for transfers between devices  255 us (20%)
  local copies, waits for them, and re-layouts  154 us (12%)
  blocking collectives  114 us (9%)
  starting transfers between devices  111 us (9%)
  other arithmetic  110 us (8%)
  between operations  16.6 us (1%)
    ppermute x75, waiting for transfers between devices, swap(): return lax.ppermute(block, axis, [(i, i ^ bit) for i in range(size)])  189 us
    dot_general x1, matrix products, on_device(): jnp.einsum('td,tj->dj', jnp.concatenate(normed_blocks, axis=0), jnp.conca...  109 us
    dot_general x24, matrix products, feature_parts(): jnp.einsum('tj,dj->td', left, weight[k * width:(k + 1) * width], preferre...  93.2 us
    psum x1, blocking collectives, on_device(): lax.psum(jnp.concatenate([gain_one_part[None], gain_two_part[None], route...  60.6 us
    dot_general x1, matrix products, on_device(): jnp.einsum('tj,td->jd', weighted_rows, jnp.concatenate(cot_blocks, axis=0...  59.8 us
    ppermute x6, waiting for transfers between devices, gather_row_line(): lax.ppermute(from_right[-1], 'row', [(i + 1, i) for i in range(0, size -...  48 us
    dot_general x4, matrix products, on_device(): jnp.dot(block, gate_up_weight[:, :own_width], preferred_element_type=f32)  48 us
    dot_general x16, matrix products, on_device(): jnp.dot(part, down_weight[:, k * width:(k + 1) * width], preferred_elemen...  44.8 us
  transfers between devices with their start and end apart: 103, of which 21 were waited for; matrix products, arithmetic and copies ran while one was open for 60% of the time, Pallas kernels for 0%

profile of v1, /device:TPU:0, one launch (start us, length us, event | category | flops | bytes accessed | tf_op | source)
XLA Modules:
  0.0 1292.6 jit_solution(10726888891667223017)
XLA Ops:
  26.7 13.8 %psum.35 = f32[1024]{0:T(1024)S(1)} all-reduce(f32[1024]{0:T(1024)S(1)} %fusion.180), channel_id=1, replica_groups=mesh['dp'=2,'row'=4,'col'=4] {'col'}, use_global_device_ids=true, to_apply=%region_1.2 | all-reduce | flops 1024 | bytes 8192 | tf_op jit(solution)/shard_map/psum | solution.py:166
  86.0 16.8 %collective-permute-done.18 = bf16[1280,384]{1,0:T(8,128)(2,1)S(1)} collective-permute-done((bf16[1280,384]{1,0:T(8,128)(2,1)}, bf16[1280,384]{1,0:T(8,128)(2,1)S(1)}, u32[]{:S(2)}, u32[]{:S(2)}) %collective-permute-start.18) | collective-permute-done | bytes 983072 | tf_op jit(solution)/shard_map/ppermute | solution.py:16
  104.3 31.2 %collective-permute-done.57 = bf16[1024,384]{0,1:T(8,128)(2,1)} collective-permute-done((bf16[1024,384]{0,1:T(8,128)(2,1)}, bf16[1024,384]{0,1:T(8,128)(2,1)}, u32[]{:S(2)}, u32[]{:S(2)}) %collective-permute-start.57) | collective-permute-done | bytes 786464 | tf_op jit(solution)/shard_map/ppermute | solution.py:57
  143.0 64.6 %collective-permute-done.19 = bf16[1280,384]{1,0:T(8,128)(2,1)} collective-permute-done((bf16[1280,384]{1,0:T(8,128)(2,1)}, bf16[1280,384]{1,0:T(8,128)(2,1)}, u32[]{:S(2)}, u32[]{:S(2)}) %collective-permute-start.19) | collective-permute-done | bytes 983072 | tf_op jit(solution)/shard_map/ppermute | solution.py:16
  208.1 9.6 fusion.110
  220.8 11.2 pad_maximum_fusion
  259.5 10.8 fusion.181
  282.4 8.5 fusion.126
  294.3 16.8 %collective-permute-done.76 = bf16[1024,384]{0,1:T(8,128)(2,1)} collective-permute-done((bf16[1024,384]{0,1:T(8,128)(2,1)}, bf16[1024,384]{0,1:T(8,128)(2,1)}, u32[]{:S(2)}, u32[]{:S(2)}) %collective-permute-start.76) | collective-permute-done | bytes 786464 | tf_op jit(solution)/shard_map/ppermute | solution.py:16
  311.7 15.4 %collective-permute-done.6 = bf16[1024,384]{0,1:T(8,128)(2,1)S(1)} collective-permute-done((bf16[1024,384]{0,1:T(8,128)(2,1)S(1)}, bf16[1024,384]{0,1:T(8,128)(2,1)S(1)}, u32[]{:S(2)}, u32[]{:S(2)}) %collective-permute-start.6) | collective-permute-done | bytes 786464 | tf_op jit(solution)/shard_map/ppermute | solution.py:16
  342.6 9.3 fusion.118
  359.0 8.8 fusion.134
  368.3 9.8 collective-permute-done.24
  413.6 13.9 %multiply_convert_fusion.7 = (bf16[1024,1280]{1,0:T(8,128)(2,1)}, bf16[1024,1280]{1,0:T(8,128)(2,1)}, bf16[1024,1280]{1,0:T(8,128)(2,1)}, f32[1024,1280]{1,0:T(8,128)}) fusion(f32[1024,1280]{1,0:T(8,128)} %fusion.148, f32[1024,1280]{1,0:T(8,128)S(1)} %fusion.239, f32[1024,1280]{1,0:T(8,128)} %fusion.126, bf16[1536,2560]{0,1:T(8,128)(2,1)} %pad_maximum_fusion, ...), kind=kOutput, calls=%fused_computation.115 | convolution fusion | flops 4061396992 | bytes 35913728 | tf_op jit(solution)/shard_map/dot_general | solution.py:342
  435.4 14.4 %collective-permute-start.83 = (f32[1024,10]{0,1:T(8,128)}, f32[1024,10]{0,1:T(8,128)}, u32[]{:S(2)}, u32[]{:S(2)}) collective-permute-start(f32[1024,10]{0,1:T(8,128)} %fusion.144), channel_id=1, source_target_pairs={{0,8},{4,12},{8,0},{12,4},{1,9},{5,13},{9,1},{13,5},{2,10},{6,14},... | collective-permute-start | bytes 122888 | tf_op jit(solution)/shard_map/ppermute | solution.py:45
  485.4 14.0 %multiply_convert_fusion.9 = (bf16[1024,1280]{1,0:T(8,128)(2,1)}, bf16[1024,1280]{1,0:T(8,128)(2,1)}, bf16[1024,1280]{1,0:T(8,128)(2,1)}, f32[1024,1280]{1,0:T(8,128)}) fusion(f32[1024,1280]{1,0:T(8,128)} %fusion.150, f32[1024,1280]{1,0:T(8,128)S(1)} %fusion.235, f32[1024,1280]{1,0:T(8,128)} %fusion.118, bf16[1536,2560]{0,1:T(8,128)(2,1)} %pad_maximum_fusion, ...), kind=kOutput, calls=%fused_computation.117 | convolution fusion | flops 4061396992 | bytes 35913728 | tf_op jit(solution)/shard_map/dot_general | solution.py:342
  513.0 8.4 fusion.146
  521.4 14.2 %multiply_convert_fusion.5 = (bf16[1024,1280]{1,0:T(8,128)(2,1)}, bf16[1024,1280]{1,0:T(8,128)(2,1)}, bf16[1024,1280]{1,0:T(8,128)(2,1)}, f32[1024,1280]{1,0:T(8,128)}) fusion(f32[1024,1280]{1,0:T(8,128)} %fusion.146, f32[1024,1280]{1,0:T(8,128)S(1)} %fusion.243, f32[1024,1280]{1,0:T(8,128)} %fusion.134, bf16[1536,2560]{0,1:T(8,128)(2,1)} %pad_maximum_fusion, ...), kind=kOutput, calls=%fused_computation.113 | convolution fusion | flops 4061396992 | bytes 35913728 | tf_op jit(solution)/shard_map/dot_general | solution.py:342
  600.2 19.4 %all-gather.1 = f32[4,10,1024]{2,1,0:T(8,128)S(1)} all-gather(f32[1,10,1024]{2,1,0:T(8,128)S(1)} %fusion.204), channel_id=1, replica_groups=mesh['dp'=2,'row'=4,'col'=4] {'col'}, dimensions={0}, use_global_device_ids=true | all-gather | bytes 204800 | tf_op jit(solution)/shard_map/all_gather | solution.py:368
  635.0 59.8 %fusion.100 = bf16[1280,1536]{1,0:T(8,128)(2,1)} fusion(bf16[1024,384]{0,1:T(8,128)(2,1)} %collective-permute-done.77, bf16[1024,384]{0,1:T(8,128)(2,1)} %collective-permute-done.76, bf16[1024,384]{0,1:T(8,128)(2,1)} %collective-permute-done.75, bf16[1024,384]{0,1:T(8,128)(2,1)} %broadcast_select_fusion, bf16[1024,384]{0,1:T(8,128)(2,1)} %copy-done.129, ...), kind=kOutput, calls=%fused_computation.103 | convolution fusion | flops 16351363072 | bytes 27000832 | tf_op jit(solution)/shard_map/tj,td->jd/dot_general | solution.py:386
  694.8 108.8 %fusion.88 = bf16[1536,2560]{1,0:T(8,128)(2,1)} fusion(bf16[1024,1280]{1,0:T(8,128)(2,1)} %get-tuple-element.117, bf16[1024,1280]{1,0:T(8,128)(2,1)} %get-tuple-element.116, bf16[1024,1280]{1,0:T(8,128)(2,1)} %get-tuple-element.114, bf16[1024,1280]{1,0:T(8,128)(2,1)} %get-tuple-element.113, bf16[1024,1280]{1,0:T(8,128)(2,1)} %get-tuple-element.111, ...), kind=kOutput, calls=%fused_computation.93 | convolution fusion | flops 32585285632 | bytes 41418752 | tf_op jit(solution)/shard_map/td,tj->dj/dot_general | solution.py:389
  842.2 8.9 collective-permute-done.64
  856.2 11.7 collective-permute-done.80
  886.4 9.3 collective-permute-done.73
  908.6 8.9 psum.37
  948.4 16.1 %fusion = (f32[2,3,1024]{2,1,0:T(4,128)S(1)}, f32[2,1024,1024,3]{2,1,3,0:T(8,128)}) fusion(f32[2,3,1024,1024]{2,3,1,0:T(8,128)} %copy-done.2, f32[2,3,1024]{2,1,0:T(4,128)S(1)} %copy-done.84, bf16[1024,2,64,1]{0,2,3,1:T(8,128)(2,1)S(1)} %bitcast.298, bf16[1024,2,3,64]{0,3,2,1:T(8,128)(2,1)S(1)} %bitcast.284), kind=kOutput, calls=%fused_computation.2 | convolution fusion | flops 824174592 | bytes 51429376 | tf_op jit(solution)/shard_map/qkgd,skd->kgqs/dot_general | solution.py:145
  964.5 16.9 %fusion.2 = bf16[2,3,1024,1024]{2,3,1,0:T(8,128)(2,1)S(1)} fusion(f32[2,1024,1024,3]{2,1,3,0:T(8,128)} %get-tuple-element.190, f32[2,3,1024,1024]{2,3,1,0:T(8,128)} %copy-done.2, f32[2,3,1024]{2,1,0:T(4,128)S(1)} %get-tuple-element.189, f32[2,3,1024]{2,1,0:T(4,128)S(1)} %copy-done.84), kind=kLoop, calls=%fused_computation.4 | loop fusion | flops 25165824 | bytes 62963712 | tf_op jit(solution)/shard_map/convert_element_type | solution.py:148
  1000.4 10.5 fusion.191
  1044.2 10.4 collective-permute-done.47
  1113.6 12.1 collective-permute-done.94
  1131.1 14.8 %collective-permute-done.95 = bf16[192,2560]{1,0:T(8,128)(2,1)} collective-permute-done((bf16[192,2560]{1,0:T(8,128)(2,1)S(1)}, bf16[192,2560]{1,0:T(8,128)(2,1)}, u32[]{:S(2)}, u32[]{:S(2)}) %collective-permute-start.95) | collective-permute-done | bytes 983072 | tf_op jit(solution)/shard_map/ppermute | solution.py:16
  1201.4 60.6 %psum.39 = f32[42,384]{1,0:T(8,128)S(1)} all-reduce(f32[42,384]{1,0:T(8,128)S(1)} %pad_maximum_fusion.26), channel_id=1, replica_groups=mesh['dp'=2,'row'=4,'col'=4] {'dp','row'}, use_global_device_ids=true, to_apply=%region_28.29 | all-reduce | flops 16128 | bytes 129024 | tf_op jit(solution)/shard_map/psum | solution.py:492
  (790 shorter events, 616.0 us)
Async XLA Ops:
  7.2 224.7 %all-gather.4.cloned.1.call-start = ((), (), s32[]{:S(2)}) async-start(), calls=%async_computation.2 | async-start | bytes 3932160 | tf_op jit(solution)/shard_map/all_gather | solution.py:215
  9.6 71.6 %collective-permute-start.56 = (bf16[1024,384]{0,1:T(8,128)(2,1)}, bf16[1024,384]{0,1:T(8,128)(2,1)}, u32[]{:S(2)}, u32[]{:S(2)}) collective-permute-start(bf16[1024,384]{0,1:T(8,128)(2,1)} %copy.425), channel_id=1, source_target_pairs={{4,0},{8,4},{12,8},{5,1},{9,5},{13,9},{6,2},{10,6},{14,10},{7,3},{... | collective-permute-start | bytes 2359304 | tf_op jit(solution)/shard_map/ppermute | solution.py:57
  10.9 71.2 %collective-permute-start.55 = (bf16[1024,384]{0,1:T(8,128)(2,1)}, bf16[1024,384]{0,1:T(8,128)(2,1)}, u32[]{:S(2)}, u32[]{:S(2)}) collective-permute-start(bf16[1024,384]{0,1:T(8,128)(2,1)} %copy.425), channel_id=1, source_target_pairs={{0,4},{4,8},{8,12},{1,5},{5,9},{9,13},{2,6},{6,10},{10,14},{3,7},{... | collective-permute-start | bytes 2359304 | tf_op jit(solution)/shard_map/ppermute | solution.py:54
  69.1 1059.6 %reduce-scatter.7.cloned.1.call-start = ((), (), s32[]{:S(2)}) async-start(), calls=%async_computation.3 | async-start | bytes 3932160
  85.4 132.3 %collective-permute-start.13 = (bf16[384,2560]{0,1:T(8,128)(2,1)}, bf16[384,2560]{0,1:T(8,128)(2,1)}, u32[]{:S(2)}, u32[]{:S(2)}) collective-permute-start(bf16[384,2560]{0,1:T(8,128)(2,1)} %pad_maximum_fusion.15), channel_id=1, source_target_pairs={{0,1},{1,0},{2,3},{3,2},{4,5},{5,4},{6,7},{7,6},{8,9},{9,8},{10,11... | collective-permute-start | bytes 5898248 | tf_op jit(solution)/shard_map/ppermute | solution.py:16
  85.9 133.4 %collective-permute-start.14 = (bf16[384,2560]{0,1:T(8,128)(2,1)}, bf16[384,2560]{0,1:T(8,128)(2,1)}, u32[]{:S(2)}, u32[]{:S(2)}) collective-permute-start(bf16[384,2560]{0,1:T(8,128)(2,1)} %pad_maximum_fusion.16), channel_id=1, source_target_pairs={{0,2},{1,3},{2,0},{3,1},{4,6},{5,7},{6,4},{7,5},{8,10},{9,11},{10,... | collective-permute-start | bytes 5898248 | tf_op jit(solution)/shard_map/ppermute | solution.py:16
  102.8 116.6 %collective-permute-start.15 = (bf16[384,2560]{0,1:T(8,128)(2,1)}, bf16[384,2560]{0,1:T(8,128)(2,1)}, u32[]{:S(2)}, u32[]{:S(2)}) collective-permute-start(bf16[384,2560]{0,1:T(8,128)(2,1)} %pad_maximum_fusion.17), channel_id=1, source_target_pairs={{0,3},{1,2},{2,1},{3,0},{4,7},{5,6},{6,5},{7,4},{8,11},{9,10},{10,... | collective-permute-start | bytes 5898248 | tf_op jit(solution)/shard_map/ppermute | solution.py:16
  135.5 72.1 %collective-permute-start.19 = (bf16[1280,384]{1,0:T(8,128)(2,1)}, bf16[1280,384]{1,0:T(8,128)(2,1)}, u32[]{:S(2)}, u32[]{:S(2)}) collective-permute-start(bf16[1280,384]{1,0:T(8,128)(2,1)} %bitcast.307), channel_id=1, source_target_pairs={{0,3},{1,2},{2,1},{3,0},{4,7},{5,6},{6,5},{7,4},{8,11},{9,10},{10,... | collective-permute-start | bytes 2949128 | tf_op jit(solution)/shard_map/ppermute | solution.py:16
  135.7 72.1 %collective-permute-start.51 = (bf16[1024,384]{0,1:T(8,128)(2,1)}, bf16[1024,384]{0,1:T(8,128)(2,1)}, u32[]{:S(2)}, u32[]{:S(2)}) collective-permute-start(bf16[1024,384]{0,1:T(8,128)(2,1)} %collective-permute-done.50), channel_id=1, source_target_pairs={{0,1},{1,0},{2,3},{3,2},{4,5},{5,4},{6,7},{7,6},{8,9},{9,8},{10,11... | collective-permute-start | bytes 2359304 | tf_op jit(solution)/shard_map/ppermute | solution.py:16
  404.9 102.4 %collective-permute-start.42 = (bf16[1024,384]{0,1:T(8,128)(2,1)}, bf16[1024,384]{0,1:T(8,128)(2,1)}, u32[]{:S(2)}, u32[]{:S(2)}) collective-permute-start(bf16[1024,384]{0,1:T(8,128)(2,1)} %broadcast_select_fusion.1), channel_id=1, source_target_pairs={{0,1},{1,0},{2,3},{3,2},{4,5},{5,4},{6,7},{7,6},{8,9},{9,8},{10,11... | collective-permute-start | bytes 2359304 | tf_op jit(solution)/shard_map/ppermute | solution.py:16
  435.4 161.6 %collective-permute-start.83 = (f32[1024,10]{0,1:T(8,128)}, f32[1024,10]{0,1:T(8,128)}, u32[]{:S(2)}, u32[]{:S(2)}) collective-permute-start(f32[1024,10]{0,1:T(8,128)} %fusion.144), channel_id=1, source_target_pairs={{0,8},{4,12},{8,0},{12,4},{1,9},{5,13},{9,1},{13,5},{2,10},{6,14},... | collective-permute-start | bytes 122888 | tf_op jit(solution)/shard_map/ppermute | solution.py:45
  472.5 357.8 %collective-permute-start.70 = (bf16[1024,384]{0,1:T(8,128)(2,1)}, bf16[1024,384]{0,1:T(8,128)(2,1)}, u32[]{:S(2)}, u32[]{:S(2)}) collective-permute-start(bf16[1024,384]{0,1:T(8,128)(2,1)} %convolution_convert_fusion.18), channel_id=1, source_target_pairs={{0,1},{1,0},{2,3},{3,2},{4,5},{5,4},{6,7},{7,6},{8,9},{9,8},{10,11... | collective-permute-start | bytes 2359304 | tf_op jit(solution)/shard_map/ppermute | solution.py:16
  472.8 111.7 %collective-permute-start.71 = (bf16[1024,384]{0,1:T(8,128)(2,1)}, bf16[1024,384]{0,1:T(8,128)(2,1)}, u32[]{:S(2)}, u32[]{:S(2)}) collective-permute-start(bf16[1024,384]{0,1:T(8,128)(2,1)} %convolution_convert_fusion.17), channel_id=1, source_target_pairs={{0,1},{1,0},{2,3},{3,2},{4,5},{5,4},{6,7},{7,6},{8,9},{9,8},{10,11... | collective-permute-start | bytes 2359304 | tf_op jit(solution)/shard_map/ppermute | solution.py:16
  507.3 84.2 %collective-permute-start.38 = (bf16[1024,384]{0,1:T(8,128)(2,1)}, bf16[1024,384]{0,1:T(8,128)(2,1)}, u32[]{:S(2)}, u32[]{:S(2)}) collective-permute-start(bf16[1024,384]{0,1:T(8,128)(2,1)} %convolution_convert_fusion.4), channel_id=1, source_target_pairs={{0,1},{1,0},{2,3},{3,2},{4,5},{5,4},{6,7},{7,6},{8,9},{9,8},{10,11... | collective-permute-start | bytes 2359304 | tf_op jit(solution)/shard_map/ppermute | solution.py:16
  507.6 89.9 %collective-permute-start.82 = (f32[1024,10]{0,1:T(8,128)}, f32[1024,10]{0,1:T(8,128)S(1)}, u32[]{:S(2)}, u32[]{:S(2)}) collective-permute-start(f32[1024,10]{0,1:T(8,128)} %fusion.143), channel_id=1, source_target_pairs={{0,12},{4,0},{8,4},{12,8},{1,13},{5,1},{9,5},{13,9},{2,14},{6,2},{... | collective-permute-start | bytes 122888 | tf_op jit(solution)/shard_map/ppermute | solution.py:45
  591.5 248.7 %collective-permute-start.62 = (bf16[1024,384]{0,1:T(8,128)(2,1)}, bf16[1024,384]{0,1:T(8,128)(2,1)}, u32[]{:S(2)}, u32[]{:S(2)}) collective-permute-start(bf16[1024,384]{0,1:T(8,128)(2,1)} %convolution_convert_fusion.20), channel_id=1, source_target_pairs={{0,1},{1,0},{2,3},{3,2},{4,5},{5,4},{6,7},{7,6},{8,9},{9,8},{10,11... | collective-permute-start | bytes 2359304 | tf_op jit(solution)/shard_map/ppermute | solution.py:16
  597.0 223.9 %collective-permute-start.63 = (bf16[1024,384]{0,1:T(8,128)(2,1)}, bf16[1024,384]{0,1:T(8,128)(2,1)}, u32[]{:S(2)}, u32[]{:S(2)}) collective-permute-start(bf16[1024,384]{0,1:T(8,128)(2,1)} %convolution_convert_fusion.19), channel_id=1, source_target_pairs={{0,1},{1,0},{2,3},{3,2},{4,5},{5,4},{6,7},{7,6},{8,9},{9,8},{10,11... | collective-permute-start | bytes 2359304 | tf_op jit(solution)/shard_map/ppermute | solution.py:16
  597.6 233.1 %collective-permute-start.72 = (bf16[1024,384]{0,1:T(8,128)(2,1)}, bf16[1024,384]{0,1:T(8,128)(2,1)}, u32[]{:S(2)}, u32[]{:S(2)}) collective-permute-start(bf16[1024,384]{0,1:T(8,128)(2,1)} %add_convert_fusion.6), channel_id=1, source_target_pairs={{0,2},{1,3},{2,0},{3,1},{4,6},{5,7},{6,4},{7,5},{8,10},{9,11},{10,... | collective-permute-start | bytes 2359304 | tf_op jit(solution)/shard_map/ppermute | solution.py:16
  597.7 228.2 %collective-permute-start.79 = (bf16[1024,384]{0,1:T(8,128)(2,1)}, bf16[1024,384]{0,1:T(8,128)(2,1)}, u32[]{:S(2)}, u32[]{:S(2)}) collective-permute-start(bf16[1024,384]{0,1:T(8,128)(2,1)} %convolution_convert_fusion.15), channel_id=1, source_target_pairs={{0,1},{1,0},{2,3},{3,2},{4,5},{5,4},{6,7},{7,6},{8,9},{9,8},{10,11... | collective-permute-start | bytes 2359304 | tf_op jit(solution)/shard_map/ppermute | solution.py:16
  923.4 116.3 %collective-permute-start.29 = (bf16[1024,384]{0,1:T(8,128)(2,1)}, bf16[1024,384]{0,1:T(8,128)(2,1)}, u32[]{:S(2)}, u32[]{:S(2)}) collective-permute-start(bf16[1024,384]{0,1:T(8,128)(2,1)} %convolution_convert_fusion.7), channel_id=1, source_target_pairs={{0,1},{1,0},{2,3},{3,2},{4,5},{5,4},{6,7},{7,6},{8,9},{9,8},{10,11... | collective-permute-start | bytes 2359304 | tf_op jit(solution)/shard_map/ppermute | solution.py:16
  923.4 116.3 %collective-permute-start.45 = (bf16[1024,384]{0,1:T(8,128)(2,1)}, bf16[1024,384]{0,1:T(8,128)(2,1)}, u32[]{:S(2)}, u32[]{:S(2)}) collective-permute-start(bf16[1024,384]{0,1:T(8,128)(2,1)} %convolution_convert_fusion.3), channel_id=1, source_target_pairs={{0,1},{1,0},{2,3},{3,2},{4,5},{5,4},{6,7},{7,6},{8,9},{9,8},{10,11... | collective-permute-start | bytes 2359304 | tf_op jit(solution)/shard_map/ppermute | solution.py:16
  942.1 91.9 %collective-permute-start.96 = (bf16[1280,4,192]{0,2,1:T(8,128)(2,1)}, bf16[1280,4,192]{0,2,1:T(8,128)(2,1)}, u32[]{:S(2)}, u32[]{:S(2)}) collective-permute-start(bf16[1280,4,192]{0,2,1:T(8,128)(2,1)} %constant_dynamic-slice_fusion), channel_id=1, source_target_pairs={{0,16},{16,0},{1,17},{17,1},{2,18},{18,2},{3,19},{19,3},{4,20},{20... | collective-permute-start | bytes 5898248 | tf_op jit(solution)/shard_map/ppermute | solution.py:74
  945.8 142.5 %collective-permute-start.92 = (bf16[4,192,2560]{2,1,0:T(8,128)(2,1)}, bf16[4,192,2560]{2,1,0:T(8,128)(2,1)}, u32[]{:S(2)}, u32[]{:S(2)}) collective-permute-start(bf16[4,192,2560]{2,1,0:T(8,128)(2,1)} %constant_dynamic-slice_fusion.1), channel_id=1, source_target_pairs={{0,16},{16,0},{1,17},{17,1},{2,18},{18,2},{3,19},{19,3},{4,20},{20... | collective-permute-start | bytes 11796488 | tf_op jit(solution)/shard_map/ppermute | solution.py:74
  946.4 93.7 %collective-permute-start.31 = (bf16[1024,384]{0,1:T(8,128)(2,1)}, bf16[1024,384]{0,1:T(8,128)(2,1)}, u32[]{:S(2)}, u32[]{:S(2)}) collective-permute-start(bf16[1024,384]{0,1:T(8,128)(2,1)} %add_convert_fusion.16), channel_id=1, source_target_pairs={{0,2},{1,3},{2,0},{3,1},{4,6},{5,7},{6,4},{7,5},{8,10},{9,11},{10,... | collective-permute-start | bytes 2359304 | tf_op jit(solution)/shard_map/ppermute | solution.py:16
  1033.9 247.4 %reduce-scatter.9.cloned.1.call-start = ((), (), s32[]{:S(2)}) async-start(), calls=%async_computation.4 | async-start | bytes 1179648
  1054.6 213.2 %collective-permute-start.17 = (bf16[1024,384]{0,1:T(8,128)(2,1)}, bf16[1024,384]{0,1:T(8,128)(2,1)}, u32[]{:S(2)}, u32[]{:S(2)}) collective-permute-start(bf16[1024,384]{0,1:T(8,128)(2,1)} %convolution_convert_fusion.9), channel_id=1, source_target_pairs={{0,1},{1,0},{2,3},{3,2},{4,5},{5,4},{6,7},{7,6},{8,9},{9,8},{10,11... | collective-permute-start | bytes 2359304 | tf_op jit(solution)/shard_map/ppermute | solution.py:16
  1063.1 204.7 %collective-permute-start.40 = (bf16[1024,384]{0,1:T(8,128)(2,1)}, bf16[1024,384]{0,1:T(8,128)(2,1)}, u32[]{:S(2)}, u32[]{:S(2)}) collective-permute-start(bf16[1024,384]{0,1:T(8,128)(2,1)} %add_convert_fusion.13), channel_id=1, source_target_pairs={{0,8},{4,12},{8,0},{12,4},{1,9},{5,13},{9,1},{13,5},{2,10},{6,14},... | collective-permute-start | bytes 2359304 | tf_op jit(solution)/shard_map/ppermute | solution.py:45
  1106.5 88.5 %collective-permute-start.88 = (bf16[1024,384]{0,1:T(8,128)(2,1)}, bf16[1024,384]{0,1:T(8,128)(2,1)}, u32[]{:S(2)}, u32[]{:S(2)}) collective-permute-start(bf16[1024,384]{0,1:T(8,128)(2,1)} %convolution_convert_fusion.11), channel_id=1, source_target_pairs={{0,1},{1,0},{2,3},{3,2},{4,5},{5,4},{6,7},{7,6},{8,9},{9,8},{10,11... | collective-permute-start | bytes 2359304 | tf_op jit(solution)/shard_map/ppermute | solution.py:16
  1125.7 69.4 %collective-permute-start.90 = (bf16[1024,384]{0,1:T(8,128)(2,1)}, bf16[1024,384]{0,1:T(8,128)(2,1)}, u32[]{:S(2)}, u32[]{:S(2)}) collective-permute-start(bf16[1024,384]{0,1:T(8,128)(2,1)} %add_convert_fusion.2), channel_id=1, source_target_pairs={{0,2},{1,3},{2,0},{3,1},{4,6},{5,7},{6,4},{7,5},{8,10},{9,11},{10,... | collective-permute-start | bytes 2359304 | tf_op jit(solution)/shard_map/ppermute | solution.py:16
  1183.8 84.0 %collective-permute-start.21 = (bf16[1024,384]{0,1:T(8,128)(2,1)}, bf16[1024,384]{0,1:T(8,128)(2,1)}, u32[]{:S(2)}, u32[]{:S(2)}) collective-permute-start(bf16[1024,384]{0,1:T(8,128)(2,1)} %add_convert_fusion.17), channel_id=1, source_target_pairs={{0,2},{1,3},{2,0},{3,1},{4,6},{5,7},{6,4},{7,5},{8,10},{9,11},{10,... | collective-permute-start | bytes 2359304 | tf_op jit(solution)/shard_map/ppermute | solution.py:16
  1195.1 72.8 %collective-permute-start.32 = (bf16[1024,384]{0,1:T(8,128)(2,1)}, bf16[1024,384]{0,1:T(8,128)(2,1)}, u32[]{:S(2)}, u32[]{:S(2)}) collective-permute-start(bf16[1024,384]{0,1:T(8,128)(2,1)} %add_convert_fusion.15), channel_id=1, source_target_pairs={{0,12},{4,0},{8,4},{12,8},{1,13},{5,1},{9,5},{13,9},{2,14},{6,2},{... | collective-permute-start | bytes 2359304 | tf_op jit(solution)/shard_map/ppermute | solution.py:45
  1195.1 72.7 %collective-permute-start.48 = (bf16[1024,384]{0,1:T(8,128)(2,1)}, bf16[1024,384]{0,1:T(8,128)(2,1)}, u32[]{:S(2)}, u32[]{:S(2)}) collective-permute-start(bf16[1024,384]{0,1:T(8,128)(2,1)} %add_convert_fusion.11), channel_id=1, source_target_pairs={{0,4},{4,8},{8,12},{12,0},{1,5},{5,9},{9,13},{13,1},{2,6},{6,10},{... | collective-permute-start | bytes 2359304 | tf_op jit(solution)/shard_map/ppermute | solution.py:45
  (250 other events, 5641.8 us)
Sparse Core Ops, SparseCore 0:
  69.2 84.4 all-gather.3
  1034.1 82.8 reduce-scatter.6
  1195.2 18.0 reduce-scatter.8

commit v2 on v1

v2 whole, which is shorter than its diff:
```python
import jax
import jax.numpy as jnp
from jax import lax
from jax.experimental import pallas as pl
from jax.experimental.pallas import tpu as pltpu
from jax.sharding import PartitionSpec as P

MODEL_WIDTH = 1536
HEAD_SIZE = 64
SEQUENCE_LENGTH = 1024
epsilon = 1e-06
f32 = jnp.float32
bf16 = jnp.bfloat16
LANES = 128
PAIR = 2
CHUNK = 512
VMEM_LIMIT = 60 * 1024 * 1024


def swap(block, axis, bit):
    size = lax.axis_size(axis)
    return lax.ppermute(block, axis, [(i, i ^ bit) for i in range(size)])


def bits_down(size):
    return [1 << i for i in reversed(range((size - 1).bit_length()))]


def gather_col(block):
    size = lax.axis_size("col")
    blocks = {0: block}
    for bit in bits_down(size):
        for k in sorted(blocks):
            blocks[k | bit] = swap(blocks[k], "col", bit)
    return [blocks[k] for k in range(size)]


def col_stage(parts, bit):
    kept = {}
    for k in sorted(parts):
        if not k & bit:
            arrived = swap(parts[k | bit].astype(bf16), "col", bit)
            kept[k] = parts[k].astype(f32) + arrived.astype(f32)
    return kept


def sum_col(parts):
    parts = dict(enumerate(parts))
    for bit in reversed(bits_down(lax.axis_size("col"))):
        parts = col_stage(parts, bit)
    return parts[0]


def after(values, *others):
    return lax.optimization_barrier((values, others))[0]


def crossed(n_row, n_col, bit):
    return [(r * n_col + c, c * n_col + (r ^ bit)) for r in range(n_row) for c in range(n_col)]


def gather_row_line(block):
    size = lax.axis_size("row")
    row = lax.axis_index("row")
    from_left, from_right = [block], [block]
    for k in range(1, size):
        from_left.append(
            lax.ppermute(from_left[-1], "row", [(i, i + 1) for i in range(k - 1, size - 1)])
        )
        from_right.append(
            lax.ppermute(from_right[-1], "row", [(i + 1, i) for i in range(0, size - k)])
        )
    return [block] + [
        jnp.where(row >= k, from_left[k], from_right[size - k]) for k in range(1, size)
    ]


def transposed_dot(left, right):
    return lax.dot_general(left, right, (((1,), (1,)), ((), ())), preferred_element_type=f32)


def expert_kernel(n_col, own_experts, hidden_width, first, scalars, *refs):
    refs = list(refs)

    def take(count):
        return [refs.pop(0) for _ in range(count)]

    x, cot = take(n_col), take(n_col)
    mask, router = take(2)
    gate, up, down = take(n_col), take(n_col), take(n_col)
    if not first:
        take(1)
    token_out = take(n_col)
    mix_out, gate_grad_out, up_grad_out, weighted_out, gates_out, terms_out = take(6)
    token_acc, mix_acc, terms_acc = take(3)
    rows, width = x[0].shape
    step = pl.program_id(0)
    lane = lax.broadcasted_iota(jnp.int32, (CHUNK, LANES), 1)

    @pl.when(step == 0)
    def _():
        token_acc[...] = jnp.zeros_like(token_acc)
        mix_acc[...] = jnp.zeros_like(mix_acc)
        terms_acc[...] = jnp.zeros_like(terms_acc)
        for start in range(0, rows, CHUNK):
            span = slice(start, start + CHUNK)
            here = jnp.concatenate([part[span, :] for part in x], axis=1)
            logits = jnp.dot(here, router[...], preferred_element_type=f32) + mask[span, :]
            raised = jnp.exp(logits - jnp.max(logits, axis=1, keepdims=True))
            gates_out[span, :] = raised / jnp.sum(raised, axis=1, keepdims=True)

    def pair(parts, axis):
        return [jnp.concatenate([part[i] for i in range(PAIR)], axis=axis) for part in parts]

    gate_w = jnp.concatenate(pair(gate, 1), axis=0)
    up_w = jnp.concatenate(pair(up, 1), axis=0)
    down_w = jnp.concatenate(pair(down, 0), axis=1)
    own_first = scalars[1] + PAIR * step
    for start in range(0, rows, CHUNK):
        span = slice(start, start + CHUNK)
        here = jnp.concatenate([part[span, :] for part in x], axis=1)
        there = jnp.concatenate([part[span, :] for part in cot], axis=1)
        gate_act = jnp.dot(here, gate_w, preferred_element_type=f32)
        up_act = jnp.dot(here, up_w, preferred_element_type=f32)
        raw = transposed_dot(there, down_w)
        gates = gates_out[span, :]
        wide = jnp.concatenate(
            [
                jnp.broadcast_to(
                    jnp.sum(jnp.where(lane == own_first + i, gates, 0.0), axis=1, keepdims=True),
                    (CHUNK, hidden_width),
                )
                for i in range(PAIR)
            ],
            axis=1,
        )
        sigmoid_gate = 1.0 / (1.0 + jnp.exp(-gate_act))
        silu_gate = gate_act * sigmoid_gate
        inner = silu_gate * up_act
        terms = inner * raw
        found = terms_acc[span, :]
        for i in range(PAIR):
            total = jnp.sum(
                terms[:, i * hidden_width : (i + 1) * hidden_width], axis=1, keepdims=True
            )
            found = jnp.where(lane == PAIR * step + i, total, found)
        terms_acc[span, :] = found
        inner_grads = wide * raw
        weighted = (wide * inner).astype(bf16)
        gate_grad = (
            inner_grads * up_act * sigmoid_gate * (1.0 + gate_act * (1.0 - sigmoid_gate))
        ).astype(bf16)
        up_grad = (inner_grads * silu_gate).astype(bf16)
        weighted_out[span, :] = weighted
        gate_grad_out[span, :] = gate_grad
        up_grad_out[span, :] = up_grad
        token_acc[span, :] += transposed_dot(
            jnp.concatenate([gate_grad, up_grad], axis=1),
            jnp.concatenate([gate_w, up_w], axis=1),
        )
        mix_acc[span, :] += jnp.dot(weighted, down_w, preferred_element_type=f32)

    @pl.when(step == pl.num_programs(0) - 1)
    def _():
        for k in range(n_col):
            columns = slice(k * width, (k + 1) * width)
            token_out[k][...] = token_acc[:, columns].astype(bf16)
            mix_out[scalars[2 + n_col + k]] = mix_acc[:, columns].astype(bf16)
        terms_out[...] = terms_acc[...].T[: terms_out.shape[0], :]


def expert_block(source, x, cot_all, mask, router, gate, up, down, mix):
    n_col = len(x)
    rows, width = x[0].shape
    own_experts, hidden_width = gate[1].shape[0], gate[1].shape[2]
    own_width = own_experts * hidden_width
    term_rows = -(-own_experts // 8) * 8
    col = lax.axis_index("col")
    others = [jnp.bitwise_xor(col, k) for k in range(n_col)]
    scalars = jnp.stack(
        [source, col * own_experts] + [source * n_col + other for other in others] + others
    ).astype(jnp.int32)
    once = pl.Buffered(1)
    whole = pl.BlockSpec((rows, width), lambda p, s: (0, 0), pipeline_mode=once)

    def cot_spec(k):
        return pl.BlockSpec((None, rows, width), lambda p, s: (s[2 + k], 0, 0), pipeline_mode=once)

    def weight_specs(parts):
        size = (PAIR,) + parts[0].shape[1:]
        return [pl.BlockSpec(size, lambda p, s: (s[1] // PAIR + p, 0, 0))] + [
            pl.BlockSpec(size, lambda p, s: (p, 0, 0))
        ] * (n_col - 1)

    in_specs = (
        [whole] * n_col
        + [cot_spec(k) for k in range(n_col)]
        + [
            pl.BlockSpec((rows, LANES), lambda p, s: (s[0], 0), pipeline_mode=once),
            pl.BlockSpec(router.shape, lambda p, s: (0, 0), pipeline_mode=once),
        ]
        + weight_specs(gate)
        + weight_specs(up)
        + weight_specs(down)
    )
    operands = [*x, *([cot_all] * n_col), mask, router, *gate, *up, *down]
    aliases = {}
    if mix is not None:
        in_specs.append(pl.BlockSpec(memory_space=pl.ANY))
        operands.append(mix)
        aliases = {len(operands): n_col}
    pair_columns = pl.BlockSpec((rows, PAIR * hidden_width), lambda p, s: (0, p))
    out = pl.pallas_call(
        lambda *refs: expert_kernel(n_col, own_experts, hidden_width, mix is None, *refs),
        grid_spec=pltpu.PrefetchScalarGridSpec(
            num_scalar_prefetch=1,
            grid=(own_experts // PAIR,),
            in_specs=in_specs,
            out_specs=[pl.BlockSpec((rows, width), lambda p, s: (0, 0))] * n_col
            + [pl.BlockSpec((n_col, rows, width), lambda p, s: (s[0], 0, 0))]
            + [pair_columns] * 3
            + [
                pl.BlockSpec((rows, LANES), lambda p, s: (0, 0)),
                pl.BlockSpec((term_rows, rows), lambda p, s: (0, 0)),
            ],
            scratch_shapes=[pltpu.VMEM((rows, n_col * width), f32)] * 2
            + [pltpu.VMEM((rows, LANES), f32)],
        ),
        out_shape=[jax.ShapeDtypeStruct((rows, width), bf16)] * n_col
        + [jax.ShapeDtypeStruct(cot_all.shape, bf16)]
        + [jax.ShapeDtypeStruct((rows, own_width), bf16)] * 3
        + [
            jax.ShapeDtypeStruct((rows, LANES), f32),
            jax.ShapeDtypeStruct((term_rows, rows), f32),
        ],
        input_output_aliases=aliases,
        compiler_params=pltpu.CompilerParams(vmem_limit_bytes=VMEM_LIMIT),
        cost_estimate=pl.CostEstimate(
            flops=12 * rows * n_col * width * own_width,
            bytes_accessed=40 * 1024 * 1024,
            transcendentals=rows * own_width,
        ),
        name="experts",
    )(scalars, *operands)
    return out[:n_col], out[n_col], out[n_col + 1 :]


def weight_grad_kernel(n_col, n_row, n_dp, own, flip, scalars, *refs):
    lefts, rights, out = refs[:n_row], refs[n_row:-1], refs[-1]
    left = jnp.concatenate([part[...] for part in lefts], axis=0)
    hidden_width = left.shape[1] // PAIR
    if own:
        right = [
            jnp.concatenate([rights[0][scalars[1 + b * n_col + k]] for b in range(n_row)], axis=0)
            for k in range(n_col)
        ]
    else:
        right = [
            jnp.concatenate([rights[b * n_col + k][...] for b in range(n_row)], axis=0)
            for k in range(n_col)
        ]
    width = right[0].shape[1]
    part = width // n_dp
    total = lax.dot_general(
        left,
        jnp.concatenate(right, axis=1),
        (((0,), (0,)), ((), ())),
        preferred_element_type=f32,
    )
    if flip:
        total = total.T
    total = total.astype(bf16) if part % 16 == 0 else total
    for d in range(n_dp):
        place = lax.rem(d - scalars[0] + n_dp, n_dp)
        for k in range(n_col):
            span = slice(k * width + d * part, k * width + (d + 1) * part)
            for i in range(PAIR):
                units = slice(i * hidden_width, (i + 1) * hidden_width)
                piece = total[span, units] if flip else total[units, span]
                out[place, k, i] = piece.astype(bf16)


def weight_grad(lefts, rights, flip, own_experts):
    n_col, n_row, n_dp = lax.axis_size("col"), lax.axis_size("row"), lax.axis_size("dp")
    row, col = lax.axis_index("row"), lax.axis_index("col")
    rows, own_width = lefts[0].shape
    hidden_width = own_width // own_experts
    whole = not isinstance(rights, list)
    width = rights.shape[-1] if whole else rights[0].shape[-1]
    part = width // n_dp
    scalars = jnp.stack(
        [lax.axis_index("dp")]
        + [
            jnp.bitwise_xor(row, b) * n_col + jnp.bitwise_xor(col, k)
            for b in range(n_row)
            for k in range(n_col)
        ]
    ).astype(jnp.int32)
    once = pl.Buffered(1)
    if whole:
        right_specs = [pl.BlockSpec(rights.shape, lambda p, s: (0, 0, 0), pipeline_mode=once)]
        rights = [rights]
    else:
        right_specs = [
            pl.BlockSpec((rows, width), lambda p, s: (0, 0), pipeline_mode=once)
        ] * len(rights)
    tail = (part, hidden_width) if flip else (hidden_width, part)
    return pl.pallas_call(
        lambda *refs: weight_grad_kernel(n_col, n_row, n_dp, whole, flip, *refs),
        grid_spec=pltpu.PrefetchScalarGridSpec(
            num_scalar_prefetch=1,
            grid=(own_experts // PAIR,),
            in_specs=[pl.BlockSpec((rows, PAIR * hidden_width), lambda p, s: (0, p))] * n_row
            + right_specs,
            out_specs=pl.BlockSpec((n_dp, n_col, PAIR) + tail, lambda p, s: (0, 0, p, 0, 0)),
        ),
        out_shape=jax.ShapeDtypeStruct((n_dp, n_col, own_experts) + tail, bf16),
        compiler_params=pltpu.CompilerParams(vmem_limit_bytes=VMEM_LIMIT),
        cost_estimate=pl.CostEstimate(
            flops=2 * n_row * rows * n_col * width * own_width,
            bytes_accessed=20 * 1024 * 1024,
            transcendentals=0,
        ),
        name="weight_grads",
    )(scalars, *lefts, *rights)


def sum_dp(pieces):
    size = lax.axis_size("dp")
    total = pieces[0].astype(f32)
    for step in range(1, size):
        arrived = lax.ppermute(pieces[step], "dp", [(i, (i + step) % size) for i in range(size)])
        total = total + arrived.astype(f32)
    return total.astype(bf16)


def sum_all(values, axes):
    for axis in axes:
        for bit in bits_down(lax.axis_size(axis)):
            values = values + swap(values, axis, bit)
    return values


def rotation_tables(positions):
    half_width = HEAD_SIZE // 2
    frequency = 10000.0 ** (-jnp.arange(half_width).astype(f32) / half_width)
    angles = positions.astype(f32)[:, None] * frequency[None, :]
    return (jnp.cos(angles)[:, None, :], jnp.sin(angles)[:, None, :])


def rotate(values_in, cosine, sine_part, direction):
    half_width = HEAD_SIZE // 2
    first_half = values_in[..., :half_width]
    second = values_in[..., half_width:]
    return jnp.concatenate(
        [
            first_half * cosine - direction * second * sine_part,
            second * cosine + direction * first_half * sine_part,
        ],
        axis=-1,
    )


def doc_mask(sequence_lengths):
    positions = jnp.arange(SEQUENCE_LENGTH)
    doc_ends = jnp.cumsum(sequence_lengths)
    doc_ids = jnp.sum((positions[:, None] >= doc_ends[None, :]).astype(jnp.int32), axis=1)
    return (doc_ids[:, None] == doc_ids[None, :]) & (positions[:, None] >= positions[None, :])


def score_block(query_matrix, projected_keys, sequence_lengths):
    local_kv = projected_keys.shape[1] // HEAD_SIZE
    grouped_queries = query_matrix.reshape(SEQUENCE_LENGTH, local_kv, -1, HEAD_SIZE)
    key_heads = projected_keys.reshape(SEQUENCE_LENGTH, local_kv, HEAD_SIZE)
    scores = jnp.einsum(
        "qkgd,skd->kgqs", grouped_queries, key_heads, preferred_element_type=f32
    ) * HEAD_SIZE ** (-0.5)
    return (
        jnp.where(doc_mask(sequence_lengths)[None, None], scores, -1e30),
        grouped_queries,
        key_heads,
    )


def attend_forward(query_matrix, projected_keys, projected_values, sequence_lengths):
    scores, grouped_queries, key_heads = score_block(query_matrix, projected_keys, sequence_lengths)
    top_score = jnp.max(scores, axis=-1, keepdims=True)
    expo_scores = jnp.exp(scores - top_score)
    totals = jnp.sum(expo_scores, axis=-1, keepdims=True)
    softmax_probs = (expo_scores / totals).astype(bf16)
    value_heads = projected_values.reshape(SEQUENCE_LENGTH, key_heads.shape[1], HEAD_SIZE)
    attention_output = jnp.einsum(
        "kgqs,skd->qkgd", softmax_probs, value_heads, preferred_element_type=f32
    )
    return (attention_output.reshape(SEQUENCE_LENGTH, -1), (top_score + jnp.log(totals))[..., 0])


def attend_backward(
    query_matrix, projected_keys, projected_values, sequence_lengths, log_totals, out_grad
):
    scores, grouped_queries, key_heads = score_block(query_matrix, projected_keys, sequence_lengths)
    softmax_probs = jnp.exp(scores - log_totals[..., None])
    local_kv = key_heads.shape[1]
    grad_grouped = out_grad.reshape(SEQUENCE_LENGTH, local_kv, -1, HEAD_SIZE)
    value_heads = projected_values.reshape(SEQUENCE_LENGTH, local_kv, HEAD_SIZE)
    prob_grads = jnp.einsum("qkgd,skd->kgqs", grad_grouped, value_heads, preferred_element_type=f32)
    score_grads = (
        softmax_probs * (prob_grads - jnp.sum(softmax_probs * prob_grads, axis=-1, keepdims=True))
    ).astype(bf16)
    query_grads = jnp.einsum(
        "kgqs,skd->qkgd", score_grads, key_heads, preferred_element_type=f32
    ) * HEAD_SIZE ** (-0.5)
    key_grads = jnp.einsum(
        "kgqs,qkgd->skd", score_grads, grouped_queries, preferred_element_type=f32
    ) * HEAD_SIZE ** (-0.5)
    value_grads = jnp.einsum(
        "kgqs,qkgd->skd", softmax_probs.astype(bf16), grad_grouped, preferred_element_type=f32
    )
    return (
        query_grads.reshape(SEQUENCE_LENGTH, -1),
        key_grads.reshape(SEQUENCE_LENGTH, -1),
        value_grads.reshape(SEQUENCE_LENGTH, -1),
    )


def row_totals(per_row):
    return lax.psum(per_row, "col")


def on_device(
    activations,
    cotangent,
    gain_one,
    gain_two,
    w_query,
    key_projection_weight,
    value_projection_weight,
    w_out,
    w_router,
    w_gate,
    w_up,
    w_down,
    routes,
    doc_lengths,
):
    n_col = lax.axis_size("col")
    n_row = lax.axis_size("row")
    n_dp = lax.axis_size("dp")
    col = lax.axis_index("col")
    row = lax.axis_index("row")
    local_rows, width = activations.shape
    sequences = local_rows // SEQUENCE_LENGTH
    query_width = w_query.shape[1]
    kv_width = key_projection_weight.shape[1]
    local_q = query_width // HEAD_SIZE
    local_kv = kv_width // HEAD_SIZE
    expert_count = w_router.shape[1]
    own_experts = expert_count // n_col
    relative = [jnp.bitwise_xor(col, k) for k in range(n_col)]

    def all_features(blocks):
        return jnp.concatenate(
            [lax.dynamic_index_in_dim(blocks, relative[k], 0, False) for k in range(n_col)], axis=0
        )

    crossing = crossed(n_row, n_col, 0)
    qkv_crossed = lax.ppermute(
        jnp.concatenate([w_query, key_projection_weight, value_projection_weight], axis=1),
        ("row", "col"),
        crossing,
    )
    qkv_blocks = lax.all_gather(qkv_crossed, "row", axis=0)
    routed = jnp.any(routes[:, :, None] == jnp.arange(LANES)[None, None, :], axis=1)
    mask = jnp.where(routed, 0.0, -1e30).astype(f32)

    gain_one_f = gain_one.astype(f32)
    gain_two_f = gain_two.astype(f32)
    inputs_f = activations.astype(f32)
    inverse_one = lax.rsqrt(
        row_totals(jnp.sum(inputs_f * inputs_f, axis=1)) / MODEL_WIDTH + epsilon
    )
    scaled_one = inputs_f * inverse_one[:, None]
    normed_one = jnp.concatenate(gather_col((scaled_one * gain_one_f).astype(bf16)), axis=1)
    router_parts = gather_col(w_router.T)
    router_weight = jnp.concatenate(router_parts, axis=1).T
    router_weight = jnp.pad(router_weight, ((0, 0), (0, LANES - expert_count)))
    normed_one, mask, router_weight = lax.optimization_barrier((normed_one, mask, router_weight))

    def trade(weight):
        received = []
        for k in reversed(range(1, n_col)):
            block = lax.dynamic_slice_in_dim(weight, relative[k] * own_experts, own_experts, 0)
            received.insert(0, swap(block, "col", k))
        return received

    traded = [trade(weight) for weight in after((w_gate, w_up, w_down), normed_one)]
    out_crossed = lax.ppermute(after(w_out.T, normed_one), ("row", "col"), crossing)
    out_blocks = gather_row_line(out_crossed)
    qkv_blocks = after(qkv_blocks, normed_one)
    cot_all = lax.all_gather(after(cotangent, qkv_blocks), ("row", "col"), axis=0)
    qkv_weight = all_features(qkv_blocks)

    qkv = jnp.dot(normed_one, qkv_weight, preferred_element_type=f32)
    positions = jnp.arange(local_rows) % SEQUENCE_LENGTH
    cosine, sine_part = rotation_tables(positions)
    query_matrix = (
        rotate(qkv[:, :query_width].reshape(-1, local_q, HEAD_SIZE), cosine, sine_part, 1.0)
        .astype(bf16)
        .reshape(-1, query_width)
    )
    projected_keys = (
        rotate(
            qkv[:, query_width : query_width + kv_width].reshape(-1, local_kv, HEAD_SIZE),
            cosine,
            sine_part,
            1.0,
        )
        .astype(bf16)
        .reshape(-1, kv_width)
    )
    projected_values = qkv[:, query_width + kv_width :].astype(bf16)
    own_lengths = lax.dynamic_slice_in_dim(doc_lengths, row * sequences, sequences, 0)

    def sequence(array, s):
        return array[s * SEQUENCE_LENGTH : (s + 1) * SEQUENCE_LENGTH]

    attended, log_totals = zip(
        *[
            attend_forward(
                sequence(query_matrix, s),
                sequence(projected_keys, s),
                sequence(projected_values, s),
                own_lengths[s],
            )
            for s in range(sequences)
        ]
    )
    attended = jnp.concatenate(attended, axis=0).astype(bf16)

    def feature_parts(left, weight):
        return [
            jnp.einsum(
                "tj,dj->td", left, weight[k * width : (k + 1) * width], preferred_element_type=f32
            )
            for k in range(n_col)
        ]

    out_blocks = jnp.stack(after(out_blocks, attended))
    out_weight = jnp.concatenate(
        [
            lax.dynamic_index_in_dim(out_blocks, lax.rem(row - relative[k] + n_row, n_row), 0, False)
            for k in range(n_col)
        ],
        axis=0,
    )
    hidden = inputs_f + sum_col(feature_parts(attended, out_weight))
    inverse_two = lax.rsqrt(row_totals(jnp.sum(hidden * hidden, axis=1)) / MODEL_WIDTH + epsilon)
    scaled_two = hidden * inverse_two[:, None]
    normed_two = (scaled_two * gain_two_f).astype(bf16)

    from_rows = [normed_two] + [swap(normed_two, "row", k) for k in range(1, n_row)]
    top = bits_down(n_col)[0]
    traded, cot_all = after((traded, cot_all), normed_two)
    gate_parts, up_parts, down_parts = (
        [weight] + parts for weight, parts in zip((w_gate, w_up, w_down), traded)
    )
    stages = list(reversed(bits_down(n_col)))
    sums = [[] for _ in range(n_row)]

    def advance(chain):
        state, done = sums[chain], len(sums[chain]) - 1
        if done < len(stages):
            state.append(col_stage(state[-1], stages[done]))
        elif done == len(stages):
            value = state[-1][0]
            state.append({0: swap(value.astype(bf16), "row", chain) if chain else value})

    def arrived(call):
        found = []
        for chain in range(n_row):
            if chain <= call - 2 and len(sums[chain]) <= len(stages) + 1:
                advance(chain)
                found.append(sums[chain][-1])
        return found

    gate_terms, normed_blocks = [], []
    lefts = ([], [], [])
    own_gates = mix = None
    halfway = {0: swap(normed_two, "col", top)}
    for k in range(n_row):
        if k:
            halfway[k] = after(halfway[k], token_part)
        blocks = {0: from_rows[k], top: halfway[k]}
        for bit in bits_down(n_col)[1:]:
            for held in sorted(blocks):
                blocks[held | bit] = swap(blocks[held], "col", bit)
        block = [blocks[held] for held in range(n_col)]
        following = [1] if k == 0 else list(range(2, n_row)) if k == 1 else []
        for held in following:
            halfway[held] = swap(from_rows[held], "col", top)
        block = after(block, arrived(k), [from_rows[held] for held in following])
        normed_blocks.append(block)
        token_part, mix, rest = expert_block(
            jnp.bitwise_xor(row, k),
            block,
            cot_all,
            mask,
            router_weight,
            gate_parts,
            up_parts,
            down_parts,
            mix,
        )
        for left, part in zip(lefts, rest[:3]):
            left.append(part)
        if k == 0:
            own_gates = rest[3][:, :expert_count]
        gate_terms.append(swap(rest[4], "row", k) if k else rest[4])
        sums[k].append(dict(enumerate(token_part)))

    normed_parts = [part for block in normed_blocks for part in block]
    gate_sum = sum(gate_terms[: n_row - 1])
    down_pieces = weight_grad(
        after(lefts[2], arrived(n_row), gate_sum), cot_all, True, own_experts
    )
    gate_sum = gate_sum + gate_terms[-1]
    gate_pieces = weight_grad(
        after(lefts[0], arrived(n_row + 1), gate_sum, down_pieces), normed_parts, True, own_experts
    )
    gate_half = swap(gate_sum, "col", top)
    last_sums = arrived(n_row + 2)
    up_pieces = weight_grad(
        after(lefts[1], last_sums, gate_half, gate_pieces), normed_parts, True, own_experts
    )
    mixed = lax.psum_scatter(
        after(mix, last_sums), ("row", "col"), scatter_dimension=0, tiled=False
    )
    arrived(n_row + 3)
    token_sum, gate_blocks, _ = lax.optimization_barrier(
        ([state[-1][0] for state in sums], {0: gate_sum, top: gate_half}, up_pieces)
    )
    for bit in bits_down(n_col)[1:]:
        for held in sorted(gate_blocks):
            gate_blocks[held | bit] = swap(gate_blocks[held], "col", bit)
    gate_grads = jnp.zeros((expert_count, local_rows), f32)
    for k in range(n_col):
        gate_grads = lax.dynamic_update_slice_in_dim(
            gate_grads, gate_blocks[k][:own_experts], relative[k] * own_experts, 0
        )
    gate_grads = gate_grads.T
    chosen_grads = own_gates * (
        gate_grads - jnp.sum(own_gates * gate_grads, axis=1, keepdims=True)
    )
    logit_grads = chosen_grads.astype(bf16)
    router_grad = jnp.einsum("gd,ge->ed", normed_two, logit_grads, preferred_element_type=f32)
    router_input_grads = jnp.einsum("ge,de->gd", logit_grads, w_router, preferred_element_type=f32)

    normed_two_grads = sum(part.astype(f32) for part in token_sum) + router_input_grads
    grad_scaled_two = normed_two_grads * gain_two_f
    stat_two = row_totals(jnp.sum(grad_scaled_two * scaled_two, axis=1)) / MODEL_WIDTH
    hidden_grads = cotangent.astype(f32) + inverse_two[:, None] * (
        grad_scaled_two - scaled_two * stat_two[:, None]
    )
    gain_two_part = jnp.sum(normed_two_grads * scaled_two, axis=0)
    branch_grads = jnp.concatenate(gather_col(hidden_grads.astype(bf16)), axis=1)

    block_out = (hidden + mixed.astype(f32)).astype(bf16)

    half = width // n_dp

    def expert_grad(pieces):
        summed = sum_dp(pieces)
        total = jnp.zeros((expert_count,) + summed.shape[2:], f32)
        for k in range(n_col):
            part = swap(summed[k], "col", k) if k else summed[k]
            total = lax.dynamic_update_slice_in_dim(
                total, part.astype(f32), relative[k] * own_experts, 0
            )
        return total

    down_out = jnp.transpose(expert_grad(down_pieces), (0, 2, 1))
    gate_grad = expert_grad(gate_pieces)
    up_grad = expert_grad(up_pieces)

    def attn_grad(blocks):
        part = blocks.shape[1] // n_dp
        blocks = blocks.reshape(n_col, n_dp, part, -1)
        index = lax.axis_index("dp")
        summed = sum_dp(
            [
                lax.dynamic_index_in_dim(blocks, lax.rem(index + step, n_dp), 1, False)
                for step in range(n_dp)
            ]
        )
        total = 0.0
        for bit in range(n_row):
            block = lax.dynamic_index_in_dim(
                summed, jnp.bitwise_xor(jnp.bitwise_xor(row, col), bit), 0, False
            )
            total = total + lax.ppermute(
                block, ("row", "col"), crossed(n_row, n_col, bit)
            ).astype(f32)
        return total

    out_grad = attn_grad(
        jnp.stack(
            [
                jnp.einsum(
                    "tj,td->jd",
                    attended,
                    branch_grads[:, k * width : (k + 1) * width],
                    preferred_element_type=f32,
                ).astype(bf16)
                for k in range(n_col)
            ]
        )
    )

    attended_grads = jnp.dot(branch_grads, out_weight, preferred_element_type=f32).astype(bf16)
    query_grads, key_grads, value_grads = (
        jnp.concatenate(parts, axis=0)
        for parts in zip(
            *[
                attend_backward(
                    sequence(query_matrix, s),
                    sequence(projected_keys, s),
                    sequence(projected_values, s),
                    own_lengths[s],
                    log_totals[s],
                    sequence(attended_grads, s),
                )
                for s in range(sequences)
            ]
        )
    )
    query_grads = rotate(
        query_grads.reshape(-1, local_q, HEAD_SIZE), cosine, sine_part, -1.0
    ).reshape(-1, query_width)
    key_grads = rotate(key_grads.reshape(-1, local_kv, HEAD_SIZE), cosine, sine_part, -1.0).reshape(
        -1, kv_width
    )
    qkv_grads = jnp.concatenate([query_grads, key_grads, value_grads], axis=1).astype(bf16)
    normed_one_grads = sum_col(feature_parts(qkv_grads, qkv_weight))

    qkv_out = attn_grad(
        jnp.einsum("td,tj->dj", normed_one, qkv_grads, preferred_element_type=f32)
        .astype(bf16)
        .reshape(n_col, width, -1)
    )

    grad_scaled_one = normed_one_grads * gain_one_f
    stat_one = row_totals(jnp.sum(grad_scaled_one * scaled_one, axis=1)) / MODEL_WIDTH
    input_grad = (
        hidden_grads + inverse_one[:, None] * (grad_scaled_one - scaled_one * stat_one[:, None])
    ).astype(bf16)
    gain_one_part = jnp.sum(normed_one_grads * scaled_one, axis=0)
    gain_one_grad = sum_all(gain_one_part, ("row", "dp"))
    totals = sum_all(jnp.concatenate([gain_two_part[None], router_grad], axis=0), ("row", "dp"))
    router_out = lax.dynamic_slice_in_dim(totals[1:], lax.axis_index("dp") * half, half, 1).T
    return (
        block_out,
        input_grad,
        gain_one_grad,
        totals[0],
        qkv_out[:, :query_width],
        qkv_out[:, query_width : query_width + kv_width],
        qkv_out[:, query_width + kv_width :],
        out_grad,
        router_out,
        gate_grad,
        up_grad,
        down_out,
    )


def solution(mesh):
    placed = (
        P(("dp", "row"), "col"),
        P(("dp", "row"), "col"),
        P("col"),
        P("col"),
        P("col", "row"),
        P("col", "row"),
        P("col", "row"),
        P("row", "col"),
        P("col", None),
        P(None, "col", "row"),
        P(None, "col", "row"),
        P(None, "row", "col"),
        P("dp", None),
        P("dp", None),
    )
    return jax.shard_map(
        on_device,
        mesh=mesh,
        in_specs=placed,
        out_specs=(
            P(("dp", "row"), "col"),
            P(("dp", "row"), "col"),
            P("col"),
            P("col"),
            P(("col", "dp"), "row"),
            P(("col", "dp"), "row"),
            P(("col", "dp"), "row"),
            P(("row", "dp"), "col"),
            P(("col", "dp"), None),
            P(None, ("col", "dp"), "row"),
            P(None, ("col", "dp"), "row"),
            P(None, "row", ("col", "dp")),
        ),
        check_vma=False,
    )
```

time: 1300 us -> 1030 us (0.79)
  matrix products: 531 us -> 78.5 us
  Pallas kernels: 0 us -> 245 us
  local copies, waits for them, and re-layouts: 154 us -> 61.4 us
  waiting for transfers between devices: 255 us -> 320 us
  blocking collectives: 114 us -> 49.6 us
  starting transfers between devices: 111 us -> 144 us
    dot_general x43 -> x4, matrix products: 372 us -> 4.48 us  [on_device(): jnp.einsum('tj,td->jd', attended, branch_grads[:, k * width:(k + 1) * wid...]
    pallas_call x0 -> x7, Pallas kernels: none -> 245 us  [the longest x4 168 us: expert_block(): pl.pallas_call(lambda *refs: expert_kernel(n_col, own_experts, hidden_wid...]
    dot_general x24 -> x8, matrix products: 93.2 us -> 11.5 us  [feature_parts(): jnp.einsum('tj,dj->td', left, weight[k * width:(k + 1) * width], preferre...]
    psum x1 -> x0, blocking collectives: 60.6 us -> none  [on_device(): lax.psum(jnp.concatenate([gain_one_part[None], gain_two_part[None], route...]
    ppermute x75, starting transfers between devices: 42.9 us -> 101 us  [swap(): return lax.ppermute(block, axis, [(i, i ^ bit) for i in range(size)])]
    ppermute x13 -> x15, waiting for transfers between devices: 17.5 us -> 53 us  [the longest x5 27.9 us: sum_dp(): lax.ppermute(pieces[step], 'dp', [(i, (i + step) % size) for i in range(s...]
    convert_element_type x24 -> x0, local copies, waits for them, and re-layouts: 34.7 us -> none  [the longest x8 12 us: on_device(): up_part = jnp.transpose(both[:, own_width:].reshape(half, own_experts, hi...]
    ppermute x6 -> x3, waiting for transfers between devices: 48 us -> 82.7 us  [gather_row_line(): lax.ppermute(from_right[-1], 'row', [(i + 1, i) for i in range(0, size -...]
  transfers between devices with their start and end apart: 103 -> 99, of which waited for: 21 -> 28; matrix products, arithmetic and copies ran while one was open for 60% -> 22% of each run, Pallas kernels for 0% -> 24%
where the time goes in v2:
time: 1030 us; the launch traced here: 1020 us
  waiting for transfers between devices  320 us (31%)
  Pallas kernels  245 us (24%)
  starting transfers between devices  144 us (14%)
  other arithmetic  107 us (10%)
  matrix products  78.5 us (8%)
  local copies, waits for them, and re-layouts  61.4 us (6%)
  blocking collectives  49.6 us (5%)
  between operations  15.9 us (2%)
    ppermute x75, waiting for transfers between devices, swap(): return lax.ppermute(block, axis, [(i, i ^ bit) for i in range(size)])  173 us
    pallas_call x4, Pallas kernels, expert_block(): pl.pallas_call(lambda *refs: expert_kernel(n_col, own_experts, hidden_wid...  168 us
    ppermute x75, starting transfers between devices, swap(): return lax.ppermute(block, axis, [(i, i ^ bit) for i in range(size)])  101 us
    ppermute x3, waiting for transfers between devices, gather_row_line(): lax.ppermute(from_right[-1], 'row', [(i + 1, i) for i in range(0, size -...  82.7 us
    pallas_call x3, Pallas kernels, weight_grad(): pl.pallas_call(lambda *refs: weight_grad_kernel(n_col, n_row, n_dp, whole...  76.2 us
    psum x4, blocking collectives, row_totals(): return lax.psum(per_row, 'col')  49.6 us
    ppermute x5, waiting for transfers between devices, sum_dp(): lax.ppermute(pieces[step], 'dp', [(i, (i + step) % size) for i in range(s...  27.9 us
    ppermute x8, waiting for transfers between devices, attn_grad(): lax.ppermute(block, ('row', 'col'), crossed(n_row, n_col, bit)).astype(f32)  25.2 us
  transfers between devices with their start and end apart: 99, of which 28 were waited for; matrix products, arithmetic and copies ran while one was open for 22% of the time, Pallas kernels for 24%

profile of v2, /device:TPU:0, one launch (start us, length us, event | category | flops | bytes accessed | tf_op | source)
XLA Modules:
  0.0 1020.9 jit_solution(8048505345496244389)
XLA Ops:
  11.2 13.1 %psum.28 = f32[1024]{0:T(1024)S(1)} all-reduce(f32[1024]{0:T(1024)S(1)} %fusion.42), channel_id=1, replica_groups=mesh['dp'=2,'row'=4,'col'=4] {'col'}, use_global_device_ids=true, to_apply=%region_1.2 | all-reduce | flops 1024 | bytes 8192 | tf_op jit(solution)/shard_map/psum | solution.py:427
  25.5 15.1 %collective-permute-start.1 = (bf16[1024,384]{1,0:T(8,128)(2,1)S(1)}, bf16[1024,384]{1,0:T(8,128)(2,1)}, u32[]{:S(2)}, u32[]{:S(2)}) collective-permute-start(bf16[1024,384]{1,0:T(8,128)(2,1)S(1)} %fusion.35), channel_id=1, source_target_pairs={{0,2},{1,3},{2,0},{3,1},{4,6},{5,7},{6,4},{7,5},{8,10},{9,11},{10,... | collective-permute-start | bytes 2359304 | tf_op jit(solution)/shard_map/ppermute | solution.py:22
  41.8 21.8 %fusion.5 = pred[4096,128]{1,0:T(8,128)(4,1)S(1)} fusion(s32[4096,8]{1,0:T(8,128)S(1)} %copy.53), kind=kLoop, calls=%fused_computation.12 | loop fusion | flops 7864320 | bytes 655360 | tf_op jit(solution)/shard_map/reduce_or | solution.py:473
  69.9 11.2 %all-gather.5.cloned.1.call-done = bf16[1536,640]{1,0:T(8,128)(2,1)} async-done(((bf16[384,640]{1,0:T(8,128)(2,1)}), bf16[1536,640]{1,0:T(8,128)(2,1)}) %all-gather.5.cloned.1.call-update) | async-done | bytes 1966096 | tf_op jit(solution)/shard_map/all_gather | solution.py:472
  93.6 19.3 %collective-permute-done.9 = bf16[384,384]{0,1:T(8,128)(2,1)S(1)} collective-permute-done((bf16[384,384]{0,1:T(8,128)(2,1)S(1)}, bf16[384,384]{0,1:T(8,128)(2,1)S(1)}, u32[]{:S(2)}, u32[]{:S(2)}) %collective-permute-start.9) | collective-permute-done | bytes 294944 | tf_op jit(solution)/shard_map/ppermute | solution.py:71
  117.2 27.5 %collective-permute-done.10 = bf16[384,384]{0,1:T(8,128)(2,1)S(1)} collective-permute-done((bf16[384,384]{0,1:T(8,128)(2,1)S(1)}, bf16[384,384]{0,1:T(8,128)(2,1)S(1)}, u32[]{:S(2)}, u32[]{:S(2)}) %collective-permute-start.10) | collective-permute-done | bytes 294944 | tf_op jit(solution)/shard_map/ppermute | solution.py:71
  148.8 35.9 %collective-permute-done.11 = bf16[384,384]{0,1:T(8,128)(2,1)} collective-permute-done((bf16[384,384]{0,1:T(8,128)(2,1)S(1)}, bf16[384,384]{0,1:T(8,128)(2,1)}, u32[]{:S(2)}, u32[]{:S(2)}) %collective-permute-start.11) | collective-permute-done | bytes 294944 | tf_op jit(solution)/shard_map/ppermute | solution.py:71
  209.1 10.6 %fusion.44 = bf16[2,64,3,1024]{3,1,2,0:T(8,128)(2,1)S(1)} fusion(bf16[1024,2,64,1]{0,2,3,1:T(8,128)(2,1)S(1)} %bitcast.261, f32[2,3,1024,1024]{2,3,1,0:T(8,128)} %copy-done.2, f32[2,3,1024]{2,1,0:T(4,128)S(1)} %fusion.3, f32[2,3,1024]{2,1,0:T(4,128)S(1)} %get-tuple-element.266), kind=kOutput, calls=%fused_computation.89 | convolution fusion | flops 824573952 | bytes 26263552 | tf_op jit(solution)/shard_map/kgqs,skd->qkgd/dot_general | solution.py:392
  231.0 14.4 %collective-permute-done.16 = bf16[1024,384]{1,0:T(8,128)(2,1)S(1)} collective-permute-done((bf16[1024,384]{1,0:T(8,128)(2,1)}, bf16[1024,384]{1,0:T(8,128)(2,1)S(1)}, u32[]{:S(2)}, u32[]{:S(2)}) %collective-permute-start.16) | collective-permute-done | bytes 786464 | tf_op jit(solution)/shard_map/ppermute | solution.py:22
  245.9 21.2 %psum.29 = f32[1024]{0:T(1024)S(1)} all-reduce(f32[1024]{0:T(1024)S(1)} %get-tuple-element.215), channel_id=1, replica_groups=mesh['dp'=2,'row'=4,'col'=4] {'col'}, use_global_device_ids=true, to_apply=%region_8.9 | all-reduce | flops 1024 | bytes 8192 | tf_op jit(solution)/shard_map/psum | solution.py:427
  272.9 15.1 %collective-permute-done.27.refs_3_.refs_7_ = bf16[1024,384]{1,0:T(8,128)(2,1)S(1)} collective-permute-done((bf16[1024,384]{1,0:T(8,128)(2,1)S(1)}, bf16[1024,384]{1,0:T(8,128)(2,1)S(1)}, u32[]{:S(2)}, u32[]{:S(2)}) %collective-permute-start.27) | collective-permute-done | bytes 786464 | tf_op jit(solution)/shard_map/ppermute | solution.py:22
  289.6 16.5 %collective-permute-done.31.refs_14_ = bf16[10,384,128]{2,1,0:T(8,128)(2,1)S(1)} collective-permute-done((bf16[10,384,128]{2,1,0:T(8,128)(2,1)}, bf16[10,384,128]{2,1,0:T(8,128)(2,1)S(1)}, u32[]{:S(2)}, u32[]{:S(2)}) %collective-permute-start.31) | collective-permute-done | bytes 983072 | tf_op jit(solution)/shard_map/ppermute | solution.py:22
  312.1 18.6 %collective-permute-done.33.refs_17_ = bf16[10,384,128]{2,1,0:T(8,128)(2,1)} collective-permute-done((bf16[10,384,128]{2,1,0:T(8,128)(2,1)}, bf16[10,384,128]{2,1,0:T(8,128)(2,1)}, u32[]{:S(2)}, u32[]{:S(2)}) %collective-permute-start.33) | collective-permute-done | bytes 983072 | tf_op jit(solution)/shard_map/ppermute | solution.py:22
  330.8 11.4 %collective-permute-start.20 = (bf16[1024,384]{1,0:T(8,128)(2,1)S(1)}, bf16[1024,384]{1,0:T(8,128)(2,1)}, u32[]{:S(2)}, u32[]{:S(2)}) collective-permute-start(bf16[1024,384]{1,0:T(8,128)(2,1)S(1)} %multiply_convert_fusion.refs_1_.refs_5_), channel_id=1, source_target_pairs={{0,8},{4,12},{8,0},{12,4},{1,9},{5,13},{9,1},{13,5},{2,10},{6,14},... | collective-permute-start | bytes 2359304 | tf_op jit(solution)/shard_map/ppermute | solution.py:22
  352.4 12.3 %collective-permute-start.17 = (bf16[1024,384]{1,0:T(8,128)(2,1)S(1)}, bf16[1024,384]{1,0:T(8,128)(2,1)S(1)}, u32[]{:S(2)}, u32[]{:S(2)}) collective-permute-start(bf16[1024,384]{1,0:T(8,128)(2,1)S(1)} %multiply_convert_fusion.refs_1_.refs_5_), channel_id=1, source_target_pairs={{0,12},{4,8},{8,4},{12,0},{1,13},{5,9},{9,5},{13,1},{2,14},{6,10},... | collective-permute-start | bytes 2359304 | tf_op jit(solution)/shard_map/ppermute | solution.py:22
  374.2 20.3 %collective-permute-done.37.refs_22_ = bf16[10,128,384]{2,1,0:T(8,128)(2,1)} collective-permute-done((bf16[10,128,384]{2,1,0:T(8,128)(2,1)S(1)}, bf16[10,128,384]{2,1,0:T(8,128)(2,1)}, u32[]{:S(2)}, u32[]{:S(2)}) %collective-permute-start.37) | collective-permute-done | bytes 983072 | tf_op jit(solution)/shard_map/ppermute | solution.py:22
  394.6 41.9 %experts.4 = (bf16[1024,384]{1,0:T(8,128)(2,1)}, bf16[1024,384]{1,0:T(8,128)(2,1)}, bf16[1024,384]{1,0:T(8,128)(2,1)}, bf16[1024,384]{1,0:T(8,128)(2,1)}, bf16[1...) custom-call(s32[10]{0:T(128)} %stack.223.refs_0_, ...), custom_call_target="tpu_custom_call" | custom-call | flops 24159191040 | bytes 41943040 | tf_op jit(solution)/shard_map/experts/pallas_call | solution.py:213
  440.0 42.3 %experts.5 = (bf16[1024,384]{1,0:T(8,128)(2,1)}, bf16[1024,384]{1,0:T(8,128)(2,1)}, bf16[1024,384]{1,0:T(8,128)(2,1)}, bf16[1024,384]{1,0:T(8,128)(2,1)}, bf16[1...) custom-call(s32[10]{0:T(128)} %stack.217.refs_0_, ...), custom_call_target="tpu_custom_call", output_to_operand_aliasing={{4}: (23, {})} | custom-call | flops 24159191040 | bytes 41943040 | tf_op jit(solution)/shard_map/experts/pallas_call | solution.py:213
  489.6 42.1 %experts.6 = (bf16[1024,384]{1,0:T(8,128)(2,1)}, bf16[1024,384]{1,0:T(8,128)(2,1)}, bf16[1024,384]{1,0:T(8,128)(2,1)}, bf16[1024,384]{1,0:T(8,128)(2,1)}, bf16[1...) custom-call(s32[10]{0:T(128)} %stack.103.refs_0_, ...), custom_call_target="tpu_custom_call", output_to_operand_aliasing={{4}: (23, {})} | custom-call | flops 24159191040 | bytes 41943040 | tf_op jit(solution)/shard_map/experts/pallas_call | solution.py:213
  540.0 11.2 %collective-permute-start.57 = (f32[16,1024]{1,0:T(8,128)S(1)}, f32[16,1024]{1,0:T(8,128)S(1)}, u32[]{:S(2)}, u32[]{:S(2)}) collective-permute-start(f32[16,1024]{1,0:T(8,128)S(1)} %copy-done.107), channel_id=1, source_target_pairs={{0,8},{4,12},{8,0},{12,4},{1,9},{5,13},{9,1},{13,5},{2,10},{6,14},... | collective-permute-start | bytes 196616 | tf_op jit(solution)/shard_map/ppermute | solution.py:22
  553.1 42.1 %experts.7 = (bf16[1024,384]{1,0:T(8,128)(2,1)}, bf16[1024,384]{1,0:T(8,128)(2,1)}, bf16[1024,384]{1,0:T(8,128)(2,1)}, bf16[1024,384]{1,0:T(8,128)(2,1)}, bf16[1...) custom-call(s32[10]{0:T(128)} %stack.97.refs_0_, ...), custom_call_target="tpu_custom_call", output_to_operand_aliasing={{4}: (23, {})} | custom-call | flops 24159191040 | bytes 41943040 | tf_op jit(solution)/shard_map/experts/pallas_call | solution.py:213
  602.5 24.8 %weight_grads.3 = bf16[2,4,10,192,128]{4,3,2,1,0:T(8,128)(2,1)} custom-call(s32[17]{0:T(128)} %stack.225.refs_0_, bf16[1024,1280]{1,0:T(8,128)(2,1)} %get-tuple-element.189.refs_1_, bf16[1024,1280]{1,0:T(8,128)(2,1)} %get-tuple-element.190.refs_2_, bf16[1024,1280]{1,0:T(8,128)(2,1)} %get-tuple-element.191.refs_3_, ...), custom_call_target="tpu_custom_call" | custom-call | flops 16106127360 | bytes 20971520 | tf_op jit(solution)/shard_map/weight_grads/pallas_call | solution.py:308
  637.6 25.3 %weight_grads.4 = bf16[2,4,10,192,128]{4,3,2,1,0:T(8,128)(2,1)} custom-call(s32[17]{0:T(128)} %stack.225.refs_0_, bf16[1024,1280]{1,0:T(8,128)(2,1)} %get-tuple-element.193.refs_1_, bf16[1024,1280]{1,0:T(8,128)(2,1)} %get-tuple-element.194.refs_2_, bf16[1024,1280]{1,0:T(8,128)(2,1)} %get-tuple-element.195.refs_3_, ...), custom_call_target="tpu_custom_call" | custom-call | flops 16106127360 | bytes 20971520 | tf_op jit(solution)/shard_map/weight_grads/pallas_call | solution.py:308
  673.4 26.1 %weight_grads.5 = bf16[2,4,10,192,128]{4,3,2,1,0:T(8,128)(2,1)} custom-call(s32[17]{0:T(128)} %stack.225.refs_0_, bf16[1024,1280]{1,0:T(8,128)(2,1)} %get-tuple-element.197.refs_1_, bf16[1024,1280]{1,0:T(8,128)(2,1)} %get-tuple-element.198.refs_2_, bf16[1024,1280]{1,0:T(8,128)(2,1)} %get-tuple-element.199.refs_3_, ...), custom_call_target="tpu_custom_call" | custom-call | flops 16106127360 | bytes 20971520 | tf_op jit(solution)/shard_map/weight_grads/pallas_call | solution.py:308
  771.6 20.0 %collective-permute-done.63 = bf16[1024,384]{1,0:T(8,128)(2,1)S(1)} collective-permute-done((bf16[1024,384]{1,0:T(8,128)(2,1)S(1)}, bf16[1024,384]{1,0:T(8,128)(2,1)S(1)}, u32[]{:S(2)}, u32[]{:S(2)}) %collective-permute-start.63) | collective-permute-done | bytes 786464 | tf_op jit(solution)/shard_map/ppermute | solution.py:22
  804.4 16.8 %collective-permute-done.87 = bf16[10,192,128]{2,1,0:T(8,128)(2,1)S(1)} collective-permute-done((bf16[10,192,128]{2,1,0:T(8,128)(2,1)S(1)}, bf16[10,192,128]{2,1,0:T(8,128)(2,1)S(1)}, u32[]{:S(2)}, u32[]{:S(2)}) %collective-permute-start.87) | collective-permute-done | bytes 491552 | tf_op jit(solution)/shard_map/ppermute | solution.py:22
  833.5 16.0 %fusion = (f32[2,3,1024]{2,1,0:T(4,128)S(1)}, f32[2,1024,1024,3]{2,1,3,0:T(8,128)}) fusion(f32[2,3,1024,1024]{2,3,1,0:T(8,128)} %copy-done.2, f32[2,3,1024]{2,1,0:T(4,128)S(1)} %copy-done.53, bf16[1024,2,64,1]{0,2,3,1:T(8,128)(2,1)S(1)} %bitcast.262, bf16[1024,2,3,64]{0,3,2,1:T(8,128)(2,1)S(1)} %bitcast.247), kind=kOutput, calls=%fused_computation.2 | convolution fusion | flops 824174592 | bytes 51429376 | tf_op jit(solution)/shard_map/qkgd,skd->kgqs/dot_general | solution.py:406
  849.5 16.8 %fusion.2 = bf16[2,3,1024,1024]{2,3,1,0:T(8,128)(2,1)S(1)} fusion(f32[2,1024,1024,3]{2,1,3,0:T(8,128)} %get-tuple-element.269, f32[2,3,1024,1024]{2,3,1,0:T(8,128)} %copy-done.2, f32[2,3,1024]{2,1,0:T(4,128)S(1)} %get-tuple-element.268, f32[2,3,1024]{2,1,0:T(4,128)S(1)} %copy-done.53), kind=kLoop, calls=%fused_computation.4 | loop fusion | flops 25165824 | bytes 62963712 | tf_op jit(solution)/shard_map/convert_element_type | solution.py:409
  916.1 18.1 %collective-permute-done.74 = bf16[4,192,640]{2,1,0:T(8,128)(2,1)S(1)} collective-permute-done((bf16[4,192,640]{2,1,0:T(8,128)(2,1)S(1)}, bf16[4,192,640]{2,1,0:T(8,128)(2,1)S(1)}, u32[]{:S(2)}, u32[]{:S(2)}) %collective-permute-start.74) | collective-permute-done | bytes 983072 | tf_op jit(solution)/shard_map/ppermute | solution.py:332
  945.2 11.1 %collective-permute-start.76 = (bf16[192,640]{1,0:T(8,128)(2,1)S(1)}, bf16[192,640]{1,0:T(8,128)(2,1)S(1)}, u32[]{:S(2)}, u32[]{:S(2)}) collective-permute-start(bf16[192,640]{1,0:T(8,128)(2,1)S(1)} %get-tuple-element.252), channel_id=1, source_target_pairs={{0,1},{1,5},{2,9},{3,13},{4,0},{5,4},{6,8},{7,12},{8,3},{9,7},{10,... | collective-permute-start | bytes 737288 | tf_op jit(solution)/shard_map/ppermute | solution.py:700
  956.3 12.4 %collective-permute-done.78 = bf16[192,640]{1,0:T(8,128)(2,1)S(1)} collective-permute-done((bf16[192,640]{1,0:T(8,128)(2,1)S(1)}, bf16[192,640]{1,0:T(8,128)(2,1)S(1)}, u32[]{:S(2)}, u32[]{:S(2)}) %collective-permute-start.78) | collective-permute-done | bytes 245792 | tf_op jit(solution)/shard_map/ppermute | solution.py:700
  970.2 12.7 %collective-permute-done.77 = bf16[192,640]{1,0:T(8,128)(2,1)S(1)} collective-permute-done((bf16[192,640]{1,0:T(8,128)(2,1)S(1)}, bf16[192,640]{1,0:T(8,128)(2,1)S(1)}, u32[]{:S(2)}, u32[]{:S(2)}) %collective-permute-start.77) | collective-permute-done | bytes 245792 | tf_op jit(solution)/shard_map/ppermute | solution.py:700
  (538 shorter events, 340.7 us)
Async XLA Ops:
  7.2 73.8 %all-gather.5.cloned.1.call-start = ((), (), s32[]{:S(2)}) async-start(), calls=%async_computation.2 | async-start | bytes 2457600 | tf_op jit(solution)/shard_map/all_gather | solution.py:472
  25.2 369.4 %all-gather.7.cloned.1.call-start = ((), (), s32[]{:S(2)}) async-start(), calls=%async_computation.3 | async-start | bytes 13369344 | tf_op jit(solution)/shard_map/all_gather | solution.py:500
  81.1 928.7 %reduce-scatter.2.cloned.1.call-start = ((), (), s32[]{:S(2)}) async-start(), calls=%async_computation.1 | async-start | bytes 13369344 | tf_op jit(solution)/shard_map/reduce_scatter | solution.py:635
  308.7 56.0 %collective-permute-start.35 = (bf16[10,128,384]{2,1,0:T(8,128)(2,1)}, bf16[10,128,384]{2,1,0:T(8,128)(2,1)}, u32[]{:S(2)}, u32[]{:S(2)}) collective-permute-start(bf16[10,128,384]{2,1,0:T(8,128)(2,1)} %get-tuple-element.219), channel_id=1, source_target_pairs={{0,1},{1,0},{2,3},{3,2},{4,5},{5,4},{6,7},{7,6},{8,9},{9,8},{10,11... | collective-permute-start | bytes 2949128 | tf_op jit(solution)/shard_map/ppermute | solution.py:22
  308.8 64.1 %collective-permute-start.36 = (bf16[10,128,384]{2,1,0:T(8,128)(2,1)}, bf16[10,128,384]{2,1,0:T(8,128)(2,1)}, u32[]{:S(2)}, u32[]{:S(2)}) collective-permute-start(bf16[10,128,384]{2,1,0:T(8,128)(2,1)} %get-tuple-element.218), channel_id=1, source_target_pairs={{0,2},{1,3},{2,0},{3,1},{4,6},{5,7},{6,4},{7,5},{8,10},{9,11},{10,... | collective-permute-start | bytes 2949128 | tf_op jit(solution)/shard_map/ppermute | solution.py:22
  310.3 84.3 %collective-permute-start.37 = (bf16[10,128,384]{2,1,0:T(8,128)(2,1)S(1)}, bf16[10,128,384]{2,1,0:T(8,128)(2,1)}, u32[]{:S(2)}, u32[]{:S(2)}) collective-permute-start(bf16[10,128,384]{2,1,0:T(8,128)(2,1)S(1)} %get-tuple-element.217), channel_id=1, source_target_pairs={{0,3},{1,2},{2,1},{3,0},{4,7},{5,6},{6,5},{7,4},{8,11},{9,10},{10,... | collective-permute-start | bytes 2949128 | tf_op jit(solution)/shard_map/ppermute | solution.py:22
  330.8 106.5 %collective-permute-start.20 = (bf16[1024,384]{1,0:T(8,128)(2,1)S(1)}, bf16[1024,384]{1,0:T(8,128)(2,1)}, u32[]{:S(2)}, u32[]{:S(2)}) collective-permute-start(bf16[1024,384]{1,0:T(8,128)(2,1)S(1)} %multiply_convert_fusion.refs_1_.refs_5_), channel_id=1, source_target_pairs={{0,8},{4,12},{8,0},{12,4},{1,9},{5,13},{9,1},{13,5},{2,10},{6,14},... | collective-permute-start | bytes 2359304 | tf_op jit(solution)/shard_map/ppermute | solution.py:22
  352.4 85.3 %collective-permute-start.17 = (bf16[1024,384]{1,0:T(8,128)(2,1)S(1)}, bf16[1024,384]{1,0:T(8,128)(2,1)S(1)}, u32[]{:S(2)}, u32[]{:S(2)}) collective-permute-start(bf16[1024,384]{1,0:T(8,128)(2,1)S(1)} %multiply_convert_fusion.refs_1_.refs_5_), channel_id=1, source_target_pairs={{0,12},{4,8},{8,4},{12,0},{1,13},{5,9},{9,5},{13,1},{2,14},{6,10},... | collective-permute-start | bytes 2359304 | tf_op jit(solution)/shard_map/ppermute | solution.py:22
  364.8 73.0 %collective-permute-start.24 = (bf16[1024,384]{1,0:T(8,128)(2,1)}, bf16[1024,384]{1,0:T(8,128)(2,1)}, u32[]{:S(2)}, u32[]{:S(2)}) collective-permute-start(bf16[1024,384]{1,0:T(8,128)(2,1)} %copy-done.98), channel_id=1, source_target_pairs={{0,1},{1,0},{2,3},{3,2},{4,5},{5,4},{6,7},{7,6},{8,9},{9,8},{10,11... | collective-permute-start | bytes 2359304 | tf_op jit(solution)/shard_map/ppermute | solution.py:22
  372.9 63.6 %collective-permute-start.25 = (bf16[1024,384]{1,0:T(8,128)(2,1)}, bf16[1024,384]{1,0:T(8,128)(2,1)}, u32[]{:S(2)}, u32[]{:S(2)}) collective-permute-start(bf16[1024,384]{1,0:T(8,128)(2,1)} %copy-done.98), channel_id=1, source_target_pairs={{0,2},{1,3},{2,0},{3,1},{4,6},{5,7},{6,4},{7,5},{8,10},{9,11},{10,... | collective-permute-start | bytes 2359304 | tf_op jit(solution)/shard_map/ppermute | solution.py:22
  437.2 45.7 %collective-permute-start.22 = (bf16[1024,384]{1,0:T(8,128)(2,1)}, bf16[1024,384]{1,0:T(8,128)(2,1)}, u32[]{:S(2)}, u32[]{:S(2)}) collective-permute-start(bf16[1024,384]{1,0:T(8,128)(2,1)} %collective-permute-done.20.refs_1_.refs_13_), channel_id=1, source_target_pairs={{0,2},{1,3},{2,0},{3,1},{4,6},{5,7},{6,4},{7,5},{8,10},{9,11},{10,... | collective-permute-start | bytes 2359304 | tf_op jit(solution)/shard_map/ppermute | solution.py:22
  437.7 47.9 %collective-permute-start.41 = (bf16[1024,384]{1,0:T(8,128)(2,1)}, bf16[1024,384]{1,0:T(8,128)(2,1)S(1)}, u32[]{:S(2)}, u32[]{:S(2)}) collective-permute-start(bf16[1024,384]{1,0:T(8,128)(2,1)} %get-tuple-element.140), channel_id=1, source_target_pairs={{0,1},{1,0},{2,3},{3,2},{4,5},{5,4},{6,7},{7,6},{8,9},{9,8},{10,11... | collective-permute-start | bytes 2359304 | tf_op jit(solution)/shard_map/ppermute | solution.py:22
  485.0 46.6 %collective-permute-start.19 = (bf16[1024,384]{1,0:T(8,128)(2,1)}, bf16[1024,384]{1,0:T(8,128)(2,1)}, u32[]{:S(2)}, u32[]{:S(2)}) collective-permute-start(bf16[1024,384]{1,0:T(8,128)(2,1)} %copy-done.100), channel_id=1, source_target_pairs={{0,2},{1,3},{2,0},{3,1},{4,6},{5,7},{6,4},{7,5},{8,10},{9,11},{10,... | collective-permute-start | bytes 2359304 | tf_op jit(solution)/shard_map/ppermute | solution.py:22
  485.6 46.1 %collective-permute-start.40 = (bf16[1024,384]{1,0:T(8,128)(2,1)}, bf16[1024,384]{1,0:T(8,128)(2,1)}, u32[]{:S(2)}, u32[]{:S(2)}) collective-permute-start(bf16[1024,384]{1,0:T(8,128)(2,1)} %get-tuple-element.138), channel_id=1, source_target_pairs={{0,1},{1,0},{2,3},{3,2},{4,5},{5,4},{6,7},{7,6},{8,9},{9,8},{10,11... | collective-permute-start | bytes 2359304 | tf_op jit(solution)/shard_map/ppermute | solution.py:22
  486.7 48.9 %collective-permute-start.44 = (bf16[1024,384]{1,0:T(8,128)(2,1)}, bf16[1024,384]{1,0:T(8,128)(2,1)S(1)}, u32[]{:S(2)}, u32[]{:S(2)}) collective-permute-start(bf16[1024,384]{1,0:T(8,128)(2,1)} %get-tuple-element.148), channel_id=1, source_target_pairs={{0,1},{1,0},{2,3},{3,2},{4,5},{5,4},{6,7},{7,6},{8,9},{9,8},{10,11... | collective-permute-start | bytes 2359304 | tf_op jit(solution)/shard_map/ppermute | solution.py:22
  487.5 45.4 %collective-permute-start.43 = (bf16[1024,384]{1,0:T(8,128)(2,1)}, bf16[1024,384]{1,0:T(8,128)(2,1)S(1)}, u32[]{:S(2)}, u32[]{:S(2)}) collective-permute-start(bf16[1024,384]{1,0:T(8,128)(2,1)} %fusion.78), channel_id=1, source_target_pairs={{0,2},{1,3},{2,0},{3,1},{4,6},{5,7},{6,4},{7,5},{8,10},{9,11},{10,... | collective-permute-start | bytes 2359304 | tf_op jit(solution)/shard_map/ppermute | solution.py:22
  489.0 49.8 %collective-permute-start.53 = (bf16[1024,384]{1,0:T(8,128)(2,1)S(1)}, bf16[1024,384]{1,0:T(8,128)(2,1)S(1)}, u32[]{:S(2)}, u32[]{:S(2)}) collective-permute-start(bf16[1024,384]{1,0:T(8,128)(2,1)S(1)} %fusion.79), channel_id=1, source_target_pairs={{0,2},{1,3},{2,0},{3,1},{4,6},{5,7},{6,4},{7,5},{8,10},{9,11},{10,... | collective-permute-start | bytes 2359304 | tf_op jit(solution)/shard_map/ppermute | solution.py:22
  532.9 65.3 %collective-permute-start.56 = (f32[16,1024]{1,0:T(8,128)}, f32[16,1024]{1,0:T(8,128)}, u32[]{:S(2)}, u32[]{:S(2)}) collective-permute-start(f32[16,1024]{1,0:T(8,128)} %get-tuple-element.174), channel_id=1, source_target_pairs={{0,4},{4,0},{8,12},{12,8},{1,5},{5,1},{9,13},{13,9},{2,6},{6,2},{1... | collective-permute-start | bytes 196616 | tf_op jit(solution)/shard_map/ppermute | solution.py:22
  535.6 59.6 %collective-permute-start.47 = (bf16[1024,384]{1,0:T(8,128)(2,1)}, bf16[1024,384]{1,0:T(8,128)(2,1)}, u32[]{:S(2)}, u32[]{:S(2)}) collective-permute-start(bf16[1024,384]{1,0:T(8,128)(2,1)} %get-tuple-element.160), channel_id=1, source_target_pairs={{0,1},{1,0},{2,3},{3,2},{4,5},{5,4},{6,7},{7,6},{8,9},{9,8},{10,11... | collective-permute-start | bytes 2359304 | tf_op jit(solution)/shard_map/ppermute | solution.py:22
  538.8 90.4 %collective-permute-start.46 = (bf16[1024,384]{1,0:T(8,128)(2,1)}, bf16[1024,384]{1,0:T(8,128)(2,1)S(1)}, u32[]{:S(2)}, u32[]{:S(2)}) collective-permute-start(bf16[1024,384]{1,0:T(8,128)(2,1)} %get-tuple-element.158), channel_id=1, source_target_pairs={{0,1},{1,0},{2,3},{3,2},{4,5},{5,4},{6,7},{7,6},{8,9},{9,8},{10,11... | collective-permute-start | bytes 2359304 | tf_op jit(solution)/shard_map/ppermute | solution.py:22
  540.0 59.5 %collective-permute-start.57 = (f32[16,1024]{1,0:T(8,128)S(1)}, f32[16,1024]{1,0:T(8,128)S(1)}, u32[]{:S(2)}, u32[]{:S(2)}) collective-permute-start(f32[16,1024]{1,0:T(8,128)S(1)} %copy-done.107), channel_id=1, source_target_pairs={{0,8},{4,12},{8,0},{12,4},{1,9},{5,13},{9,1},{13,5},{2,10},{6,14},... | collective-permute-start | bytes 196616 | tf_op jit(solution)/shard_map/ppermute | solution.py:22
  551.2 85.7 %collective-permute-start.54 = (bf16[1024,384]{1,0:T(8,128)(2,1)}, bf16[1024,384]{1,0:T(8,128)(2,1)S(1)}, u32[]{:S(2)}, u32[]{:S(2)}) collective-permute-start(bf16[1024,384]{1,0:T(8,128)(2,1)} %convert_add_fusion.7), channel_id=1, source_target_pairs={{0,4},{4,0},{8,12},{12,8},{1,5},{5,1},{9,13},{13,9},{2,6},{6,2},{1... | collective-permute-start | bytes 2359304 | tf_op jit(solution)/shard_map/ppermute | solution.py:22
  601.6 64.3 %collective-permute-start.50 = (bf16[1024,384]{1,0:T(8,128)(2,1)}, bf16[1024,384]{1,0:T(8,128)(2,1)}, u32[]{:S(2)}, u32[]{:S(2)}) collective-permute-start(bf16[1024,384]{1,0:T(8,128)(2,1)} %get-tuple-element.169), channel_id=1, source_target_pairs={{0,1},{1,0},{2,3},{3,2},{4,5},{5,4},{6,7},{7,6},{8,9},{9,8},{10,11... | collective-permute-start | bytes 2359304 | tf_op jit(solution)/shard_map/ppermute | solution.py:22
  630.6 72.8 %collective-permute-start.92 = (bf16[4,10,192,128]{3,2,1,0:T(8,128)(2,1)S(1)}, bf16[4,10,192,128]{3,2,1,0:T(8,128)(2,1)}, u32[]{:S(2)}, u32[]{:S(2)}) collective-permute-start(bf16[4,10,192,128]{3,2,1,0:T(8,128)(2,1)S(1)} %slice_bitcast_fusion), channel_id=1, source_target_pairs={{0,16},{16,0},{1,17},{17,1},{2,18},{18,2},{3,19},{19,3},{4,20},{20... | collective-permute-start | bytes 5898248 | tf_op jit(solution)/shard_map/ppermute | solution.py:332
  666.0 100.4 %collective-permute-start.84 = (bf16[4,10,192,128]{3,2,1,0:T(8,128)(2,1)}, bf16[4,10,192,128]{3,2,1,0:T(8,128)(2,1)}, u32[]{:S(2)}, u32[]{:S(2)}) collective-permute-start(bf16[4,10,192,128]{3,2,1,0:T(8,128)(2,1)} %slice_bitcast_fusion.4), channel_id=1, source_target_pairs={{0,16},{16,0},{1,17},{17,1},{2,18},{18,2},{3,19},{19,3},{4,20},{20... | collective-permute-start | bytes 5898248 | tf_op jit(solution)/shard_map/ppermute | solution.py:332
  702.6 120.6 %collective-permute-start.88 = (bf16[4,10,192,128]{3,2,1,0:T(8,128)(2,1)}, bf16[4,10,192,128]{3,2,1,0:T(8,128)(2,1)}, u32[]{:S(2)}, u32[]{:S(2)}) collective-permute-start(bf16[4,10,192,128]{3,2,1,0:T(8,128)(2,1)} %slice_bitcast_fusion.2), channel_id=1, source_target_pairs={{0,16},{16,0},{1,17},{17,1},{2,18},{18,2},{3,19},{19,3},{4,20},{20... | collective-permute-start | bytes 5898248 | tf_op jit(solution)/shard_map/ppermute | solution.py:332
  745.6 46.0 %collective-permute-start.63 = (bf16[1024,384]{1,0:T(8,128)(2,1)S(1)}, bf16[1024,384]{1,0:T(8,128)(2,1)S(1)}, u32[]{:S(2)}, u32[]{:S(2)}) collective-permute-start(bf16[1024,384]{1,0:T(8,128)(2,1)S(1)} %fusion.82), channel_id=1, source_target_pairs={{0,2},{1,3},{2,0},{3,1},{4,6},{5,7},{6,4},{7,5},{8,10},{9,11},{10,... | collective-permute-start | bytes 2359304 | tf_op jit(solution)/shard_map/ppermute | solution.py:22
  826.6 72.0 %collective-permute-start.89 = (bf16[10,192,128]{2,1,0:T(8,128)(2,1)}, bf16[10,192,128]{2,1,0:T(8,128)(2,1)}, u32[]{:S(2)}, u32[]{:S(2)}) collective-permute-start(bf16[10,192,128]{2,1,0:T(8,128)(2,1)} %get-tuple-element.231), channel_id=1, source_target_pairs={{0,1},{1,0},{2,3},{3,2},{4,5},{5,4},{6,7},{7,6},{8,9},{9,8},{10,11... | collective-permute-start | bytes 1474568 | tf_op jit(solution)/shard_map/ppermute | solution.py:22
  826.8 74.9 %collective-permute-start.90 = (bf16[10,192,128]{2,1,0:T(8,128)(2,1)}, bf16[10,192,128]{2,1,0:T(8,128)(2,1)}, u32[]{:S(2)}, u32[]{:S(2)}) collective-permute-start(bf16[10,192,128]{2,1,0:T(8,128)(2,1)} %get-tuple-element.230), channel_id=1, source_target_pairs={{0,2},{1,3},{2,0},{3,1},{4,6},{5,7},{6,4},{7,5},{8,10},{9,11},{10,... | collective-permute-start | bytes 1474568 | tf_op jit(solution)/shard_map/ppermute | solution.py:22
  828.2 107.8 %collective-permute-start.91 = (bf16[10,192,128]{2,1,0:T(8,128)(2,1)}, bf16[10,192,128]{2,1,0:T(8,128)(2,1)}, u32[]{:S(2)}, u32[]{:S(2)}) collective-permute-start(bf16[10,192,128]{2,1,0:T(8,128)(2,1)} %get-tuple-element.229), channel_id=1, source_target_pairs={{0,3},{1,2},{2,1},{3,0},{4,7},{5,6},{6,5},{7,4},{8,11},{9,10},{10,... | collective-permute-start | bytes 1474568 | tf_op jit(solution)/shard_map/ppermute | solution.py:22
  901.7 81.3 %collective-permute-start.65 = (bf16[1024,384]{1,0:T(8,128)(2,1)S(1)}, bf16[1024,384]{1,0:T(8,128)(2,1)S(1)}, u32[]{:S(2)}, u32[]{:S(2)}) collective-permute-start(bf16[1024,384]{1,0:T(8,128)(2,1)S(1)} %convolution_convert_fusion.2), channel_id=1, source_target_pairs={{0,1},{1,0},{2,3},{3,2},{4,5},{5,4},{6,7},{7,6},{8,9},{9,8},{10,11... | collective-permute-start | bytes 2359304 | tf_op jit(solution)/shard_map/ppermute | solution.py:22
  934.2 48.9 %collective-permute-start.67 = (bf16[1024,384]{1,0:T(8,128)(2,1)S(1)}, bf16[1024,384]{1,0:T(8,128)(2,1)S(1)}, u32[]{:S(2)}, u32[]{:S(2)}) collective-permute-start(bf16[1024,384]{1,0:T(8,128)(2,1)S(1)} %add_convert_fusion), channel_id=1, source_target_pairs={{0,2},{1,3},{2,0},{3,1},{4,6},{5,7},{6,4},{7,5},{8,10},{9,11},{10,... | collective-permute-start | bytes 2359304 | tf_op jit(solution)/shard_map/ppermute | solution.py:22
  (175 other events, 3054.1 us)
Sparse Core Ops, SparseCore 0:
  25.3 55.7 all-gather.4
  83.3 115.8 all-gather.6
  672.6 160.0 reduce-scatter.1

commit v3 on v2

--- a/solution.py
+++ b/solution.py
@@ -86,7 +86,7 @@
         return [refs.pop(0) for _ in range(count)]
 
     x, cot = take(n_col), take(n_col)
-    mask, router = take(2)
+    routes, router = take(2)
     gate, up, down = take(n_col), take(n_col), take(n_col)
     if not first:
         take(1)
@@ -105,7 +105,12 @@
         for start in range(0, rows, CHUNK):
             span = slice(start, start + CHUNK)
             here = jnp.concatenate([part[span, :] for part in x], axis=1)
-            logits = jnp.dot(here, router[...], preferred_element_type=f32) + mask[span, :]
+            logits = jnp.dot(here, router[...], preferred_element_type=f32)
+            named = routes[span, :]
+            routed = lane == named[:, :1]
+            for i in range(1, named.shape[1]):
+                routed = jnp.logical_or(routed, lane == named[:, i : i + 1])
+            logits = jnp.where(routed, logits, -1e30)
             raised = jnp.exp(logits - jnp.max(logits, axis=1, keepdims=True))
             gates_out[span, :] = raised / jnp.sum(raised, axis=1, keepdims=True)
 
@@ -169,7 +174,7 @@
         terms_out[...] = terms_acc[...].T[: terms_out.shape[0], :]
 
 
-def expert_block(source, x, cot_all, mask, router, gate, up, down, mix):
+def expert_block(source, x, cot_all, routes, router, gate, up, down, mix):
     n_col = len(x)
     rows, width = x[0].shape
     own_experts, hidden_width = gate[1].shape[0], gate[1].shape[2]
@@ -196,14 +201,14 @@
         [whole] * n_col
         + [cot_spec(k) for k in range(n_col)]
         + [
-            pl.BlockSpec((rows, LANES), lambda p, s: (s[0], 0), pipeline_mode=once),
+            pl.BlockSpec((rows, routes.shape[1]), lambda p, s: (s[0], 0), pipeline_mode=once),
             pl.BlockSpec(router.shape, lambda p, s: (0, 0), pipeline_mode=once),
         ]
         + weight_specs(gate)
         + weight_specs(up)
         + weight_specs(down)
     )
-    operands = [*x, *([cot_all] * n_col), mask, router, *gate, *up, *down]
+    operands = [*x, *([cot_all] * n_col), routes, router, *gate, *up, *down]
     aliases = {}
     if mix is not None:
         in_specs.append(pl.BlockSpec(memory_space=pl.ANY))
@@ -325,13 +330,16 @@
     )(scalars, *lefts, *rights)
 
 
-def sum_dp(pieces):
+def send_dp(pieces):
     size = lax.axis_size("dp")
-    total = pieces[0].astype(f32)
-    for step in range(1, size):
-        arrived = lax.ppermute(pieces[step], "dp", [(i, (i + step) % size) for i in range(size)])
-        total = total + arrived.astype(f32)
-    return total.astype(bf16)
+    return [pieces[0]] + [
+        lax.ppermute(pieces[step], "dp", [(i, (i + step) % size) for i in range(size)])
+        for step in range(1, size)
+    ]
+
+
+def add_up(terms):
+    return sum(term.astype(f32) for term in terms).astype(bf16)
 
 
 def sum_all(values, axes):
@@ -396,7 +404,7 @@
 
 
 def attend_backward(
-    query_matrix, projected_keys, projected_values, sequence_lengths, log_totals, out_grad
+    query_matrix, projected_keys, projected_values, sequence_lengths, log_totals, out_grad, others
 ):
     scores, grouped_queries, key_heads = score_block(query_matrix, projected_keys, sequence_lengths)
     softmax_probs = jnp.exp(scores - log_totals[..., None])
@@ -407,6 +415,7 @@
     score_grads = (
         softmax_probs * (prob_grads - jnp.sum(softmax_probs * prob_grads, axis=-1, keepdims=True))
     ).astype(bf16)
+    score_grads = after(score_grads, others)
     query_grads = jnp.einsum(
         "kgqs,skd->qkgd", score_grads, key_heads, preferred_element_type=f32
     ) * HEAD_SIZE ** (-0.5)
@@ -469,9 +478,8 @@
         ("row", "col"),
         crossing,
     )
+    out_crossed = lax.ppermute(w_out.T, ("row", "col"), crossing)
     qkv_blocks = lax.all_gather(qkv_crossed, "row", axis=0)
-    routed = jnp.any(routes[:, :, None] == jnp.arange(LANES)[None, None, :], axis=1)
-    mask = jnp.where(routed, 0.0, -1e30).astype(f32)
 
     gain_one_f = gain_one.astype(f32)
     gain_two_f = gain_two.astype(f32)
@@ -480,27 +488,41 @@
         row_totals(jnp.sum(inputs_f * inputs_f, axis=1)) / MODEL_WIDTH + epsilon
     )
     scaled_one = inputs_f * inverse_one[:, None]
-    normed_one = jnp.concatenate(gather_col((scaled_one * gain_one_f).astype(bf16)), axis=1)
+    normed_local = (scaled_one * gain_one_f).astype(bf16)
+    normed_one = jnp.concatenate(gather_col(normed_local), axis=1)
     router_parts = gather_col(w_router.T)
     router_weight = jnp.concatenate(router_parts, axis=1).T
     router_weight = jnp.pad(router_weight, ((0, 0), (0, LANES - expert_count)))
-    normed_one, mask, router_weight = lax.optimization_barrier((normed_one, mask, router_weight))
-
-    def trade(weight):
-        received = []
-        for k in reversed(range(1, n_col)):
-            block = lax.dynamic_slice_in_dim(weight, relative[k] * own_experts, own_experts, 0)
-            received.insert(0, swap(block, "col", k))
-        return received
-
-    traded = [trade(weight) for weight in after((w_gate, w_up, w_down), normed_one)]
-    out_crossed = lax.ppermute(after(w_out.T, normed_one), ("row", "col"), crossing)
-    out_blocks = gather_row_line(out_crossed)
+    normed_one, router_weight = lax.optimization_barrier((normed_one, router_weight))
+
+    dp_index = lax.axis_index("dp")
+
+    def send(weight, k):
+        block = lax.dynamic_slice_in_dim(weight, relative[k] * own_experts, own_experts, 0)
+        if k > 1:
+            part = weight.shape[1] // n_dp
+            block = lax.dynamic_slice_in_dim(block, dp_index * part, part, 1)
+        return swap(block, "col", k)
+
+    def complete(part):
+        if n_dp != 2:
+            return lax.all_gather(part, "dp", axis=1, tiled=True)
+        other = swap(part, "dp", 1)
+        return jnp.where(
+            dp_index == 0,
+            jnp.concatenate([part, other], axis=1),
+            jnp.concatenate([other, part], axis=1),
+        )
+
+    held_weights = after((w_gate, w_up, w_down), normed_local)
+    sent = [[send(weight, k) for k in range(2, n_col)] for weight in held_weights]
+    normed_one, sent = lax.optimization_barrier((normed_one, sent))
+    near = [send(weight, 1) for weight in after((w_gate, w_up, w_down), normed_one)]
     qkv_blocks = after(qkv_blocks, normed_one)
-    cot_all = lax.all_gather(after(cotangent, qkv_blocks), ("row", "col"), axis=0)
     qkv_weight = all_features(qkv_blocks)
-
+    out_blocks = lax.all_gather(after(out_crossed, qkv_blocks), "row", axis=0)
     qkv = jnp.dot(normed_one, qkv_weight, preferred_element_type=f32)
+    cot_all = lax.all_gather(after(cotangent, qkv), ("row", "col"), axis=0)
     positions = jnp.arange(local_rows) % SEQUENCE_LENGTH
     cosine, sine_part = rotation_tables(positions)
     query_matrix = (
@@ -545,24 +567,21 @@
             for k in range(n_col)
         ]
 
-    out_blocks = jnp.stack(after(out_blocks, attended))
-    out_weight = jnp.concatenate(
-        [
-            lax.dynamic_index_in_dim(out_blocks, lax.rem(row - relative[k] + n_row, n_row), 0, False)
-            for k in range(n_col)
-        ],
-        axis=0,
-    )
+    far = [[complete(part) for part in parts] for parts in sent]
+    attended = after(attended, far[0])
+    out_weight = all_features(after(out_blocks, attended))
     hidden = inputs_f + sum_col(feature_parts(attended, out_weight))
+    hidden = after(hidden, far[1])
     inverse_two = lax.rsqrt(row_totals(jnp.sum(hidden * hidden, axis=1)) / MODEL_WIDTH + epsilon)
     scaled_two = hidden * inverse_two[:, None]
     normed_two = (scaled_two * gain_two_f).astype(bf16)
 
     from_rows = [normed_two] + [swap(normed_two, "row", k) for k in range(1, n_row)]
     top = bits_down(n_col)[0]
-    traded, cot_all = after((traded, cot_all), normed_two)
+    near, far, cot_all = after((near, far, cot_all), normed_two)
     gate_parts, up_parts, down_parts = (
-        [weight] + parts for weight, parts in zip((w_gate, w_up, w_down), traded)
+        [weight, first] + parts
+        for weight, first, parts in zip((w_gate, w_up, w_down), near, far)
     )
     stages = list(reversed(bits_down(n_col)))
     sums = [[] for _ in range(n_row)]
@@ -604,7 +623,7 @@
             jnp.bitwise_xor(row, k),
             block,
             cot_all,
-            mask,
+            routes,
             router_weight,
             gate_parts,
             up_parts,
@@ -623,31 +642,38 @@
     down_pieces = weight_grad(
         after(lefts[2], arrived(n_row), gate_sum), cot_all, True, own_experts
     )
+    down_terms = send_dp(down_pieces)
     gate_sum = gate_sum + gate_terms[-1]
     gate_pieces = weight_grad(
         after(lefts[0], arrived(n_row + 1), gate_sum, down_pieces), normed_parts, True, own_experts
     )
+    gate_pair_terms = send_dp(gate_pieces)
     gate_half = swap(gate_sum, "col", top)
     last_sums = arrived(n_row + 2)
     up_pieces = weight_grad(
-        after(lefts[1], last_sums, gate_half, gate_pieces), normed_parts, True, own_experts
-    )
+        after(lefts[1], last_sums, gate_half, gate_pieces, down_terms), normed_parts, True, own_experts
+    )
+    up_terms = send_dp(up_pieces)
     mixed = lax.psum_scatter(
         after(mix, last_sums), ("row", "col"), scatter_dimension=0, tiled=False
     )
     arrived(n_row + 3)
-    token_sum, gate_blocks, _ = lax.optimization_barrier(
-        ([state[-1][0] for state in sums], {0: gate_sum, top: gate_half}, up_pieces)
+    token_sum, gate_blocks, gate_pair_terms, _ = lax.optimization_barrier(
+        ([state[-1][0] for state in sums], {0: gate_sum, top: gate_half}, gate_pair_terms, up_pieces)
     )
     for bit in bits_down(n_col)[1:]:
         for held in sorted(gate_blocks):
             gate_blocks[held | bit] = swap(gate_blocks[held], "col", bit)
-    gate_grads = jnp.zeros((expert_count, local_rows), f32)
-    for k in range(n_col):
-        gate_grads = lax.dynamic_update_slice_in_dim(
-            gate_grads, gate_blocks[k][:own_experts], relative[k] * own_experts, 0
-        )
-    gate_grads = gate_grads.T
+    gate_grads = jnp.concatenate(
+        [
+            sum(
+                jnp.where(relative[k] == owner, gate_blocks[k][:own_experts], 0.0)
+                for k in range(n_col)
+            )
+            for owner in range(n_col)
+        ],
+        axis=0,
+    ).T
     chosen_grads = own_gates * (
         gate_grads - jnp.sum(own_gates * gate_grads, axis=1, keepdims=True)
     )
@@ -668,41 +694,44 @@
 
     half = width // n_dp
 
-    def expert_grad(pieces):
-        summed = sum_dp(pieces)
-        total = jnp.zeros((expert_count,) + summed.shape[2:], f32)
+    def expert_sums(terms):
+        summed = add_up(terms)
+        return [summed[0]] + [swap(summed[k], "col", k) for k in reversed(range(1, n_col))][::-1]
+
+    def expert_grad(parts):
+        total = jnp.zeros((expert_count,) + parts[0].shape[1:], f32)
         for k in range(n_col):
-            part = swap(summed[k], "col", k) if k else summed[k]
             total = lax.dynamic_update_slice_in_dim(
-                total, part.astype(f32), relative[k] * own_experts, 0
+                total, parts[k].astype(f32), relative[k] * own_experts, 0
             )
         return total
 
-    down_out = jnp.transpose(expert_grad(down_pieces), (0, 2, 1))
-    gate_grad = expert_grad(gate_pieces)
-    up_grad = expert_grad(up_pieces)
-
-    def attn_grad(blocks):
+    expert_parts = [expert_sums(after(terms, branch_grads)) for terms in (down_terms, gate_pair_terms)]
+
+    def halves(blocks):
         part = blocks.shape[1] // n_dp
         blocks = blocks.reshape(n_col, n_dp, part, -1)
-        index = lax.axis_index("dp")
-        summed = sum_dp(
+        return send_dp(
             [
-                lax.dynamic_index_in_dim(blocks, lax.rem(index + step, n_dp), 1, False)
+                lax.dynamic_index_in_dim(blocks, lax.rem(dp_index + step, n_dp), 1, False)
                 for step in range(n_dp)
             ]
         )
-        total = 0.0
-        for bit in range(n_row):
-            block = lax.dynamic_index_in_dim(
-                summed, jnp.bitwise_xor(jnp.bitwise_xor(row, col), bit), 0, False
+
+    def cross(terms):
+        summed = add_up(terms)
+        return [
+            lax.ppermute(
+                lax.dynamic_index_in_dim(
+                    summed, jnp.bitwise_xor(jnp.bitwise_xor(row, col), bit), 0, False
+                ),
+                ("row", "col"),
+                crossed(n_row, n_col, bit),
             )
-            total = total + lax.ppermute(
-                block, ("row", "col"), crossed(n_row, n_col, bit)
-            ).astype(f32)
-        return total
-
-    out_grad = attn_grad(
+            for bit in range(n_row)
+        ]
+
+    out_terms = halves(
         jnp.stack(
             [
                 jnp.einsum(
@@ -728,11 +757,15 @@
                     own_lengths[s],
                     log_totals[s],
                     sequence(attended_grads, s),
+                    (up_terms, expert_parts[0]),
                 )
                 for s in range(sequences)
             ]
         )
     )
+    expert_parts.append(expert_sums(up_terms))
+    query_grads = after(query_grads, expert_parts[1])
+    out_terms = cross(after(out_terms, query_grads))
     query_grads = rotate(
         query_grads.reshape(-1, local_q, HEAD_SIZE), cosine, sine_part, -1.0
     ).reshape(-1, query_width)
@@ -741,12 +774,18 @@
     )
     qkv_grads = jnp.concatenate([query_grads, key_grads, value_grads], axis=1).astype(bf16)
     normed_one_grads = sum_col(feature_parts(qkv_grads, qkv_weight))
-
-    qkv_out = attn_grad(
+    expert_parts = after(expert_parts, normed_one_grads)
+    down_out = jnp.transpose(expert_grad(expert_parts[0]), (0, 2, 1))
+    gate_grad = expert_grad(expert_parts[1])
+    up_grad = expert_grad(expert_parts[2])
+
+    qkv_terms = halves(
         jnp.einsum("td,tj->dj", normed_one, qkv_grads, preferred_element_type=f32)
         .astype(bf16)
         .reshape(n_col, width, -1)
     )
+    qkv_out = sum(part.astype(f32) for part in cross(qkv_terms))
+    out_grad = sum(part.astype(f32) for part in after(out_terms, normed_one_grads))
 
     grad_scaled_one = normed_one_grads * gain_one_f
     stat_one = row_totals(jnp.sum(grad_scaled_one * scaled_one, axis=1)) / MODEL_WIDTH
@@ -754,14 +793,16 @@
         hidden_grads + inverse_one[:, None] * (grad_scaled_one - scaled_one * stat_one[:, None])
     ).astype(bf16)
     gain_one_part = jnp.sum(normed_one_grads * scaled_one, axis=0)
-    gain_one_grad = sum_all(gain_one_part, ("row", "dp"))
-    totals = sum_all(jnp.concatenate([gain_two_part[None], router_grad], axis=0), ("row", "dp"))
-    router_out = lax.dynamic_slice_in_dim(totals[1:], lax.axis_index("dp") * half, half, 1).T
+    totals = sum_all(
+        jnp.concatenate([gain_one_part[None], gain_two_part[None], router_grad], axis=0),
+        ("row", "dp"),
+    )
+    router_out = lax.dynamic_slice_in_dim(totals[2:], dp_index * half, half, 1).T
     return (
         block_out,
         input_grad,
-        gain_one_grad,
         totals[0],
+        totals[1],
         qkv_out[:, :query_width],
         qkv_out[:, query_width : query_width + kv_width],
         qkv_out[:, query_width + kv_width :],

time: 1030 us -> 969 us (0.941)
  starting transfers between devices: 144 us -> 91.4 us
  other arithmetic: 107 us -> 79.9 us
  matrix products: 78.5 us -> 96.8 us
  waiting for transfers between devices: 320 us -> 307 us
    ppermute x20 -> x14, waiting for transfers between devices: 136 us -> 84.6 us  [the longest x5 54.8 us: send_dp(): lax.ppermute(pieces[step], 'dp', [(i, (i + step) % size) for i in range(s...]
    ppermute x75 -> x78, waiting for transfers between devices: 173 us -> 222 us  [swap(): return lax.ppermute(block, axis, [(i, i ^ bit) for i in range(size)])]
    ppermute x75 -> x78, starting transfers between devices: 101 us -> 69.3 us  [swap(): return lax.ppermute(block, axis, [(i, i ^ bit) for i in range(size)])]
    sub x0 -> x1, matrix products: none -> 26.3 us  [attend_backward(): prob_grads - jnp.sum(softmax_probs * prob_grads, axis=-1, keepdims=True)]
    reduce_or x1 -> x0, other arithmetic: 21.8 us -> none  [on_device(): jnp.any(routes[:, :, None] == jnp.arange(LANES)[None, None, :], axis=1)]
    ppermute x20 -> x14, starting transfers between devices: 42.1 us -> 20.8 us  [the longest x8 14.5 us: cross(): lax.ppermute(lax.dynamic_index_in_dim(summed, jnp.bitwise_xor(jnp.bitwise...]
    convert_element_type x7 -> x6, other arithmetic: 24.1 us -> 6.3 us  [the longest x5 6.05 us: add_up(): return sum((term.astype(f32) for term in terms)).astype(bf16)]
    dot_general x1 -> x0, matrix products: 16 us -> none  [attend_backward(): jnp.einsum('qkgd,skd->kgqs', grad_grouped, value_heads, preferred_element...]
  transfers between devices with their start and end apart: 99 -> 97, of which waited for: 28 -> 29; matrix products, arithmetic and copies ran while one was open for 22% -> 23% of each run, Pallas kernels for 24% -> 26%
where the time goes in v3:
time: 969 us; the launch traced here: 963 us
  waiting for transfers between devices  307 us (32%)
  Pallas kernels  250 us (26%)
  matrix products  96.8 us (10%)
  starting transfers between devices  91.4 us (9%)
  other arithmetic  79.9 us (8%)
  local copies, waits for them, and re-layouts  63.4 us (7%)
  blocking collectives  58.4 us (6%)
  between operations  15.8 us (2%)
    ppermute x78, waiting for transfers between devices, swap(): return lax.ppermute(block, axis, [(i, i ^ bit) for i in range(size)])  222 us
    pallas_call x4, Pallas kernels, expert_block(): pl.pallas_call(lambda *refs: expert_kernel(n_col, own_experts, hidden_wid...  174 us
    pallas_call x3, Pallas kernels, weight_grad(): pl.pallas_call(lambda *refs: weight_grad_kernel(n_col, n_row, n_dp, whole...  76.5 us
    ppermute x78, starting transfers between devices, swap(): return lax.ppermute(block, axis, [(i, i ^ bit) for i in range(size)])  69.3 us
    psum x4, blocking collectives, row_totals(): return lax.psum(per_row, 'col')  58.4 us
    ppermute x5, waiting for transfers between devices, send_dp(): lax.ppermute(pieces[step], 'dp', [(i, (i + step) % size) for i in range(s...  54.8 us
    ppermute x8, waiting for transfers between devices, cross(): lax.ppermute(lax.dynamic_index_in_dim(summed, jnp.bitwise_xor(jnp.bitwise...  29.8 us
    sub x1, matrix products, attend_backward(): prob_grads - jnp.sum(softmax_probs * prob_grads, axis=-1, keepdims=True)  26.3 us
  transfers between devices with their start and end apart: 97, of which 29 were waited for; matrix products, arithmetic and copies ran while one was open for 23% of the time, Pallas kernels for 26%

profile of v3, /device:TPU:0, one launch (start us, length us, event | category | flops | bytes accessed | tf_op | source)
XLA Modules:
  0.0 963.0 jit_solution(12015275984757371660)
XLA Ops:
  10.9 33.7 %psum.28 = f32[1024]{0:T(1024)S(1)} all-reduce(f32[1024]{0:T(1024)S(1)} %fusion.33), channel_id=1, replica_groups=mesh['dp'=2,'row'=4,'col'=4] {'col'}, use_global_device_ids=true, to_apply=%region_1.0 | all-reduce | flops 1024 | bytes 8192 | tf_op jit(solution)/shard_map/psum | solution.py:436
  47.7 17.6 %collective-permute-done.1 = bf16[1024,384]{1,0:T(8,128)(2,1)S(1)} collective-permute-done((bf16[1024,384]{1,0:T(8,128)(2,1)S(1)}, bf16[1024,384]{1,0:T(8,128)(2,1)S(1)}, u32[]{:S(2)}, u32[]{:S(2)}) %collective-permute-start.1) | collective-permute-done | bytes 786464 | tf_op jit(solution)/shard_map/ppermute | solution.py:22
  71.3 21.5 %collective-permute-done.4 = bf16[40,384]{1,0:T(8,128)(2,1)S(1)} collective-permute-done((bf16[40,384]{1,0:T(8,128)(2,1)S(1)}, bf16[40,384]{1,0:T(8,128)(2,1)S(1)}, u32[]{:S(2)}, u32[]{:S(2)}) %collective-permute-start.4) | collective-permute-done | bytes 30752 | tf_op jit(solution)/shard_map/ppermute | solution.py:22
  113.4 15.3 %collective-permute-done.9 = bf16[10,192,128]{2,1,0:T(8,128)(2,1)} collective-permute-done((bf16[10,192,128]{2,1,0:T(8,128)(2,1)}, bf16[10,192,128]{2,1,0:T(8,128)(2,1)}, u32[]{:S(2)}, u32[]{:S(2)}) %collective-permute-start.9) | collective-permute-done | bytes 491552 | tf_op jit(solution)/shard_map/ppermute | solution.py:22
  128.7 10.5 %collective-permute-done.10 = bf16[10,64,384]{2,1,0:T(8,128)(2,1)} collective-permute-done((bf16[10,64,384]{2,1,0:T(8,128)(2,1)}, bf16[10,64,384]{2,1,0:T(8,128)(2,1)}, u32[]{:S(2)}, u32[]{:S(2)}) %collective-permute-start.10) | collective-permute-done | bytes 491552 | tf_op jit(solution)/shard_map/ppermute | solution.py:22
  139.3 9.6 %collective-permute-done.11 = bf16[10,64,384]{2,1,0:T(8,128)(2,1)} collective-permute-done((bf16[10,64,384]{2,1,0:T(8,128)(2,1)}, bf16[10,64,384]{2,1,0:T(8,128)(2,1)}, u32[]{:S(2)}, u32[]{:S(2)}) %collective-permute-start.11) | collective-permute-done | bytes 491552 | tf_op jit(solution)/shard_map/ppermute | solution.py:22
  160.8 10.6 %collective-permute-done.13 = bf16[10,192,128]{2,1,0:T(8,128)(2,1)} collective-permute-done((bf16[10,192,128]{2,1,0:T(8,128)(2,1)}, bf16[10,192,128]{2,1,0:T(8,128)(2,1)}, u32[]{:S(2)}, u32[]{:S(2)}) %collective-permute-start.13) | collective-permute-done | bytes 491552 | tf_op jit(solution)/shard_map/ppermute | solution.py:22
  200.0 10.7 %fusion.35 = bf16[2,64,3,1024]{3,1,2,0:T(8,128)(2,1)S(1)} fusion(bf16[1024,2,64,1]{0,2,3,1:T(8,128)(2,1)S(1)} %bitcast.259, f32[2,3,1024,1024]{2,3,1,0:T(8,128)} %copy-done.2, f32[2,3,1024]{2,1,0:T(4,128)S(1)} %fusion.3, f32[2,3,1024]{2,1,0:T(4,128)S(1)} %get-tuple-element.345), kind=kOutput, calls=%fused_computation.79 | convolution fusion | flops 824573952 | bytes 26263552 | tf_op jit(solution)/shard_map/kgqs,skd->qkgd/dot_general | solution.py:400
  220.6 7.4 collective-permute-done.19
  230.4 7.7 collective-permute-done.20
  241.3 12.2 %collective-permute-done.18 = bf16[1024,384]{1,0:T(8,128)(2,1)S(1)} collective-permute-done((bf16[1024,384]{1,0:T(8,128)(2,1)S(1)}, bf16[1024,384]{1,0:T(8,128)(2,1)S(1)}, u32[]{:S(2)}, u32[]{:S(2)}) %collective-permute-start.18) | collective-permute-done | bytes 786464 | tf_op jit(solution)/shard_map/ppermute | solution.py:22
  277.4 9.9 %collective-permute-done.37 = bf16[10,64,384]{2,1,0:T(8,128)(2,1)} collective-permute-done((bf16[10,64,384]{2,1,0:T(8,128)(2,1)}, bf16[10,64,384]{2,1,0:T(8,128)(2,1)}, u32[]{:S(2)}, u32[]{:S(2)}) %collective-permute-start.37) | collective-permute-done | bytes 491552 | tf_op jit(solution)/shard_map/ppermute | solution.py:22
  297.3 20.0 %collective-permute-done.27.refs_1_.refs_9_ = bf16[1024,384]{1,0:T(8,128)(2,1)} collective-permute-done((bf16[1024,384]{1,0:T(8,128)(2,1)S(1)}, bf16[1024,384]{1,0:T(8,128)(2,1)}, u32[]{:S(2)}, u32[]{:S(2)}) %collective-permute-start.27) | collective-permute-done | bytes 786464 | tf_op jit(solution)/shard_map/ppermute | solution.py:22
  322.1 43.4 %experts.4 = (bf16[1024,384]{1,0:T(8,128)(2,1)}, bf16[1024,384]{1,0:T(8,128)(2,1)}, bf16[1024,384]{1,0:T(8,128)(2,1)}, bf16[1024,384]{1,0:T(8,128)(2,1)}, bf16[1...) custom-call(s32[10]{0:T(128)} %stack.100.refs_0_, ...), custom_call_target="tpu_custom_call" | custom-call | flops 24159191040 | bytes 41943040 | tf_op jit(solution)/shard_map/experts/pallas_call | solution.py:218
  374.2 43.6 %experts.5 = (bf16[1024,384]{1,0:T(8,128)(2,1)}, bf16[1024,384]{1,0:T(8,128)(2,1)}, bf16[1024,384]{1,0:T(8,128)(2,1)}, bf16[1024,384]{1,0:T(8,128)(2,1)}, bf16[1...) custom-call(s32[10]{0:T(128)} %stack.94.refs_0_, ...), custom_call_target="tpu_custom_call", output_to_operand_aliasing={{4}: (23, {})} | custom-call | flops 24159191040 | bytes 41943040 | tf_op jit(solution)/shard_map/experts/pallas_call | solution.py:218
  425.4 43.4 %experts.6 = (bf16[1024,384]{1,0:T(8,128)(2,1)}, bf16[1024,384]{1,0:T(8,128)(2,1)}, bf16[1024,384]{1,0:T(8,128)(2,1)}, bf16[1024,384]{1,0:T(8,128)(2,1)}, bf16[1...) custom-call(s32[10]{0:T(128)} %stack.88.refs_0_, ...), custom_call_target="tpu_custom_call", output_to_operand_aliasing={{4}: (23, {})} | custom-call | flops 24159191040 | bytes 41943040 | tf_op jit(solution)/shard_map/experts/pallas_call | solution.py:218
  470.7 15.3 %collective-permute-start.56 = (f32[16,1024]{1,0:T(8,128)}, f32[16,1024]{1,0:T(8,128)}, u32[]{:S(2)}, u32[]{:S(2)}) collective-permute-start(f32[16,1024]{1,0:T(8,128)} %get-tuple-element.216), channel_id=1, source_target_pairs={{0,4},{4,0},{8,12},{12,8},{1,5},{5,1},{9,13},{13,9},{2,6},{6,2},{1... | collective-permute-start | bytes 196616 | tf_op jit(solution)/shard_map/ppermute | solution.py:22
  494.3 43.5 %experts.7 = (bf16[1024,384]{1,0:T(8,128)(2,1)}, bf16[1024,384]{1,0:T(8,128)(2,1)}, bf16[1024,384]{1,0:T(8,128)(2,1)}, bf16[1024,384]{1,0:T(8,128)(2,1)}, bf16[1...) custom-call(s32[10]{0:T(128)} %stack.82.refs_0_, ...), custom_call_target="tpu_custom_call", output_to_operand_aliasing={{4}: (23, {})} | custom-call | flops 24159191040 | bytes 41943040 | tf_op jit(solution)/shard_map/experts/pallas_call | solution.py:218
  545.7 25.2 %weight_grads.3 = bf16[2,4,10,192,128]{4,3,2,1,0:T(8,128)(2,1)} custom-call(s32[17]{0:T(128)} %stack.102.refs_0_, bf16[1024,1280]{1,0:T(8,128)(2,1)} %get-tuple-element.227.refs_1_, bf16[1024,1280]{1,0:T(8,128)(2,1)} %get-tuple-element.228.refs_2_, bf16[1024,1280]{1,0:T(8,128)(2,1)} %get-tuple-element.229.refs_3_, ...), custom_call_target="tpu_custom_call" | custom-call | flops 16106127360 | bytes 20971520 | tf_op jit(solution)/shard_map/weight_grads/pallas_call | solution.py:313
  582.6 24.8 %weight_grads.4 = bf16[2,4,10,192,128]{4,3,2,1,0:T(8,128)(2,1)} custom-call(s32[17]{0:T(128)} %stack.102.refs_0_, bf16[1024,1280]{1,0:T(8,128)(2,1)} %get-tuple-element.231.refs_1_, bf16[1024,1280]{1,0:T(8,128)(2,1)} %get-tuple-element.232.refs_2_, bf16[1024,1280]{1,0:T(8,128)(2,1)} %get-tuple-element.233.refs_3_, ...), custom_call_target="tpu_custom_call" | custom-call | flops 16106127360 | bytes 20971520 | tf_op jit(solution)/shard_map/weight_grads/pallas_call | solution.py:313
  621.1 26.5 %weight_grads.5 = bf16[2,4,10,192,128]{4,3,2,1,0:T(8,128)(2,1)} custom-call(s32[17]{0:T(128)} %stack.102.refs_0_, bf16[1024,1280]{1,0:T(8,128)(2,1)} %get-tuple-element.239.refs_1_, bf16[1024,1280]{1,0:T(8,128)(2,1)} %get-tuple-element.240.refs_2_, bf16[1024,1280]{1,0:T(8,128)(2,1)} %get-tuple-element.241.refs_3_, ...), custom_call_target="tpu_custom_call" | custom-call | flops 16106127360 | bytes 20971520 | tf_op jit(solution)/shard_map/weight_grads/pallas_call | solution.py:313
  647.6 15.4 %collective-permute-done.60 = bf16[4,10,192,128]{3,2,1,0:T(8,128)(2,1)} collective-permute-done((bf16[4,10,192,128]{3,2,1,0:T(8,128)(2,1)}, bf16[4,10,192,128]{3,2,1,0:T(8,128)(2,1)}, u32[]{:S(2)}, u32[]{:S(2)}) %collective-permute-start.60) | collective-permute-done | bytes 1966112 | tf_op jit(solution)/shard_map/ppermute | solution.py:336
  687.0 14.0 %collective-permute-done.65 = bf16[1024,384]{1,0:T(8,128)(2,1)} collective-permute-done((bf16[1024,384]{1,0:T(8,128)(2,1)}, bf16[1024,384]{1,0:T(8,128)(2,1)}, u32[]{:S(2)}, u32[]{:S(2)}) %collective-permute-start.65) | collective-permute-done | bytes 786464 | tf_op jit(solution)/shard_map/ppermute | solution.py:22
  704.7 7.4 collective-permute-done.67
  727.7 13.1 %fusion.41 = bf16[2,64,1024]{2,1,0:T(8,128)(2,1)} fusion(bf16[1024,2,3,64]{0,3,2,1:T(8,128)(2,1)} %bitcast.242, f32[2,3,1024,1024]{2,3,1,0:T(8,128)} %copy-done.2, f32[2,3,1024]{2,1,0:T(4,128)} %log_add_fusion), kind=kOutput, calls=%fused_computation.94 | convolution fusion | flops 818020352 | bytes 26238976 | tf_op jit(solution)/shard_map/kgqs,qkgd->skd/dot_general | solution.py:425
  740.7 26.3 %fusion.2 = bf16[2,3,1024,1024]{2,3,1,0:T(8,128)(2,1)} fusion(f32[2,3,1024,1024]{2,3,1,0:T(8,128)} %copy-done.2, f32[2,3,1024]{2,1,0:T(4,128)} %log_add_fusion, bf16[1024,2,64,1]{0,2,3,1:T(8,128)(2,1)} %bitcast.258, bf16[1024,2,3,64]{0,3,2,1:T(8,128)(2,1)} %bitcast.243), kind=kOutput, calls=%fused_computation.4 | convolution fusion | flops 1648368640 | bytes 38821888 | tf_op jit(solution)/shard_map/sub | solution.py:416
  781.6 9.2 collective-permute-done.73
  790.8 8.7 fusion.40
  810.6 30.7 %collective-permute-done.85 = bf16[4,192,384]{2,1,0:T(8,128)(2,1)S(1)} collective-permute-done((bf16[4,192,384]{2,1,0:T(8,128)(2,1)S(1)}, bf16[4,192,384]{2,1,0:T(8,128)(2,1)S(1)}, u32[]{:S(2)}, u32[]{:S(2)}) %collective-permute-start.85) | collective-permute-done | bytes 589856 | tf_op jit(solution)/shard_map/ppermute | solution.py:336
  853.3 24.4 %collective-permute-done.83 = bf16[192,640]{1,0:T(8,128)(2,1)S(1)} collective-permute-done((bf16[192,640]{1,0:T(8,128)(2,1)S(1)}, bf16[192,640]{1,0:T(8,128)(2,1)S(1)}, u32[]{:S(2)}, u32[]{:S(2)}) %collective-permute-start.83) | collective-permute-done | bytes 245792 | tf_op jit(solution)/shard_map/ppermute | solution.py:724
  899.0 14.3 %collective-permute-done.92 = bf16[10,192,128]{2,1,0:T(8,128)(2,1)S(1)} collective-permute-done((bf16[10,192,128]{2,1,0:T(8,128)(2,1)S(1)}, bf16[10,192,128]{2,1,0:T(8,128)(2,1)S(1)}, u32[]{:S(2)}, u32[]{:S(2)}) %collective-permute-start.92) | collective-permute-done | bytes 491552 | tf_op jit(solution)/shard_map/ppermute | solution.py:22
  936.2 10.4 %psum.31 = f32[1024]{0:T(1024)S(1)} all-reduce(f32[1024]{0:T(1024)S(1)} %get-tuple-element.279), channel_id=1, replica_groups=mesh['dp'=2,'row'=4,'col'=4] {'col'}, use_global_device_ids=true, to_apply=%region_14.15 | all-reduce | flops 1024 | bytes 8192 | tf_op jit(solution)/shard_map/psum | solution.py:436
  (512 shorter events, 320.7 us)
Async XLA Ops:
  7.2 141.7 %all-gather.7.cloned.1.call-start = ((), (), s32[]{:S(2)}) async-start(), calls=%async_computation.2 | async-start | bytes 2457600 | tf_op jit(solution)/shard_map/all_gather | solution.py:482
  9.9 200.8 %all-gather.9.cloned.1.call-start = ((), (), s32[]{:S(2)}) async-start(), calls=%async_computation.3 | async-start | bytes 1474560 | tf_op jit(solution)/shard_map/all_gather | solution.py:523
  47.7 53.6 %collective-permute-start = (bf16[1024,384]{1,0:T(8,128)(2,1)S(1)}, bf16[1024,384]{1,0:T(8,128)(2,1)S(1)}, u32[]{:S(2)}, u32[]{:S(2)}) collective-permute-start(bf16[1024,384]{1,0:T(8,128)(2,1)S(1)} %fusion.26), channel_id=1, source_target_pairs={{0,1},{1,0},{2,3},{3,2},{4,5},{5,4},{6,7},{7,6},{8,9},{9,8},{10,11... | collective-permute-start | bytes 2359304 | tf_op jit(solution)/shard_map/ppermute | solution.py:22
  101.4 47.5 %collective-permute-start.11 = (bf16[10,64,384]{2,1,0:T(8,128)(2,1)}, bf16[10,64,384]{2,1,0:T(8,128)(2,1)}, u32[]{:S(2)}, u32[]{:S(2)}) collective-permute-start(bf16[10,64,384]{2,1,0:T(8,128)(2,1)} %get-tuple-element.290), channel_id=1, source_target_pairs={{0,3},{1,2},{2,1},{3,0},{4,7},{5,6},{6,5},{7,4},{8,11},{9,10},{10,... | collective-permute-start | bytes 1474568 | tf_op jit(solution)/shard_map/ppermute | solution.py:22
  103.0 46.0 %collective-permute-start.15 = (bf16[384,384]{0,1:T(8,128)(2,1)S(1)}, bf16[384,384]{0,1:T(8,128)(2,1)S(1)}, u32[]{:S(2)}, u32[]{:S(2)}) collective-permute-start(bf16[384,384]{0,1:T(8,128)(2,1)S(1)} %bitcast.286), channel_id=1, source_target_pairs={{0,0},{1,4},{2,8},{3,12},{4,1},{5,5},{6,9},{7,13},{8,2},{9,6},{10,... | collective-permute-start | bytes 884744 | tf_op jit(solution)/shard_map/ppermute | solution.py:481
  149.7 172.4 %all-gather.11.cloned.1.call-start = ((), (), s32[]{:S(2)}) async-start(), calls=%async_computation.4 | async-start | bytes 13369344 | tf_op jit(solution)/shard_map/all_gather | solution.py:525
  155.1 797.3 %reduce-scatter.2.cloned.1.call-start = ((), (), s32[]{:S(2)}) async-start(), calls=%async_computation.1 | async-start | bytes 13369344 | tf_op jit(solution)/shard_map/reduce_scatter | solution.py:657
  267.3 53.8 %collective-permute-start.33 = (bf16[10,384,128]{2,1,0:T(8,128)(2,1)}, bf16[10,384,128]{2,1,0:T(8,128)(2,1)}, u32[]{:S(2)}, u32[]{:S(2)}) collective-permute-start(bf16[10,384,128]{2,1,0:T(8,128)(2,1)} %constant_dynamic-slice_fusion.2), channel_id=1, source_target_pairs={{0,1},{1,0},{2,3},{3,2},{4,5},{5,4},{6,7},{7,6},{8,9},{9,8},{10,11... | collective-permute-start | bytes 2949128 | tf_op jit(solution)/shard_map/ppermute | solution.py:22
  317.3 55.5 %collective-permute-start.24 = (bf16[1024,384]{1,0:T(8,128)(2,1)S(1)}, bf16[1024,384]{1,0:T(8,128)(2,1)}, u32[]{:S(2)}, u32[]{:S(2)}) collective-permute-start(bf16[1024,384]{1,0:T(8,128)(2,1)S(1)} %multiply_convert_fusion.refs_1_.refs_5_), channel_id=1, source_target_pairs={{0,8},{4,12},{8,0},{12,4},{1,9},{5,13},{9,1},{13,5},{2,10},{6,14},... | collective-permute-start | bytes 2359304 | tf_op jit(solution)/shard_map/ppermute | solution.py:22
  321.0 52.3 %collective-permute-start.21 = (bf16[1024,384]{1,0:T(8,128)(2,1)S(1)}, bf16[1024,384]{1,0:T(8,128)(2,1)}, u32[]{:S(2)}, u32[]{:S(2)}) collective-permute-start(bf16[1024,384]{1,0:T(8,128)(2,1)S(1)} %multiply_convert_fusion.refs_1_.refs_5_), channel_id=1, source_target_pairs={{0,12},{4,8},{8,4},{12,0},{1,13},{5,9},{9,5},{13,1},{2,14},{6,10},... | collective-permute-start | bytes 2359304 | tf_op jit(solution)/shard_map/ppermute | solution.py:22
  321.2 52.1 %collective-permute-start.28 = (bf16[1024,384]{1,0:T(8,128)(2,1)}, bf16[1024,384]{1,0:T(8,128)(2,1)}, u32[]{:S(2)}, u32[]{:S(2)}) collective-permute-start(bf16[1024,384]{1,0:T(8,128)(2,1)} %collective-permute-done.27.refs_1_.refs_9_), channel_id=1, source_target_pairs={{0,1},{1,0},{2,3},{3,2},{4,5},{5,4},{6,7},{7,6},{8,9},{9,8},{10,11... | collective-permute-start | bytes 2359304 | tf_op jit(solution)/shard_map/ppermute | solution.py:22
  372.9 45.7 %collective-permute-start.26 = (bf16[1024,384]{1,0:T(8,128)(2,1)}, bf16[1024,384]{1,0:T(8,128)(2,1)}, u32[]{:S(2)}, u32[]{:S(2)}) collective-permute-start(bf16[1024,384]{1,0:T(8,128)(2,1)} %collective-permute-done.24.refs_1_.refs_13_), channel_id=1, source_target_pairs={{0,2},{1,3},{2,0},{3,1},{4,6},{5,7},{6,4},{7,5},{8,10},{9,11},{10,... | collective-permute-start | bytes 2359304 | tf_op jit(solution)/shard_map/ppermute | solution.py:22
  373.3 47.8 %collective-permute-start.41 = (bf16[1024,384]{1,0:T(8,128)(2,1)}, bf16[1024,384]{1,0:T(8,128)(2,1)S(1)}, u32[]{:S(2)}, u32[]{:S(2)}) collective-permute-start(bf16[1024,384]{1,0:T(8,128)(2,1)} %get-tuple-element.182), channel_id=1, source_target_pairs={{0,1},{1,0},{2,3},{3,2},{4,5},{5,4},{6,7},{7,6},{8,9},{9,8},{10,11... | collective-permute-start | bytes 2359304 | tf_op jit(solution)/shard_map/ppermute | solution.py:22
  419.5 49.2 %collective-permute-start.23 = (bf16[1024,384]{1,0:T(8,128)(2,1)}, bf16[1024,384]{1,0:T(8,128)(2,1)}, u32[]{:S(2)}, u32[]{:S(2)}) collective-permute-start(bf16[1024,384]{1,0:T(8,128)(2,1)} %collective-permute-done.21.refs_1_.refs_17_), channel_id=1, source_target_pairs={{0,2},{1,3},{2,0},{3,1},{4,6},{5,7},{6,4},{7,5},{8,10},{9,11},{10,... | collective-permute-start | bytes 2359304 | tf_op jit(solution)/shard_map/ppermute | solution.py:22
  421.1 47.8 %collective-permute-start.40 = (bf16[1024,384]{1,0:T(8,128)(2,1)}, bf16[1024,384]{1,0:T(8,128)(2,1)}, u32[]{:S(2)}, u32[]{:S(2)}) collective-permute-start(bf16[1024,384]{1,0:T(8,128)(2,1)} %get-tuple-element.180), channel_id=1, source_target_pairs={{0,1},{1,0},{2,3},{3,2},{4,5},{5,4},{6,7},{7,6},{8,9},{9,8},{10,11... | collective-permute-start | bytes 2359304 | tf_op jit(solution)/shard_map/ppermute | solution.py:22
  421.3 67.7 %collective-permute-start.44 = (bf16[1024,384]{1,0:T(8,128)(2,1)}, bf16[1024,384]{1,0:T(8,128)(2,1)S(1)}, u32[]{:S(2)}, u32[]{:S(2)}) collective-permute-start(bf16[1024,384]{1,0:T(8,128)(2,1)} %get-tuple-element.190), channel_id=1, source_target_pairs={{0,1},{1,0},{2,3},{3,2},{4,5},{5,4},{6,7},{7,6},{8,9},{9,8},{10,11... | collective-permute-start | bytes 2359304 | tf_op jit(solution)/shard_map/ppermute | solution.py:22
  423.3 47.4 %collective-permute-start.43 = (bf16[1024,384]{1,0:T(8,128)(2,1)S(1)}, bf16[1024,384]{1,0:T(8,128)(2,1)}, u32[]{:S(2)}, u32[]{:S(2)}) collective-permute-start(bf16[1024,384]{1,0:T(8,128)(2,1)S(1)} %fusion.62), channel_id=1, source_target_pairs={{0,2},{1,3},{2,0},{3,1},{4,6},{5,7},{6,4},{7,5},{8,10},{9,11},{10,... | collective-permute-start | bytes 2359304 | tf_op jit(solution)/shard_map/ppermute | solution.py:22
  424.1 65.0 %collective-permute-start.53 = (bf16[1024,384]{1,0:T(8,128)(2,1)S(1)}, bf16[1024,384]{1,0:T(8,128)(2,1)S(1)}, u32[]{:S(2)}, u32[]{:S(2)}) collective-permute-start(bf16[1024,384]{1,0:T(8,128)(2,1)S(1)} %fusion.63), channel_id=1, source_target_pairs={{0,2},{1,3},{2,0},{3,1},{4,6},{5,7},{6,4},{7,5},{8,10},{9,11},{10,... | collective-permute-start | bytes 2359304 | tf_op jit(solution)/shard_map/ppermute | solution.py:22
  470.7 70.4 %collective-permute-start.56 = (f32[16,1024]{1,0:T(8,128)}, f32[16,1024]{1,0:T(8,128)}, u32[]{:S(2)}, u32[]{:S(2)}) collective-permute-start(f32[16,1024]{1,0:T(8,128)} %get-tuple-element.216), channel_id=1, source_target_pairs={{0,4},{4,0},{8,12},{12,8},{1,5},{5,1},{9,13},{13,9},{2,6},{6,2},{1... | collective-permute-start | bytes 196616 | tf_op jit(solution)/shard_map/ppermute | solution.py:22
  489.0 48.8 %collective-permute-start.47 = (bf16[1024,384]{1,0:T(8,128)(2,1)}, bf16[1024,384]{1,0:T(8,128)(2,1)}, u32[]{:S(2)}, u32[]{:S(2)}) collective-permute-start(bf16[1024,384]{1,0:T(8,128)(2,1)} %get-tuple-element.202), channel_id=1, source_target_pairs={{0,1},{1,0},{2,3},{3,2},{4,5},{5,4},{6,7},{7,6},{8,9},{9,8},{10,11... | collective-permute-start | bytes 2359304 | tf_op jit(solution)/shard_map/ppermute | solution.py:22
  489.1 86.2 %collective-permute-start.46 = (bf16[1024,384]{1,0:T(8,128)(2,1)}, bf16[1024,384]{1,0:T(8,128)(2,1)S(1)}, u32[]{:S(2)}, u32[]{:S(2)}) collective-permute-start(bf16[1024,384]{1,0:T(8,128)(2,1)} %get-tuple-element.200), channel_id=1, source_target_pairs={{0,1},{1,0},{2,3},{3,2},{4,5},{5,4},{6,7},{7,6},{8,9},{9,8},{10,11... | collective-permute-start | bytes 2359304 | tf_op jit(solution)/shard_map/ppermute | solution.py:22
  490.8 51.2 %collective-permute-start.57 = (f32[16,1024]{1,0:T(8,128)}, f32[16,1024]{1,0:T(8,128)S(1)}, u32[]{:S(2)}, u32[]{:S(2)}) collective-permute-start(f32[16,1024]{1,0:T(8,128)} %get-tuple-element.217), channel_id=1, source_target_pairs={{0,8},{4,12},{8,0},{12,4},{1,9},{5,13},{9,1},{13,5},{2,10},{6,14},... | collective-permute-start | bytes 196616 | tf_op jit(solution)/shard_map/ppermute | solution.py:22
  492.3 90.2 %collective-permute-start.54 = (bf16[1024,384]{1,0:T(8,128)(2,1)}, bf16[1024,384]{1,0:T(8,128)(2,1)S(1)}, u32[]{:S(2)}, u32[]{:S(2)}) collective-permute-start(bf16[1024,384]{1,0:T(8,128)(2,1)} %convert_add_fusion.4), channel_id=1, source_target_pairs={{0,4},{4,0},{8,12},{12,8},{1,5},{5,1},{9,13},{13,9},{2,6},{6,2},{1... | collective-permute-start | bytes 2359304 | tf_op jit(solution)/shard_map/ppermute | solution.py:22
  544.2 69.4 %collective-permute-start.50 = (bf16[1024,384]{1,0:T(8,128)(2,1)}, bf16[1024,384]{1,0:T(8,128)(2,1)}, u32[]{:S(2)}, u32[]{:S(2)}) collective-permute-start(bf16[1024,384]{1,0:T(8,128)(2,1)} %get-tuple-element.211), channel_id=1, source_target_pairs={{0,1},{1,0},{2,3},{3,2},{4,5},{5,4},{6,7},{7,6},{8,9},{9,8},{10,11... | collective-permute-start | bytes 2359304 | tf_op jit(solution)/shard_map/ppermute | solution.py:22
  575.3 45.8 %collective-permute-start.61 = (bf16[4,10,192,128]{3,2,1,0:T(8,128)(2,1)}, bf16[4,10,192,128]{3,2,1,0:T(8,128)(2,1)S(1)}, u32[]{:S(2)}, u32[]{:S(2)}) collective-permute-start(bf16[4,10,192,128]{3,2,1,0:T(8,128)(2,1)} %get-tuple-element.286), channel_id=1, source_target_pairs={{0,16},{16,0},{1,17},{17,1},{2,18},{18,2},{3,19},{19,3},{4,20},{20... | collective-permute-start | bytes 5898248 | tf_op jit(solution)/shard_map/ppermute | solution.py:336
  611.8 51.2 %collective-permute-start.60 = (bf16[4,10,192,128]{3,2,1,0:T(8,128)(2,1)}, bf16[4,10,192,128]{3,2,1,0:T(8,128)(2,1)}, u32[]{:S(2)}, u32[]{:S(2)}) collective-permute-start(bf16[4,10,192,128]{3,2,1,0:T(8,128)(2,1)} %get-tuple-element.288), channel_id=1, source_target_pairs={{0,16},{16,0},{1,17},{17,1},{2,18},{18,2},{3,19},{19,3},{4,20},{20... | collective-permute-start | bytes 5898248 | tf_op jit(solution)/shard_map/ppermute | solution.py:336
  720.9 48.2 %collective-permute-start.68 = (bf16[10,192,128]{2,1,0:T(8,128)(2,1)}, bf16[10,192,128]{2,1,0:T(8,128)(2,1)}, u32[]{:S(2)}, u32[]{:S(2)}) collective-permute-start(bf16[10,192,128]{2,1,0:T(8,128)(2,1)} %get-tuple-element.306), channel_id=1, source_target_pairs={{0,1},{1,0},{2,3},{3,2},{4,5},{5,4},{6,7},{7,6},{8,9},{9,8},{10,11... | collective-permute-start | bytes 1474568 | tf_op jit(solution)/shard_map/ppermute | solution.py:22
  720.9 49.0 %collective-permute-start.69 = (bf16[10,192,128]{2,1,0:T(8,128)(2,1)}, bf16[10,192,128]{2,1,0:T(8,128)(2,1)}, u32[]{:S(2)}, u32[]{:S(2)}) collective-permute-start(bf16[10,192,128]{2,1,0:T(8,128)(2,1)} %get-tuple-element.305), channel_id=1, source_target_pairs={{0,2},{1,3},{2,0},{3,1},{4,6},{5,7},{6,4},{7,5},{8,10},{9,11},{10,... | collective-permute-start | bytes 1474568 | tf_op jit(solution)/shard_map/ppermute | solution.py:22
  722.1 47.8 %collective-permute-start.70 = (bf16[10,192,128]{2,1,0:T(8,128)(2,1)}, bf16[10,192,128]{2,1,0:T(8,128)(2,1)}, u32[]{:S(2)}, u32[]{:S(2)}) collective-permute-start(bf16[10,192,128]{2,1,0:T(8,128)(2,1)} %get-tuple-element.304), channel_id=1, source_target_pairs={{0,3},{1,2},{2,1},{3,0},{4,7},{5,6},{6,5},{7,4},{8,11},{9,10},{10,... | collective-permute-start | bytes 1474568 | tf_op jit(solution)/shard_map/ppermute | solution.py:22
  809.3 73.5 %collective-permute-start.74 = (bf16[1024,384]{1,0:T(8,128)(2,1)S(1)}, bf16[1024,384]{1,0:T(8,128)(2,1)S(1)}, u32[]{:S(2)}, u32[]{:S(2)}) collective-permute-start(bf16[1024,384]{1,0:T(8,128)(2,1)S(1)} %convolution_convert_fusion.2), channel_id=1, source_target_pairs={{0,1},{1,0},{2,3},{3,2},{4,5},{5,4},{6,7},{7,6},{8,9},{9,8},{10,11... | collective-permute-start | bytes 2359304 | tf_op jit(solution)/shard_map/ppermute | solution.py:22
  882.8 52.5 %collective-permute-start.86 = (bf16[192,384]{1,0:T(8,128)(2,1)S(1)}, bf16[192,384]{1,0:T(8,128)(2,1)S(1)}, u32[]{:S(2)}, u32[]{:S(2)}) collective-permute-start(bf16[192,384]{1,0:T(8,128)(2,1)S(1)} %get-tuple-element.335), channel_id=1, source_target_pairs={{0,0},{1,4},{2,8},{3,12},{4,1},{5,5},{6,9},{7,13},{8,2},{9,6},{10,... | collective-permute-start | bytes 442376 | tf_op jit(solution)/shard_map/ppermute | solution.py:724
  883.5 51.8 %collective-permute-start.87 = (bf16[192,384]{1,0:T(8,128)(2,1)S(1)}, bf16[192,384]{1,0:T(8,128)(2,1)S(1)}, u32[]{:S(2)}, u32[]{:S(2)}) collective-permute-start(bf16[192,384]{1,0:T(8,128)(2,1)S(1)} %get-tuple-element.334), channel_id=1, source_target_pairs={{0,1},{1,5},{2,9},{3,13},{4,0},{5,4},{6,8},{7,12},{8,3},{9,7},{10,... | collective-permute-start | bytes 442376 | tf_op jit(solution)/shard_map/ppermute | solution.py:724
  (163 other events, 2821.3 us)
Sparse Core Ops, SparseCore 0:
  10.2 70.6 all-gather.6
  149.8 29.0 all-gather.8
  181.2 127.4 all-gather.10
  619.0 139.0 reduce-scatter.1

commit v4 on v3

--- a/solution.py
+++ b/solution.py
@@ -757,15 +757,15 @@
                     own_lengths[s],
                     log_totals[s],
                     sequence(attended_grads, s),
-                    (up_terms, expert_parts[0]),
+                    (up_terms, expert_parts[0], out_terms),
                 )
                 for s in range(sequences)
             ]
         )
     )
     expert_parts.append(expert_sums(up_terms))
-    query_grads = after(query_grads, expert_parts[1])
-    out_terms = cross(after(out_terms, query_grads))
+    out_terms = cross(out_terms)
+    query_grads = after(query_grads, expert_parts[1], out_terms)
     query_grads = rotate(
         query_grads.reshape(-1, local_q, HEAD_SIZE), cosine, sine_part, -1.0
     ).reshape(-1, query_width)

time: 969 us -> 967 us (level)
    ppermute x8, waiting for transfers between devices: 29.8 us -> 61.3 us  [cross(): lax.ppermute(lax.dynamic_index_in_dim(summed, jnp.bitwise_xor(jnp.bitwise...]
    ppermute x5, waiting for transfers between devices: 54.8 us -> 37.7 us  [send_dp(): lax.ppermute(pieces[step], 'dp', [(i, (i + step) % size) for i in range(s...]
    ppermute x78, starting transfers between devices: 69.3 us -> 79.1 us  [swap(): return lax.ppermute(block, axis, [(i, i ^ bit) for i in range(size)])]
  transfers between devices with their start and end apart: 97 -> 97, of which waited for: 29 -> 30; matrix products, arithmetic and copies ran while one was open for 23% -> 22% of each run, Pallas kernels for 26% -> 26%
where the time goes in v4:
time: 967 us; the launch traced here: 961 us
  waiting for transfers between devices  313 us (32%)
  Pallas kernels  249 us (26%)
  starting transfers between devices  95.9 us (10%)
  matrix products  92.2 us (10%)
  other arithmetic  77.5 us (8%)
  local copies, waits for them, and re-layouts  62.7 us (6%)
  blocking collectives  55.1 us (6%)
  between operations  15.6 us (2%)
    ppermute x78, waiting for transfers between devices, swap(): return lax.ppermute(block, axis, [(i, i ^ bit) for i in range(size)])  214 us
    pallas_call x4, Pallas kernels, expert_block(): pl.pallas_call(lambda *refs: expert_kernel(n_col, own_experts, hidden_wid...  174 us
    ppermute x78, starting transfers between devices, swap(): return lax.ppermute(block, axis, [(i, i ^ bit) for i in range(size)])  79.1 us
    pallas_call x3, Pallas kernels, weight_grad(): pl.pallas_call(lambda *refs: weight_grad_kernel(n_col, n_row, n_dp, whole...  74.8 us
    ppermute x8, waiting for transfers between devices, cross(): lax.ppermute(lax.dynamic_index_in_dim(summed, jnp.bitwise_xor(jnp.bitwise...  61.3 us
    psum x4, blocking collectives, row_totals(): return lax.psum(per_row, 'col')  55.1 us
    ppermute x5, waiting for transfers between devices, send_dp(): lax.ppermute(pieces[step], 'dp', [(i, (i + step) % size) for i in range(s...  37.7 us
    sub x1, matrix products, attend_backward(): prob_grads - jnp.sum(softmax_probs * prob_grads, axis=-1, keepdims=True)  24.9 us
  transfers between devices with their start and end apart: 97, of which 30 were waited for; matrix products, arithmetic and copies ran while one was open for 22% of the time, Pallas kernels for 26%

profile of v4, /device:TPU:0, one launch (start us, length us, event | category | flops | bytes accessed | tf_op | source)
XLA Modules:
  0.0 960.5 jit_solution(747137779149699060)
XLA Ops:
  10.9 33.7 %psum.28 = f32[1024]{0:T(1024)S(1)} all-reduce(f32[1024]{0:T(1024)S(1)} %fusion.33), channel_id=1, replica_groups=mesh['dp'=2,'row'=4,'col'=4] {'col'}, use_global_device_ids=true, to_apply=%region_1.0 | all-reduce | flops 1024 | bytes 8192 | tf_op jit(solution)/shard_map/psum | solution.py:436
  47.7 17.6 %collective-permute-done.1 = bf16[1024,384]{1,0:T(8,128)(2,1)S(1)} collective-permute-done((bf16[1024,384]{1,0:T(8,128)(2,1)S(1)}, bf16[1024,384]{1,0:T(8,128)(2,1)S(1)}, u32[]{:S(2)}, u32[]{:S(2)}) %collective-permute-start.1) | collective-permute-done | bytes 786464 | tf_op jit(solution)/shard_map/ppermute | solution.py:22
  71.3 21.5 %collective-permute-done.4 = bf16[40,384]{1,0:T(8,128)(2,1)S(1)} collective-permute-done((bf16[40,384]{1,0:T(8,128)(2,1)S(1)}, bf16[40,384]{1,0:T(8,128)(2,1)S(1)}, u32[]{:S(2)}, u32[]{:S(2)}) %collective-permute-start.4) | collective-permute-done | bytes 30752 | tf_op jit(solution)/shard_map/ppermute | solution.py:22
  106.4 8.5 collective-permute-done.8
  114.9 13.8 %collective-permute-done.9 = bf16[10,192,128]{2,1,0:T(8,128)(2,1)} collective-permute-done((bf16[10,192,128]{2,1,0:T(8,128)(2,1)}, bf16[10,192,128]{2,1,0:T(8,128)(2,1)}, u32[]{:S(2)}, u32[]{:S(2)}) %collective-permute-start.9) | collective-permute-done | bytes 491552 | tf_op jit(solution)/shard_map/ppermute | solution.py:22
  128.7 10.5 %collective-permute-done.10 = bf16[10,64,384]{2,1,0:T(8,128)(2,1)} collective-permute-done((bf16[10,64,384]{2,1,0:T(8,128)(2,1)}, bf16[10,64,384]{2,1,0:T(8,128)(2,1)}, u32[]{:S(2)}, u32[]{:S(2)}) %collective-permute-start.10) | collective-permute-done | bytes 491552 | tf_op jit(solution)/shard_map/ppermute | solution.py:22
  139.2 9.6 %collective-permute-done.11 = bf16[10,64,384]{2,1,0:T(8,128)(2,1)} collective-permute-done((bf16[10,64,384]{2,1,0:T(8,128)(2,1)}, bf16[10,64,384]{2,1,0:T(8,128)(2,1)}, u32[]{:S(2)}, u32[]{:S(2)}) %collective-permute-start.11) | collective-permute-done | bytes 491552 | tf_op jit(solution)/shard_map/ppermute | solution.py:22
  160.4 10.6 %collective-permute-done.13 = bf16[10,192,128]{2,1,0:T(8,128)(2,1)} collective-permute-done((bf16[10,192,128]{2,1,0:T(8,128)(2,1)}, bf16[10,192,128]{2,1,0:T(8,128)(2,1)}, u32[]{:S(2)}, u32[]{:S(2)}) %collective-permute-start.13) | collective-permute-done | bytes 491552 | tf_op jit(solution)/shard_map/ppermute | solution.py:22
  199.6 10.7 %fusion.35 = bf16[2,64,3,1024]{3,1,2,0:T(8,128)(2,1)S(1)} fusion(bf16[1024,2,64,1]{0,2,3,1:T(8,128)(2,1)S(1)} %bitcast.259, f32[2,3,1024,1024]{2,3,1,0:T(8,128)} %copy-done.2, f32[2,3,1024]{2,1,0:T(4,128)S(1)} %fusion.3, f32[2,3,1024]{2,1,0:T(4,128)S(1)} %get-tuple-element.341), kind=kOutput, calls=%fused_computation.79 | convolution fusion | flops 824573952 | bytes 26263552 | tf_op jit(solution)/shard_map/kgqs,skd->qkgd/dot_general | solution.py:400
  230.0 7.7 collective-permute-done.20
  240.8 11.7 %collective-permute-done.18 = bf16[1024,384]{1,0:T(8,128)(2,1)S(1)} collective-permute-done((bf16[1024,384]{1,0:T(8,128)(2,1)S(1)}, bf16[1024,384]{1,0:T(8,128)(2,1)S(1)}, u32[]{:S(2)}, u32[]{:S(2)}) %collective-permute-start.18) | collective-permute-done | bytes 786464 | tf_op jit(solution)/shard_map/ppermute | solution.py:22
  276.5 9.9 %collective-permute-done.37 = bf16[10,64,384]{2,1,0:T(8,128)(2,1)} collective-permute-done((bf16[10,64,384]{2,1,0:T(8,128)(2,1)}, bf16[10,64,384]{2,1,0:T(8,128)(2,1)}, u32[]{:S(2)}, u32[]{:S(2)}) %collective-permute-start.37) | collective-permute-done | bytes 491552 | tf_op jit(solution)/shard_map/ppermute | solution.py:22
  296.9 20.5 %collective-permute-done.27.refs_1_.refs_9_ = bf16[1024,384]{1,0:T(8,128)(2,1)} collective-permute-done((bf16[1024,384]{1,0:T(8,128)(2,1)S(1)}, bf16[1024,384]{1,0:T(8,128)(2,1)}, u32[]{:S(2)}, u32[]{:S(2)}) %collective-permute-start.27) | collective-permute-done | bytes 786464 | tf_op jit(solution)/shard_map/ppermute | solution.py:22
  322.1 43.6 %experts.4 = (bf16[1024,384]{1,0:T(8,128)(2,1)}, bf16[1024,384]{1,0:T(8,128)(2,1)}, bf16[1024,384]{1,0:T(8,128)(2,1)}, bf16[1024,384]{1,0:T(8,128)(2,1)}, bf16[1...) custom-call(s32[10]{0:T(128)} %stack.100.refs_0_, ...), custom_call_target="tpu_custom_call" | custom-call | flops 24159191040 | bytes 41943040 | tf_op jit(solution)/shard_map/experts/pallas_call | solution.py:218
  374.3 43.4 %experts.5 = (bf16[1024,384]{1,0:T(8,128)(2,1)}, bf16[1024,384]{1,0:T(8,128)(2,1)}, bf16[1024,384]{1,0:T(8,128)(2,1)}, bf16[1024,384]{1,0:T(8,128)(2,1)}, bf16[1...) custom-call(s32[10]{0:T(128)} %stack.94.refs_0_, ...), custom_call_target="tpu_custom_call", output_to_operand_aliasing={{4}: (23, {})} | custom-call | flops 24159191040 | bytes 41943040 | tf_op jit(solution)/shard_map/experts/pallas_call | solution.py:218
  424.7 43.5 %experts.6 = (bf16[1024,384]{1,0:T(8,128)(2,1)}, bf16[1024,384]{1,0:T(8,128)(2,1)}, bf16[1024,384]{1,0:T(8,128)(2,1)}, bf16[1024,384]{1,0:T(8,128)(2,1)}, bf16[1...) custom-call(s32[10]{0:T(128)} %stack.88.refs_0_, ...), custom_call_target="tpu_custom_call", output_to_operand_aliasing={{4}: (23, {})} | custom-call | flops 24159191040 | bytes 41943040 | tf_op jit(solution)/shard_map/experts/pallas_call | solution.py:218
  470.1 15.9 %collective-permute-start.56 = (f32[16,1024]{1,0:T(8,128)S(1)}, f32[16,1024]{1,0:T(8,128)S(1)}, u32[]{:S(2)}, u32[]{:S(2)}) collective-permute-start(f32[16,1024]{1,0:T(8,128)S(1)} %copy-done.90), channel_id=1, source_target_pairs={{0,4},{4,0},{8,12},{12,8},{1,5},{5,1},{9,13},{13,9},{2,6},{6,2},{1... | collective-permute-start | bytes 196616 | tf_op jit(solution)/shard_map/ppermute | solution.py:22
  493.2 43.7 %experts.7 = (bf16[1024,384]{1,0:T(8,128)(2,1)}, bf16[1024,384]{1,0:T(8,128)(2,1)}, bf16[1024,384]{1,0:T(8,128)(2,1)}, bf16[1024,384]{1,0:T(8,128)(2,1)}, bf16[1...) custom-call(s32[10]{0:T(128)} %stack.82.refs_0_, ...), custom_call_target="tpu_custom_call", output_to_operand_aliasing={{4}: (23, {})} | custom-call | flops 24159191040 | bytes 41943040 | tf_op jit(solution)/shard_map/experts/pallas_call | solution.py:218
  543.3 25.0 %weight_grads.3 = bf16[2,4,10,192,128]{4,3,2,1,0:T(8,128)(2,1)} custom-call(s32[17]{0:T(128)} %stack.102.refs_0_, bf16[1024,1280]{1,0:T(8,128)(2,1)} %get-tuple-element.225.refs_1_, bf16[1024,1280]{1,0:T(8,128)(2,1)} %get-tuple-element.226.refs_2_, bf16[1024,1280]{1,0:T(8,128)(2,1)} %get-tuple-element.227.refs_3_, ...), custom_call_target="tpu_custom_call" | custom-call | flops 16106127360 | bytes 20971520 | tf_op jit(solution)/shard_map/weight_grads/pallas_call | solution.py:313
  580.2 24.8 %weight_grads.4 = bf16[2,4,10,192,128]{4,3,2,1,0:T(8,128)(2,1)} custom-call(s32[17]{0:T(128)} %stack.102.refs_0_, bf16[1024,1280]{1,0:T(8,128)(2,1)} %get-tuple-element.229.refs_1_, bf16[1024,1280]{1,0:T(8,128)(2,1)} %get-tuple-element.230.refs_2_, bf16[1024,1280]{1,0:T(8,128)(2,1)} %get-tuple-element.231.refs_3_, ...), custom_call_target="tpu_custom_call" | custom-call | flops 16106127360 | bytes 20971520 | tf_op jit(solution)/shard_map/weight_grads/pallas_call | solution.py:313
  618.6 25.0 %weight_grads.5 = bf16[2,4,10,192,128]{4,3,2,1,0:T(8,128)(2,1)} custom-call(s32[17]{0:T(128)} %stack.102.refs_0_, bf16[1024,1280]{1,0:T(8,128)(2,1)} %get-tuple-element.237.refs_1_, bf16[1024,1280]{1,0:T(8,128)(2,1)} %get-tuple-element.238.refs_2_, bf16[1024,1280]{1,0:T(8,128)(2,1)} %get-tuple-element.239.refs_3_, ...), custom_call_target="tpu_custom_call" | custom-call | flops 16106127360 | bytes 20971520 | tf_op jit(solution)/shard_map/weight_grads/pallas_call | solution.py:313
  643.5 16.9 %collective-permute-done.60 = bf16[4,10,192,128]{3,2,1,0:T(8,128)(2,1)} collective-permute-done((bf16[4,10,192,128]{3,2,1,0:T(8,128)(2,1)}, bf16[4,10,192,128]{3,2,1,0:T(8,128)(2,1)}, u32[]{:S(2)}, u32[]{:S(2)}) %collective-permute-start.60) | collective-permute-done | bytes 1966112 | tf_op jit(solution)/shard_map/ppermute | solution.py:336
  681.5 12.9 %collective-permute-done.65 = bf16[1024,384]{1,0:T(8,128)(2,1)} collective-permute-done((bf16[1024,384]{1,0:T(8,128)(2,1)}, bf16[1024,384]{1,0:T(8,128)(2,1)}, u32[]{:S(2)}, u32[]{:S(2)}) %collective-permute-start.65) | collective-permute-done | bytes 786464 | tf_op jit(solution)/shard_map/ppermute | solution.py:22
  711.7 24.9 %fusion.2 = bf16[2,3,1024,1024]{2,3,1,0:T(8,128)(2,1)} fusion(f32[2,3,1024,1024]{2,3,1,0:T(8,128)} %copy-done.2, f32[2,3,1024]{2,1,0:T(4,128)S(1)} %log_add_fusion, bf16[1024,2,64,1]{0,2,3,1:T(8,128)(2,1)S(1)} %bitcast.260, bf16[1024,2,3,64]{0,3,2,1:T(8,128)(2,1)S(1)} %bitcast.243), kind=kOutput, calls=%fused_computation.4 | convolution fusion | flops 1648368640 | bytes 38821888 | tf_op jit(solution)/shard_map/sub | solution.py:416
  736.6 13.3 %fusion.41 = bf16[2,64,1024]{2,1,0:T(8,128)(2,1)} fusion(bf16[1024,2,3,64]{0,3,2,1:T(8,128)(2,1)} %bitcast.244, f32[2,3,1024,1024]{2,3,1,0:T(8,128)} %copy-done.2, f32[2,3,1024]{2,1,0:T(4,128)} %copy-done.72), kind=kOutput, calls=%fused_computation.94 | convolution fusion | flops 818020352 | bytes 26238976 | tf_op jit(solution)/shard_map/kgqs,qkgd->skd/dot_general | solution.py:425
  763.9 8.6 fusion.40
  778.4 11.2 %collective-permute-done.74 = bf16[10,192,128]{2,1,0:T(8,128)(2,1)S(1)} collective-permute-done((bf16[10,192,128]{2,1,0:T(8,128)(2,1)S(1)}, bf16[10,192,128]{2,1,0:T(8,128)(2,1)S(1)}, u32[]{:S(2)}, u32[]{:S(2)}) %collective-permute-start.74) | collective-permute-done | bytes 491552 | tf_op jit(solution)/shard_map/ppermute | solution.py:22
  789.7 29.8 %collective-permute-done.77 = bf16[192,384]{1,0:T(8,128)(2,1)S(1)} collective-permute-done((bf16[192,384]{1,0:T(8,128)(2,1)S(1)}, bf16[192,384]{1,0:T(8,128)(2,1)S(1)}, u32[]{:S(2)}, u32[]{:S(2)}) %collective-permute-start.77) | collective-permute-done | bytes 147488 | tf_op jit(solution)/shard_map/ppermute | solution.py:724
  833.8 17.8 %collective-permute-done.85 = bf16[4,192,640]{2,1,0:T(8,128)(2,1)S(1)} collective-permute-done((bf16[4,192,640]{2,1,0:T(8,128)(2,1)S(1)}, bf16[4,192,640]{2,1,0:T(8,128)(2,1)S(1)}, u32[]{:S(2)}, u32[]{:S(2)}) %collective-permute-start.85) | collective-permute-done | bytes 983072 | tf_op jit(solution)/shard_map/ppermute | solution.py:336
  853.8 8.9 collective-permute-done.89
  864.7 22.5 %collective-permute-done.88 = bf16[192,640]{1,0:T(8,128)(2,1)S(1)} collective-permute-done((bf16[192,640]{1,0:T(8,128)(2,1)S(1)}, bf16[192,640]{1,0:T(8,128)(2,1)S(1)}, u32[]{:S(2)}, u32[]{:S(2)}) %collective-permute-start.88) | collective-permute-done | bytes 245792 | tf_op jit(solution)/shard_map/ppermute | solution.py:724
  900.2 11.7 %collective-permute-done.92 = bf16[10,192,128]{2,1,0:T(8,128)(2,1)S(1)} collective-permute-done((bf16[10,192,128]{2,1,0:T(8,128)(2,1)S(1)}, bf16[10,192,128]{2,1,0:T(8,128)(2,1)S(1)}, u32[]{:S(2)}, u32[]{:S(2)}) %collective-permute-start.92) | collective-permute-done | bytes 491552 | tf_op jit(solution)/shard_map/ppermute | solution.py:22
  (498 shorter events, 315.4 us)
Async XLA Ops:
  7.2 141.7 %all-gather.7.cloned.1.call-start = ((), (), s32[]{:S(2)}) async-start(), calls=%async_computation.2 | async-start | bytes 2457600 | tf_op jit(solution)/shard_map/all_gather | solution.py:482
  9.9 200.4 %all-gather.9.cloned.1.call-start = ((), (), s32[]{:S(2)}) async-start(), calls=%async_computation.3 | async-start | bytes 1474560 | tf_op jit(solution)/shard_map/all_gather | solution.py:523
  47.7 53.6 %collective-permute-start = (bf16[1024,384]{1,0:T(8,128)(2,1)S(1)}, bf16[1024,384]{1,0:T(8,128)(2,1)S(1)}, u32[]{:S(2)}, u32[]{:S(2)}) collective-permute-start(bf16[1024,384]{1,0:T(8,128)(2,1)S(1)} %fusion.26), channel_id=1, source_target_pairs={{0,1},{1,0},{2,3},{3,2},{4,5},{5,4},{6,7},{7,6},{8,9},{9,8},{10,11... | collective-permute-start | bytes 2359304 | tf_op jit(solution)/shard_map/ppermute | solution.py:22
  101.4 47.5 %collective-permute-start.11 = (bf16[10,64,384]{2,1,0:T(8,128)(2,1)}, bf16[10,64,384]{2,1,0:T(8,128)(2,1)}, u32[]{:S(2)}, u32[]{:S(2)}) collective-permute-start(bf16[10,64,384]{2,1,0:T(8,128)(2,1)} %get-tuple-element.288), channel_id=1, source_target_pairs={{0,3},{1,2},{2,1},{3,0},{4,7},{5,6},{6,5},{7,4},{8,11},{9,10},{10,... | collective-permute-start | bytes 1474568 | tf_op jit(solution)/shard_map/ppermute | solution.py:22
  102.9 46.0 %collective-permute-start.15 = (bf16[384,384]{0,1:T(8,128)(2,1)S(1)}, bf16[384,384]{0,1:T(8,128)(2,1)S(1)}, u32[]{:S(2)}, u32[]{:S(2)}) collective-permute-start(bf16[384,384]{0,1:T(8,128)(2,1)S(1)} %bitcast.287), channel_id=1, source_target_pairs={{0,0},{1,4},{2,8},{3,12},{4,1},{5,5},{6,9},{7,13},{8,2},{9,6},{10,... | collective-permute-start | bytes 884744 | tf_op jit(solution)/shard_map/ppermute | solution.py:481
  149.6 172.5 %all-gather.11.cloned.1.call-start = ((), (), s32[]{:S(2)}) async-start(), calls=%async_computation.4 | async-start | bytes 13369344 | tf_op jit(solution)/shard_map/all_gather | solution.py:525
  155.1 795.1 %reduce-scatter.2.cloned.1.call-start = ((), (), s32[]{:S(2)}) async-start(), calls=%async_computation.1 | async-start | bytes 13369344 | tf_op jit(solution)/shard_map/reduce_scatter | solution.py:657
  266.5 54.7 %collective-permute-start.33 = (bf16[10,384,128]{2,1,0:T(8,128)(2,1)}, bf16[10,384,128]{2,1,0:T(8,128)(2,1)}, u32[]{:S(2)}, u32[]{:S(2)}) collective-permute-start(bf16[10,384,128]{2,1,0:T(8,128)(2,1)} %constant_dynamic-slice_fusion.2), channel_id=1, source_target_pairs={{0,1},{1,0},{2,3},{3,2},{4,5},{5,4},{6,7},{7,6},{8,9},{9,8},{10,11... | collective-permute-start | bytes 2949128 | tf_op jit(solution)/shard_map/ppermute | solution.py:22
  317.3 55.1 %collective-permute-start.24 = (bf16[1024,384]{1,0:T(8,128)(2,1)S(1)}, bf16[1024,384]{1,0:T(8,128)(2,1)}, u32[]{:S(2)}, u32[]{:S(2)}) collective-permute-start(bf16[1024,384]{1,0:T(8,128)(2,1)S(1)} %multiply_convert_fusion.refs_1_.refs_5_), channel_id=1, source_target_pairs={{0,8},{4,12},{8,0},{12,4},{1,9},{5,13},{9,1},{13,5},{2,10},{6,14},... | collective-permute-start | bytes 2359304 | tf_op jit(solution)/shard_map/ppermute | solution.py:22
  319.8 53.6 %collective-permute-start.21 = (bf16[1024,384]{1,0:T(8,128)(2,1)S(1)}, bf16[1024,384]{1,0:T(8,128)(2,1)}, u32[]{:S(2)}, u32[]{:S(2)}) collective-permute-start(bf16[1024,384]{1,0:T(8,128)(2,1)S(1)} %multiply_convert_fusion.refs_1_.refs_5_), channel_id=1, source_target_pairs={{0,12},{4,8},{8,4},{12,0},{1,13},{5,9},{9,5},{13,1},{2,14},{6,10},... | collective-permute-start | bytes 2359304 | tf_op jit(solution)/shard_map/ppermute | solution.py:22
  321.2 52.2 %collective-permute-start.28 = (bf16[1024,384]{1,0:T(8,128)(2,1)}, bf16[1024,384]{1,0:T(8,128)(2,1)}, u32[]{:S(2)}, u32[]{:S(2)}) collective-permute-start(bf16[1024,384]{1,0:T(8,128)(2,1)} %collective-permute-done.27.refs_1_.refs_9_), channel_id=1, source_target_pairs={{0,1},{1,0},{2,3},{3,2},{4,5},{5,4},{6,7},{7,6},{8,9},{9,8},{10,11... | collective-permute-start | bytes 2359304 | tf_op jit(solution)/shard_map/ppermute | solution.py:22
  372.4 46.0 %collective-permute-start.26 = (bf16[1024,384]{1,0:T(8,128)(2,1)}, bf16[1024,384]{1,0:T(8,128)(2,1)}, u32[]{:S(2)}, u32[]{:S(2)}) collective-permute-start(bf16[1024,384]{1,0:T(8,128)(2,1)} %collective-permute-done.24.refs_1_.refs_13_), channel_id=1, source_target_pairs={{0,2},{1,3},{2,0},{3,1},{4,6},{5,7},{6,4},{7,5},{8,10},{9,11},{10,... | collective-permute-start | bytes 2359304 | tf_op jit(solution)/shard_map/ppermute | solution.py:22
  373.4 47.1 %collective-permute-start.41 = (bf16[1024,384]{1,0:T(8,128)(2,1)}, bf16[1024,384]{1,0:T(8,128)(2,1)S(1)}, u32[]{:S(2)}, u32[]{:S(2)}) collective-permute-start(bf16[1024,384]{1,0:T(8,128)(2,1)} %get-tuple-element.180), channel_id=1, source_target_pairs={{0,1},{1,0},{2,3},{3,2},{4,5},{5,4},{6,7},{7,6},{8,9},{9,8},{10,11... | collective-permute-start | bytes 2359304 | tf_op jit(solution)/shard_map/ppermute | solution.py:22
  419.4 48.8 %collective-permute-start.23 = (bf16[1024,384]{1,0:T(8,128)(2,1)}, bf16[1024,384]{1,0:T(8,128)(2,1)}, u32[]{:S(2)}, u32[]{:S(2)}) collective-permute-start(bf16[1024,384]{1,0:T(8,128)(2,1)} %collective-permute-done.21.refs_1_.refs_17_), channel_id=1, source_target_pairs={{0,2},{1,3},{2,0},{3,1},{4,6},{5,7},{6,4},{7,5},{8,10},{9,11},{10,... | collective-permute-start | bytes 2359304 | tf_op jit(solution)/shard_map/ppermute | solution.py:22
  420.5 47.9 %collective-permute-start.40 = (bf16[1024,384]{1,0:T(8,128)(2,1)}, bf16[1024,384]{1,0:T(8,128)(2,1)}, u32[]{:S(2)}, u32[]{:S(2)}) collective-permute-start(bf16[1024,384]{1,0:T(8,128)(2,1)} %get-tuple-element.178), channel_id=1, source_target_pairs={{0,1},{1,0},{2,3},{3,2},{4,5},{5,4},{6,7},{7,6},{8,9},{9,8},{10,11... | collective-permute-start | bytes 2359304 | tf_op jit(solution)/shard_map/ppermute | solution.py:22
  420.7 68.3 %collective-permute-start.44 = (bf16[1024,384]{1,0:T(8,128)(2,1)}, bf16[1024,384]{1,0:T(8,128)(2,1)S(1)}, u32[]{:S(2)}, u32[]{:S(2)}) collective-permute-start(bf16[1024,384]{1,0:T(8,128)(2,1)} %get-tuple-element.188), channel_id=1, source_target_pairs={{0,1},{1,0},{2,3},{3,2},{4,5},{5,4},{6,7},{7,6},{8,9},{9,8},{10,11... | collective-permute-start | bytes 2359304 | tf_op jit(solution)/shard_map/ppermute | solution.py:22
  422.6 47.4 %collective-permute-start.43 = (bf16[1024,384]{1,0:T(8,128)(2,1)S(1)}, bf16[1024,384]{1,0:T(8,128)(2,1)}, u32[]{:S(2)}, u32[]{:S(2)}) collective-permute-start(bf16[1024,384]{1,0:T(8,128)(2,1)S(1)} %fusion.62), channel_id=1, source_target_pairs={{0,2},{1,3},{2,0},{3,1},{4,6},{5,7},{6,4},{7,5},{8,10},{9,11},{10,... | collective-permute-start | bytes 2359304 | tf_op jit(solution)/shard_map/ppermute | solution.py:22
  423.7 65.3 %collective-permute-start.53 = (bf16[1024,384]{1,0:T(8,128)(2,1)S(1)}, bf16[1024,384]{1,0:T(8,128)(2,1)S(1)}, u32[]{:S(2)}, u32[]{:S(2)}) collective-permute-start(bf16[1024,384]{1,0:T(8,128)(2,1)S(1)} %fusion.63), channel_id=1, source_target_pairs={{0,2},{1,3},{2,0},{3,1},{4,6},{5,7},{6,4},{7,5},{8,10},{9,11},{10,... | collective-permute-start | bytes 2359304 | tf_op jit(solution)/shard_map/ppermute | solution.py:22
  470.1 70.0 %collective-permute-start.56 = (f32[16,1024]{1,0:T(8,128)S(1)}, f32[16,1024]{1,0:T(8,128)S(1)}, u32[]{:S(2)}, u32[]{:S(2)}) collective-permute-start(f32[16,1024]{1,0:T(8,128)S(1)} %copy-done.90), channel_id=1, source_target_pairs={{0,4},{4,0},{8,12},{12,8},{1,5},{5,1},{9,13},{13,9},{2,6},{6,2},{1... | collective-permute-start | bytes 196616 | tf_op jit(solution)/shard_map/ppermute | solution.py:22
  489.0 47.9 %collective-permute-start.47 = (bf16[1024,384]{1,0:T(8,128)(2,1)}, bf16[1024,384]{1,0:T(8,128)(2,1)S(1)}, u32[]{:S(2)}, u32[]{:S(2)}) collective-permute-start(bf16[1024,384]{1,0:T(8,128)(2,1)} %get-tuple-element.200), channel_id=1, source_target_pairs={{0,1},{1,0},{2,3},{3,2},{4,5},{5,4},{6,7},{7,6},{8,9},{9,8},{10,11... | collective-permute-start | bytes 2359304 | tf_op jit(solution)/shard_map/ppermute | solution.py:22
  489.0 83.0 %collective-permute-start.46 = (bf16[1024,384]{1,0:T(8,128)(2,1)}, bf16[1024,384]{1,0:T(8,128)(2,1)S(1)}, u32[]{:S(2)}, u32[]{:S(2)}) collective-permute-start(bf16[1024,384]{1,0:T(8,128)(2,1)} %get-tuple-element.198), channel_id=1, source_target_pairs={{0,1},{1,0},{2,3},{3,2},{4,5},{5,4},{6,7},{7,6},{8,9},{9,8},{10,11... | collective-permute-start | bytes 2359304 | tf_op jit(solution)/shard_map/ppermute | solution.py:22
  490.7 50.1 %collective-permute-start.57 = (f32[16,1024]{1,0:T(8,128)}, f32[16,1024]{1,0:T(8,128)S(1)}, u32[]{:S(2)}, u32[]{:S(2)}) collective-permute-start(f32[16,1024]{1,0:T(8,128)} %get-tuple-element.215), channel_id=1, source_target_pairs={{0,8},{4,12},{8,0},{12,4},{1,9},{5,13},{9,1},{13,5},{2,10},{6,14},... | collective-permute-start | bytes 196616 | tf_op jit(solution)/shard_map/ppermute | solution.py:22
  491.3 88.9 %collective-permute-start.54 = (bf16[1024,384]{1,0:T(8,128)(2,1)}, bf16[1024,384]{1,0:T(8,128)(2,1)}, u32[]{:S(2)}, u32[]{:S(2)}) collective-permute-start(bf16[1024,384]{1,0:T(8,128)(2,1)} %convert_add_fusion.4), channel_id=1, source_target_pairs={{0,4},{4,0},{8,12},{12,8},{1,5},{5,1},{9,13},{13,9},{2,6},{6,2},{1... | collective-permute-start | bytes 2359304 | tf_op jit(solution)/shard_map/ppermute | solution.py:22
  543.2 66.9 %collective-permute-start.50 = (bf16[1024,384]{1,0:T(8,128)(2,1)}, bf16[1024,384]{1,0:T(8,128)(2,1)}, u32[]{:S(2)}, u32[]{:S(2)}) collective-permute-start(bf16[1024,384]{1,0:T(8,128)(2,1)} %get-tuple-element.209), channel_id=1, source_target_pairs={{0,1},{1,0},{2,3},{3,2},{4,5},{5,4},{6,7},{7,6},{8,9},{9,8},{10,11... | collective-permute-start | bytes 2359304 | tf_op jit(solution)/shard_map/ppermute | solution.py:22
  572.9 45.6 %collective-permute-start.61 = (bf16[4,10,192,128]{3,2,1,0:T(8,128)(2,1)S(1)}, bf16[4,10,192,128]{3,2,1,0:T(8,128)(2,1)S(1)}, u32[]{:S(2)}, u32[]{:S(2)}) collective-permute-start(bf16[4,10,192,128]{3,2,1,0:T(8,128)(2,1)S(1)} %get-tuple-element.284), channel_id=1, source_target_pairs={{0,16},{16,0},{1,17},{17,1},{2,18},{18,2},{3,19},{19,3},{4,20},{20... | collective-permute-start | bytes 5898248 | tf_op jit(solution)/shard_map/ppermute | solution.py:336
  609.4 51.0 %collective-permute-start.60 = (bf16[4,10,192,128]{3,2,1,0:T(8,128)(2,1)}, bf16[4,10,192,128]{3,2,1,0:T(8,128)(2,1)}, u32[]{:S(2)}, u32[]{:S(2)}) collective-permute-start(bf16[4,10,192,128]{3,2,1,0:T(8,128)(2,1)} %get-tuple-element.286), channel_id=1, source_target_pairs={{0,16},{16,0},{1,17},{17,1},{2,18},{18,2},{3,19},{19,3},{4,20},{20... | collective-permute-start | bytes 5898248 | tf_op jit(solution)/shard_map/ppermute | solution.py:336
  680.0 74.8 %collective-permute-start.67 = (bf16[4,10,192,128]{3,2,1,0:T(8,128)(2,1)}, bf16[4,10,192,128]{3,2,1,0:T(8,128)(2,1)}, u32[]{:S(2)}, u32[]{:S(2)}) collective-permute-start(bf16[4,10,192,128]{3,2,1,0:T(8,128)(2,1)} %slice_bitcast_fusion), channel_id=1, source_target_pairs={{0,16},{16,0},{1,17},{17,1},{2,18},{18,2},{3,19},{19,3},{4,20},{20... | collective-permute-start | bytes 5898248 | tf_op jit(solution)/shard_map/ppermute | solution.py:336
  703.2 52.5 %collective-permute-start.68 = (bf16[10,192,128]{2,1,0:T(8,128)(2,1)}, bf16[10,192,128]{2,1,0:T(8,128)(2,1)}, u32[]{:S(2)}, u32[]{:S(2)}) collective-permute-start(bf16[10,192,128]{2,1,0:T(8,128)(2,1)} %get-tuple-element.304), channel_id=1, source_target_pairs={{0,1},{1,0},{2,3},{3,2},{4,5},{5,4},{6,7},{7,6},{8,9},{9,8},{10,11... | collective-permute-start | bytes 1474568 | tf_op jit(solution)/shard_map/ppermute | solution.py:22
  703.8 52.8 %collective-permute-start.69 = (bf16[10,192,128]{2,1,0:T(8,128)(2,1)}, bf16[10,192,128]{2,1,0:T(8,128)(2,1)}, u32[]{:S(2)}, u32[]{:S(2)}) collective-permute-start(bf16[10,192,128]{2,1,0:T(8,128)(2,1)} %get-tuple-element.303), channel_id=1, source_target_pairs={{0,2},{1,3},{2,0},{3,1},{4,6},{5,7},{6,4},{7,5},{8,10},{9,11},{10,... | collective-permute-start | bytes 1474568 | tf_op jit(solution)/shard_map/ppermute | solution.py:22
  704.9 51.7 %collective-permute-start.70 = (bf16[10,192,128]{2,1,0:T(8,128)(2,1)}, bf16[10,192,128]{2,1,0:T(8,128)(2,1)}, u32[]{:S(2)}, u32[]{:S(2)}) collective-permute-start(bf16[10,192,128]{2,1,0:T(8,128)(2,1)} %get-tuple-element.302), channel_id=1, source_target_pairs={{0,3},{1,2},{2,1},{3,0},{4,7},{5,6},{6,5},{7,4},{8,11},{9,10},{10,... | collective-permute-start | bytes 1474568 | tf_op jit(solution)/shard_map/ppermute | solution.py:22
  832.1 62.8 %collective-permute-start.79 = (bf16[1024,384]{1,0:T(8,128)(2,1)S(1)}, bf16[1024,384]{1,0:T(8,128)(2,1)S(1)}, u32[]{:S(2)}, u32[]{:S(2)}) collective-permute-start(bf16[1024,384]{1,0:T(8,128)(2,1)S(1)} %convolution_convert_fusion.2), channel_id=1, source_target_pairs={{0,1},{1,0},{2,3},{3,2},{4,5},{5,4},{6,7},{7,6},{8,9},{9,8},{10,11... | collective-permute-start | bytes 2359304 | tf_op jit(solution)/shard_map/ppermute | solution.py:22
  833.7 61.2 %collective-permute-start.81 = (bf16[1024,384]{1,0:T(8,128)(2,1)S(1)}, bf16[1024,384]{1,0:T(8,128)(2,1)S(1)}, u32[]{:S(2)}, u32[]{:S(2)}) collective-permute-start(bf16[1024,384]{1,0:T(8,128)(2,1)S(1)} %add_convert_fusion.3), channel_id=1, source_target_pairs={{0,2},{1,3},{2,0},{3,1},{4,6},{5,7},{6,4},{7,5},{8,10},{9,11},{10,... | collective-permute-start | bytes 2359304 | tf_op jit(solution)/shard_map/ppermute | solution.py:22
  (156 other events, 2609.6 us)
Sparse Core Ops, SparseCore 0:
  10.2 70.6 all-gather.6
  149.8 29.1 all-gather.8
  181.2 128.3 all-gather.10
  661.3 159.1 reduce-scatter.1
